TPU v7x, 32 devices: a whole 2x2x4 slice. The times are simulated.
32 devices in a mesh: seq: 2 (over x), dp: 16 (over z, y, core).
Axes of the slice: x: 2, y: 2, z: 4, core: 2. Of those that a mesh axis runs over, the one named last changes fastest.
Arguments:
- queries: bfloat16 [16, 256, 2048], P('dp', 'seq'), may hold values from -6 to 6
- key_rows: bfloat16 [16, 256, 256], P('dp', 'seq'), may hold values from -6 to 6
- value_matrix: bfloat16 [16, 256, 256], P('dp', 'seq'), may hold values from -6 to 6
- head_sink_logits: float32 [32], replicated, may hold values from 2 to 6
- residual: bfloat16 [16, 256, 2880], P('dp', 'seq'), may hold values from -6 to 6
- out_weight: bfloat16 [2048, 2880], P('dp'), may hold values from -0.125 to 0.125
- norm_gain: float32 [2880], replicated, may hold values from 0.25 to 1.75
- router: bfloat16 [2880, 128], replicated, may hold values from -0.109375 to 0.109375
- expert_gate: bfloat16 [2880, 4096], P('dp', 'seq'), may hold values from -0.109375 to 0.109375
- expert_up: bfloat16 [2880, 4096], P('dp', 'seq'), may hold values from -0.109375 to 0.109375
- expert_down: bfloat16 [2880, 4096], P('dp', 'seq'), may hold values from -0.125 to 0.125
- routes: int32 [16, 256, 4], P('dp', 'seq'), may hold values from 0 to 127, as said below
- group_ids: int32 [16], P('dp'), may hold values from 0 to 3, never falling along the last dimension, each value on 1 to 8 neighbouring positions
- rewards: int32 [16], P('dp'), may hold values from 0 to 3
- response_mask: int32 [16, 256], P('dp', 'seq'), may hold values from 0 to 1, as said below
- upstream: bfloat16 [16, 256, 2880], P('dp', 'seq'), may hold values from -6 to 6
Outputs:
- grad_queries: bfloat16 [16, 256, 2048], P('dp', 'seq')
- grad_keys: bfloat16 [16, 256, 256], P('dp', 'seq')
- grad_values: bfloat16 [16, 256, 256], P('dp', 'seq')
- grad_residual: bfloat16 [16, 256, 2880], P('dp', 'seq')
- grad_sinks: float32 [32], replicated
Inputs may be any that keep to these rules, and one draw needn't show every extreme that they name: `routes`: each token names 4 different experts. Among the 128 positions of every aligned block of a rollout at most 4 tokens name a given expert below 2; the first block of the first rollout has exactly 4 for each of them. `group_ids`: the rollouts of one group are adjacent and every group has 1 to 8 rollouts. `response_mask`: in each rollout the ones form one run that starts within the first quarter of the positions and ends within the last quarter.
All inputs are finite; a program needn't handle non-finite values.
Results may differ from a plain program's by a relative error of at most 0.0095.
Values may be sent and summed in bfloat16 or wider, within the bound.
A program may use at most 128 MiB of HBM per device.

v0:
```python
import jax
import jax.numpy as jnp
from jax import lax
from jax.sharding import PartitionSpec as P

D = 2880
HEAD_SIZE = 64
WINDOW = 128
EXPERTS = 128
QUERY_HEADS = 32
KEY_VALUE_HEADS = 4
EW = 2
CAP = 4


NORM_EPS = 1e-05
GLU_SLOPE = 1.702
HIGHEST = lax.Precision.HIGHEST
CONTRACT_LAST = (((1,), (1,)), ((), ()))


def passed_along(value, axis, steps):
    count = lax.axis_size(axis)
    initial, last = (max(0, -steps), min(count, count - steps))
    return lax.ppermute(value, axis, [(source, source + steps) for source in range(initial, last)])


def glu_forward(gate_pre, up_pre):
    return ((up_pre + 1.0) * gate_pre * jax.nn.sigmoid(GLU_SLOPE * gate_pre)).astype(jnp.bfloat16)


def glu_grads(grad_act, gate_pre, up_pre):
    sigmoid_gate = jax.nn.sigmoid(GLU_SLOPE * gate_pre)
    grad_up = grad_act * (gate_pre * sigmoid_gate)
    grad_gate = (
        grad_act
        * (up_pre + 1.0)
        * (sigmoid_gate + GLU_SLOPE * gate_pre * sigmoid_gate * (1.0 - sigmoid_gate))
    )
    return (grad_gate, grad_up)


def head_scores(query_tile_block, key_tile_block, head_sink_logits, allowed):
    query_total_count = query_tile_block.shape[0]
    key_total_count = key_tile_block.shape[0]
    query_head_rows = query_tile_block.reshape(
        query_total_count, KEY_VALUE_HEADS, QUERY_HEADS // KEY_VALUE_HEADS, HEAD_SIZE
    )
    key_head_rows = key_tile_block.reshape(key_total_count, KEY_VALUE_HEADS, HEAD_SIZE)
    attention_scores = jnp.einsum(
        "baqj,eaj->aqbe", query_head_rows, key_head_rows, preferred_element_type=jnp.float32
    ) * HEAD_SIZE ** (-0.5)
    attention_scores = jnp.where(allowed[None, None], attention_scores, -1e30)
    sink_logit_column = head_sink_logits.reshape(KEY_VALUE_HEADS, QUERY_HEADS // KEY_VALUE_HEADS)[
        :, :, None
    ]
    largest = jnp.maximum(jnp.max(attention_scores, axis=3), sink_logit_column)
    raised = jnp.where(allowed[None, None], jnp.exp(attention_scores - largest[..., None]), 0.0)
    sink_raised = jnp.exp(sink_logit_column - largest)
    denominator = jnp.sum(raised, axis=3) + sink_raised
    return (raised / denominator[..., None], sink_raised / denominator)


def head_mix(reduced_probabilities, value_tile_block):
    key_total_count = value_tile_block.shape[0]
    value_head_rows = value_tile_block.reshape(key_total_count, KEY_VALUE_HEADS, HEAD_SIZE)
    mixed_output = jnp.einsum(
        "amlh,hai->lami", reduced_probabilities, value_head_rows, preferred_element_type=jnp.float32
    )
    return mixed_output.reshape(mixed_output.shape[0], QUERY_HEADS * HEAD_SIZE).astype(jnp.bfloat16)


def head_grads(
    probs,
    reduced_probabilities,
    sink_probs,
    query_tile_block,
    key_tile_block,
    value_tile_block,
    mixed_gradient,
):
    query_total_count = query_tile_block.shape[0]
    key_total_count = key_tile_block.shape[0]
    query_head_rows = query_tile_block.reshape(
        query_total_count, KEY_VALUE_HEADS, QUERY_HEADS // KEY_VALUE_HEADS, HEAD_SIZE
    )
    key_head_rows = key_tile_block.reshape(key_total_count, KEY_VALUE_HEADS, HEAD_SIZE)
    value_head_rows = value_tile_block.reshape(key_total_count, KEY_VALUE_HEADS, HEAD_SIZE)
    heads_gradient = mixed_gradient.reshape(
        query_total_count, KEY_VALUE_HEADS, QUERY_HEADS // KEY_VALUE_HEADS, HEAD_SIZE
    )
    probability_gradient = jnp.einsum(
        "baqj,eaj->aqbe", heads_gradient, value_head_rows, preferred_element_type=jnp.float32
    )
    spread = jnp.sum(probs * probability_gradient, axis=3)
    score_gradient = (probs * (probability_gradient - spread[..., None])).astype(jnp.bfloat16)
    head_scaling = HEAD_SIZE ** (-0.5)
    query_gradient = (
        jnp.einsum(
            "amlh,hai->lami", score_gradient, key_head_rows, preferred_element_type=jnp.float32
        )
        * head_scaling
    )
    key_gradient = (
        jnp.einsum(
            "ujko,kujm->oum", score_gradient, query_head_rows, preferred_element_type=jnp.float32
        )
        * head_scaling
    )
    value_gradient = jnp.einsum(
        "ujko,kujm->oum", reduced_probabilities, heads_gradient, preferred_element_type=jnp.float32
    )
    sink_gradient = -jnp.sum(sink_probs * spread, axis=2).reshape(QUERY_HEADS)
    return (
        query_gradient.reshape(query_total_count, QUERY_HEADS * HEAD_SIZE).astype(jnp.bfloat16),
        key_gradient.reshape(key_total_count, KEY_VALUE_HEADS * HEAD_SIZE),
        value_gradient.reshape(key_total_count, KEY_VALUE_HEADS * HEAD_SIZE),
        sink_gradient,
    )


def block_backward(grad_flat, gate_pre, up_pre, gate_full, up_full, down_full):
    grad_act = jnp.dot(grad_flat, down_full, preferred_element_type=jnp.float32)
    grad_gate, grad_up = glu_grads(grad_act, gate_pre, up_pre)
    grad_pair = jnp.concatenate([grad_gate, grad_up], axis=1).astype(jnp.bfloat16)
    weight_pair = jnp.concatenate([gate_full, up_full], axis=1)
    return lax.dot_general(
        grad_pair, weight_pair, CONTRACT_LAST, preferred_element_type=jnp.float32
    ).astype(jnp.bfloat16)


def shards(
    queries,
    key_rows,
    value_matrix,
    head_sink_logits,
    residual,
    out_weight,
    norm_gain,
    router,
    expert_gate,
    expert_up,
    expert_down,
    routes,
    group_ids,
    rewards,
    response_mask,
    upstream,
):
    seq_count = lax.axis_size("seq")
    dp_count = lax.axis_size("dp")
    seq_index = lax.axis_index("seq")
    query_rows = queries[0]
    own_keys = key_rows[0]
    own_values = value_matrix[0]
    tokens_here = query_rows.shape[0]
    pieces = seq_count // EW
    group_count = max(dp_count // 4, 1)
    all_tokens = dp_count * seq_count * tokens_here
    group_hot = (group_ids[0] == jnp.arange(group_count, dtype=jnp.int32)).astype(jnp.float32)
    reward = rewards[0].astype(jnp.float32)
    group_terms = (
        group_hot[:, None] * jnp.stack([jnp.ones_like(reward), reward, reward * reward])[None, :]
    )
    mask_wide = response_mask[0].astype(jnp.float32)
    local_count = jnp.sum(mask_wide)
    first_device = (seq_index == 0).astype(jnp.float32)
    group_totals, token_total = lax.psum((group_terms * first_device, local_count), ("seq", "dp"))
    group_sizes = group_totals[:, 0]
    group_means = group_totals[:, 1] / group_sizes
    group_spread = group_totals[:, 2] / group_sizes - group_means * group_means
    own_mean = jnp.sum(group_hot * group_means)
    own_spread = jnp.sum(group_hot * group_spread)
    advantage = (reward - own_mean) / jnp.sqrt(jnp.maximum(own_spread, 1.0))
    token_scale = -advantage * all_tokens / token_total
    loss_weight = token_scale * mask_wide
    halo_keys, halo_values = passed_along((own_keys, own_values), "seq", 1)
    key_tile_block = jnp.concatenate([halo_keys, own_keys], axis=0)
    value_tile_block = jnp.concatenate([halo_values, own_values], axis=0)
    row_index = jnp.arange(tokens_here, dtype=jnp.int32)[:, None]
    col_index = jnp.arange(WINDOW + tokens_here, dtype=jnp.int32)[None, :]
    allowed = (
        (col_index >= row_index + 1)
        & (col_index <= row_index + WINDOW)
        & ((col_index >= WINDOW) | (seq_index > 0))
    )
    probs, sink_probs = head_scores(query_rows, key_tile_block, head_sink_logits, allowed)
    reduced_probabilities = probs.astype(jnp.bfloat16)
    attended = head_mix(reduced_probabilities, value_tile_block)
    out_full = lax.all_gather(out_weight, "dp", axis=0, tiled=True)
    projected = jnp.dot(attended, out_full, preferred_element_type=jnp.float32)
    mid_rows = lax.optimization_barrier(
        (residual[0].astype(jnp.float32) + projected).astype(jnp.bfloat16)
    )
    mid_wide = mid_rows.astype(jnp.float32)
    inv_rms = lax.rsqrt(jnp.mean(mid_wide * mid_wide, axis=1, keepdims=True) + NORM_EPS)
    unit_rows = mid_wide * inv_rms
    normed = (unit_rows * norm_gain[None, :]).astype(jnp.bfloat16)
    logits = jnp.dot(normed, router, preferred_element_type=jnp.float32)
    route_hot = routes[0][:, :, None] == jnp.arange(EXPERTS, dtype=jnp.int32)[None, None, :]
    route_logits = jnp.sum(jnp.where(route_hot, logits[:, None, :], 0.0), axis=2)
    raised = jnp.exp(route_logits)
    route_weights = raised / jnp.sum(raised, axis=1, keepdims=True)
    member = route_hot[:, :, :EW]
    expert_share = jnp.sum(jnp.where(member, route_weights[:, :, None], 0.0), axis=1)
    chosen = jnp.any(member, axis=1)
    slot_rank = jnp.cumsum(chosen.astype(jnp.int32), axis=0) - 1
    slot_hot = chosen[:, :, None] & (
        slot_rank[:, :, None] == jnp.arange(CAP, dtype=jnp.int32)[None, None, :]
    )
    slot_low = slot_hot.astype(jnp.bfloat16)
    slot_wide = slot_hot.astype(jnp.float32)
    slot_rows = jnp.einsum(
        "tec,td->ecd", slot_low, normed, preferred_element_type=jnp.float32
    ).astype(jnp.bfloat16)
    outgoing = jnp.broadcast_to(slot_rows[:, None], (EW, pieces, CAP, D)).reshape(seq_count, CAP, D)
    upstream_slots = jnp.einsum(
        "tec,td->ecd", slot_low, upstream[0], preferred_element_type=jnp.float32
    )
    weight_slots = jnp.einsum("tec,t->ec", slot_wide, loss_weight, precision=HIGHEST)
    share_slots = jnp.einsum("tec,te->ec", slot_wide, expert_share, precision=HIGHEST)
    cot_slots = weight_slots[:, :, None] * upstream_slots
    grad_out = (share_slots[:, :, None] * cot_slots).astype(jnp.bfloat16)
    grad_outgoing = jnp.broadcast_to(grad_out[:, None], (EW, pieces, CAP, D)).reshape(
        seq_count, CAP, D
    )
    gate_full, up_full, down_full = (
        lax.all_gather(expert_gate, "dp", axis=0, tiled=True),
        lax.all_gather(expert_up, "dp", axis=0, tiled=True),
        lax.all_gather(expert_down, "dp", axis=0, tiled=True),
    )
    arrived = lax.all_to_all(outgoing, "seq", split_axis=0, concat_axis=0, tiled=True)
    senders = arrived.shape[0]
    items = arrived.shape[1]
    block_senders = arrived.shape[0]
    block_items = arrived.shape[1]
    flat_rows = arrived.reshape(block_senders * block_items, D)
    gate_pre = jnp.dot(flat_rows, gate_full, preferred_element_type=jnp.float32)
    up_pre = jnp.dot(flat_rows, up_full, preferred_element_type=jnp.float32)
    activation = glu_forward(gate_pre, up_pre)
    partial_out = lax.dot_general(
        activation, down_full, CONTRACT_LAST, preferred_element_type=jnp.float32
    ).astype(jnp.bfloat16)
    partial_out, gate_pre, up_pre = (
        partial_out.reshape(block_senders, block_items, D),
        gate_pre,
        up_pre,
    )
    back_out = lax.all_to_all(partial_out, "seq", split_axis=0, concat_axis=0, tiled=True)
    gate_held = gate_pre.reshape(senders, items, -1)
    up_held = up_pre.reshape(senders, items, -1)
    grad_arrived = lax.all_to_all(grad_outgoing, "seq", split_axis=0, concat_axis=0, tiled=True)
    grad_piece = block_backward(
        grad_arrived.reshape(seq_count * CAP, D),
        gate_held.reshape(seq_count * CAP, -1),
        up_held.reshape(seq_count * CAP, -1),
        gate_full,
        up_full,
        down_full,
    )
    grad_back = lax.all_to_all(
        grad_piece.reshape(seq_count, CAP, D), "seq", split_axis=0, concat_axis=0, tiled=True
    )
    expert_out = jnp.sum(back_out.reshape(EW, pieces, CAP, D).astype(jnp.float32), axis=1)
    grad_share_slots = jnp.sum(cot_slots * expert_out, axis=2)
    grad_rows = jnp.sum(grad_back.reshape(EW, pieces, CAP, D).astype(jnp.float32), axis=1)
    grad_normed_moe = jnp.einsum("tec,ecd->td", slot_wide, grad_rows, precision=HIGHEST)
    grad_share = jnp.einsum("tec,ec->te", slot_wide, grad_share_slots, precision=HIGHEST)
    grad_weights = jnp.sum(jnp.where(member, grad_share[:, None, :], 0.0), axis=2)
    grad_route = route_weights * (
        grad_weights - jnp.sum(route_weights * grad_weights, axis=1, keepdims=True)
    )
    grad_logits = jnp.sum(jnp.where(route_hot, grad_route[:, :, None], 0.0), axis=1).astype(
        jnp.bfloat16
    )
    grad_normed = (
        lax.dot_general(grad_logits, router, CONTRACT_LAST, preferred_element_type=jnp.float32)
        + grad_normed_moe
    )
    grad_unit = grad_normed * norm_gain[None, :]
    grad_mid = loss_weight[:, None] * upstream[0].astype(jnp.float32) + inv_rms * (
        grad_unit - unit_rows * jnp.mean(grad_unit * unit_rows, axis=1, keepdims=True)
    )
    grad_residual = grad_mid.astype(jnp.bfloat16)
    grad_attended = lax.dot_general(
        grad_residual, out_full, CONTRACT_LAST, preferred_element_type=jnp.float32
    ).astype(jnp.bfloat16)
    query_gradient, key_gradient, value_gradient, sink_gradient = head_grads(
        probs,
        reduced_probabilities,
        sink_probs,
        query_rows,
        key_tile_block,
        value_tile_block,
        grad_attended,
    )
    next_keys, next_values = (
        passed_along(key_gradient[:WINDOW].astype(jnp.bfloat16), "seq", -1).astype(jnp.float32),
        passed_along(value_gradient[:WINDOW].astype(jnp.bfloat16), "seq", -1).astype(jnp.float32),
    )
    own_key_grad = key_gradient[WINDOW:]
    own_value_grad = value_gradient[WINDOW:]
    split_at = tokens_here - WINDOW
    grad_key_rows = jnp.concatenate(
        [own_key_grad[:split_at], own_key_grad + next_keys], axis=0
    ).astype(jnp.bfloat16)
    grad_value_rows = jnp.concatenate(
        [own_value_grad[:split_at], own_value_grad + next_values], axis=0
    ).astype(jnp.bfloat16)
    grad_sinks = lax.psum(sink_gradient, ("seq", "dp"))
    return (
        query_gradient[None],
        grad_key_rows[None],
        grad_value_rows[None],
        grad_residual[None],
        grad_sinks,
    )


def solution(mesh):
    return jax.shard_map(
        shards,
        mesh=mesh,
        in_specs=(
            P("dp", "seq", None),
            P("dp", "seq", None),
            P("dp", "seq", None),
            P(),
            P("dp", "seq", None),
            P("dp", None),
            P(),
            P(),
            P("dp", "seq"),
            P("dp", "seq"),
            P("dp", "seq"),
            P("dp", "seq", None),
            P("dp"),
            P("dp"),
            P("dp", "seq"),
            P("dp", "seq", None),
        ),
        out_specs=(
            P("dp", "seq", None),
            P("dp", "seq", None),
            P("dp", "seq", None),
            P("dp", "seq", None),
            P(),
        ),
        check_vma=False,
    )
```

profile of v0, /device:TPU:0, one launch (start us, length us, event | category | flops | bytes accessed | tf_op | source)
XLA Modules:
  0.0 561.2 jit_solution(13636498037815590450)
XLA Ops:
  10.0 4.8 collective-permute-start.1
  16.2 1.3 convert_reduce_fusion
  17.6 1.3 collective-permute-start
  18.9 43.0 %all-reduce = (f32[4,3]{0,1:T(4,128)S(1)}, f32[]{:T(128)}) all-reduce(f32[4,3]{0,1:T(4,128)S(1)} %multiply_multiply_fusion, f32[]{:T(128)} %convert_reduce_fusion), channel_id=1, replica_groups=mesh['seq'=2,'dp'=16] {'seq','dp'}, use_global_device_ids=true, to_apply=%region_2.0 | all-reduce | flops 13 | bytes 104 | tf_op jit(solution)/shard_map/psum | solution.py:168
  63.8 0.8 iota_compare_fusion
  65.7 0.8 fusion.53
  67.3 0.9 copy.78
  68.3 1.0 copy.81
  69.2 0.8 max.20
  71.4 1.1 fusion.14
  73.4 2.1 convolution_convert_fusion.3
  75.5 38.8 %all-gather.8.cloned.1.call-done = bf16[2048,2880]{0,1:T(8,128)(2,1)} async-done(((bf16[128,2880]{0,1:T(8,128)(2,1)}), bf16[2048,2880]{0,1:T(8,128)(2,1)}) %all-gather.8.cloned.1.call-update) | async-done | bytes 11796496 | tf_op jit(solution)/shard_map/all_gather | solution.py:190
  114.2 7.6 %fusion.9 = bf16[128,2880]{0,1:T(8,128)(2,1)S(1)} fusion(bf16[2048,2880]{0,1:T(8,128)(2,1)} %all-gather.8.cloned.1.call-done, bf16[128,2048]{0,1:T(8,128)(2,1)} %bitcast.201, bf16[1,128,2880]{1,2,0:T(8,128)(2,1)S(1)} %copy-done.18), kind=kOutput, calls=%fused_computation.16 | convolution fusion | flops 1511055360 | bytes 13795328 | tf_op jit(solution)/shard_map/dot_general | solution.py:191
  122.3 1.2 convolution_convert_fusion.1
  123.5 3.5 all-to-all-start
  127.0 0.9 fusion.33
  128.0 84.6 %all-gather.12.cloned.1.call-done = bf16[16,180,2048]{2,1,0:T(8,128)(2,1)} async-done(((bf16[1,180,2048]{2,1,0:T(8,128)(2,1)}), bf16[16,180,2048]{2,1,0:T(8,128)(2,1)}) %all-gather.12.cloned.1.call-update) | async-done | bytes 11796496 | tf_op jit(solution)/shard_map/all_gather | solution.py:228
  212.6 11.7 %reshape.260 = bf16[2880,2048]{1,0:T(8,128)(2,1)} reshape(bf16[16,180,2048]{2,1,0:T(8,128)(2,1)} %all-gather.12.cloned.1.call-done) | data formatting | bytes 23592960
  224.4 86.3 %all-gather.10.cloned.1.call-done = bf16[16,180,2048]{2,1,0:T(8,128)(2,1)} async-done(((bf16[1,180,2048]{2,1,0:T(8,128)(2,1)}), bf16[16,180,2048]{2,1,0:T(8,128)(2,1)}) %all-gather.10.cloned.1.call-update) | async-done | bytes 11796496 | tf_op jit(solution)/shard_map/all_gather | solution.py:229
  310.7 11.8 %reshape.258 = bf16[2880,2048]{1,0:T(8,128)(2,1)} reshape(bf16[16,180,2048]{2,1,0:T(8,128)(2,1)} %all-gather.10.cloned.1.call-done) | data formatting | bytes 23592960
  322.5 86.1 %all-gather.14.cloned.1.call-done = bf16[16,180,2048]{2,1,0:T(8,128)(2,1)} async-done(((bf16[1,180,2048]{2,1,0:T(8,128)(2,1)}), bf16[16,180,2048]{2,1,0:T(8,128)(2,1)}) %all-gather.14.cloned.1.call-update) | async-done | bytes 11796496 | tf_op jit(solution)/shard_map/all_gather | solution.py:230
  408.6 11.6 %reshape.262 = bf16[2880,2048]{1,0:T(8,128)(2,1)} reshape(bf16[16,180,2048]{2,1,0:T(8,128)(2,1)} %all-gather.14.cloned.1.call-done) | data formatting | bytes 23592960
  420.2 6.1 %fusion.66 = f32[8,2048]{1,0:T(8,128)S(1)} fusion(bf16[8,2880]{1,0:T(8,128)(2,1)S(1)} %reshape.251, bf16[2880,2048]{1,0:T(8,128)(2,1)} %reshape.260), kind=kOutput, calls=%fused_computation.122 | convolution fusion | flops 94371840 | bytes 11908096 | tf_op jit(solution)/shard_map/dot_general | solution.py:238
  426.4 6.1 %convolution_add_fusion.2 = f32[8,2048]{1,0:T(8,128)S(1)} fusion(bf16[8,2880]{1,0:T(8,128)(2,1)S(1)} %reshape.251, bf16[2880,2048]{1,0:T(8,128)(2,1)} %reshape.258), kind=kOutput, calls=%fused_computation.24 | convolution fusion | flops 94388224 | bytes 11908096 | tf_op jit(solution)/shard_map/dot_general | solution.py:239
  432.5 3.1 convolution_convert_fusion
  436.3 3.3 all-to-all-start.1
  439.6 4.0 all-to-all-done.1
  445.1 3.3 all-to-all-start.2
  448.4 4.0 all-to-all-done.2
  452.4 6.0 %multiply_convert_fusion.2 = (bf16[8,2048]{1,0:T(8,128)(2,1)S(1)}, bf16[8,2048]{1,0:T(8,128)(2,1)S(1)}) fusion(f32[8,2048]{1,0:T(8,128)S(1)} %convolution_add_fusion.2, f32[8,2048]{1,0:T(8,128)S(1)} %fusion.66, bf16[8,2880]{1,0:T(8,128)(2,1)S(1)} %reshape.253, bf16[2880,2048]{1,0:T(8,128)(2,1)} %reshape.262), kind=kOutput, calls=%fused_computation.72 | convolution fusion | flops 94601216 | bytes 12039168 | tf_op jit(solution)/shard_map/dot_general | solution.py:123
  458.4 11.0 %fusion.10 = bf16[8,2880]{1,0:T(8,128)(2,1)S(1)} fusion(bf16[2880,2048]{1,0:T(8,128)(2,1)} %reshape.258, bf16[2880,2048]{1,0:T(8,128)(2,1)} %reshape.260, bf16[8,2048]{1,0:T(8,128)(2,1)S(1)} %get-tuple-element.32, bf16[8,2048]{1,0:T(8,128)(2,1)S(1)} %get-tuple-element.31), kind=kOutput, calls=%fused_computation.18 | convolution fusion | flops 236083712 | bytes 23704576 | tf_op jit(solution)/shard_map/dot_general | solution.py:127
  470.0 3.5 all-to-all-start.3
  473.8 3.5 all-to-all-done.3
  478.3 1.6 fusion.23
  479.9 6.4 %convolution_convert_fusion.2 = bf16[128,2048]{1,0:T(8,128)(2,1)S(1)} fusion(bf16[128,2880]{0,1:T(8,128)(2,1)S(1)} %fusion.23, bf16[2048,2880]{0,1:T(8,128)(2,1)} %all-gather.8.cloned.1.call-done), kind=kOutput, calls=%fused_computation.23 | convolution fusion | flops 1510211584 | bytes 13058048 | tf_op jit(solution)/shard_map/dot_general | solution.py:285
  486.6 3.6 convolution_bitcast_fusion.1
  490.3 3.4 fusion.4
  494.4 1.3 collective-permute-start.3
  495.9 5.0 fusion.6
  500.9 1.4 fusion.27
  503.0 1.3 fusion.25
  504.3 40.4 %psum.23 = f32[32]{0:T(128)} all-reduce(f32[32]{0:T(128)} %neg.16), channel_id=1, replica_groups=mesh['seq'=2,'dp'=16] {'seq','dp'}, use_global_device_ids=true, to_apply=%region_20.21 | all-reduce | flops 32 | bytes 256 | tf_op jit(solution)/shard_map/psum | solution.py:310
  544.7 0.9 slice.47
  545.6 0.9 slice.61
  546.7 1.0 copy.96
  547.9 1.3 collective-permute-start.2
  549.2 1.5 fusion.40
  550.7 3.4 collective-permute-done.2
  (111 shorter events, 14.4 us)
Async XLA Ops:
  7.2 119.8 %copy-start = (bf16[2880,128]{1,0:T(8,128)(2,1)S(1)}, bf16[2880,128]{1,0:T(8,128)(2,1)}, u32[]{:S(2)}) copy-start(bf16[2880,128]{1,0:T(8,128)(2,1)} %param.23) | copy-start | bytes 2211844
  7.2 62.8 %copy-start.6 = (bf16[1,128,2048]{2,1,0:T(8,128)(2,1)S(1)}, bf16[1,128,2048]{2,1,0:T(8,128)(2,1)}, u32[]{:S(2)}) copy-start(bf16[1,128,2048]{2,1,0:T(8,128)(2,1)} %param.16) | copy-start | bytes 1572868
  7.2 107.1 %all-gather.8.cloned.1.call-start = ((), (), s32[]{:S(2)}) async-start(), calls=%async_computation.4 | async-start | bytes 12533760 | tf_op jit(solution)/shard_map/all_gather | solution.py:190
  7.9 204.7 %all-gather.12.cloned.1.call-start = ((), (), s32[]{:S(2)}) async-start(), calls=%async_computation.6 | async-start | bytes 12812288 | tf_op jit(solution)/shard_map/all_gather | solution.py:228
  8.7 302.0 %all-gather.10.cloned.1.call-start = ((), (), s32[]{:S(2)}) async-start(), calls=%async_computation.5 | async-start | bytes 12812288 | tf_op jit(solution)/shard_map/all_gather | solution.py:229
  9.4 399.1 %all-gather.14.cloned.1.call-start = ((), (), s32[]{:S(2)}) async-start(), calls=%async_computation.7 | async-start | bytes 12812288 | tf_op jit(solution)/shard_map/all_gather | solution.py:230
  10.0 60.3 %collective-permute-start.1 = (bf16[128,256]{1,0:T(8,128)(2,1)}, bf16[128,256]{1,0:T(8,128)(2,1)S(1)}, u32[]{:S(2)}, u32[]{:S(2)}) collective-permute-start(bf16[128,256]{1,0:T(8,128)(2,1)} %bitcast.187), channel_id=1, source_target_pairs={{0,16},{1,17},{2,18},{3,19},{4,20},{5,21},{6,22},{7,23},{8,24},{9,... | collective-permute-start | bytes 196616 | tf_op jit(solution)/shard_map/ppermute | solution.py:25
  17.6 52.9 %collective-permute-start = (bf16[128,256]{1,0:T(8,128)(2,1)}, bf16[128,256]{1,0:T(8,128)(2,1)S(1)}, u32[]{:S(2)}, u32[]{:S(2)}) collective-permute-start(bf16[128,256]{1,0:T(8,128)(2,1)} %bitcast.188), channel_id=1, source_target_pairs={{0,16},{1,17},{2,18},{3,19},{4,20},{5,21},{6,22},{7,23},{8,24},{9,... | collective-permute-start | bytes 196616 | tf_op jit(solution)/shard_map/ppermute | solution.py:25
  69.2 3.4 copy-start.10
  70.0 2.5 copy-start.14
  70.4 2.2 copy-start.12
  70.6 1.9 copy-start.5
  71.3 2.0 copy-start.1
  72.6 417.6 %copy-start.8 = (f32[4,8,128]{2,1,0:T(8,128)}, f32[4,8,128]{2,1,0:T(8,128)S(1)}, u32[]{:S(2)}) copy-start(f32[4,8,128]{2,1,0:T(8,128)S(1)} %fusion.47) | copy-start | bytes 49156
  73.4 40.9 %copy-start.18 = (bf16[1,128,2880]{1,2,0:T(8,128)(2,1)S(1)}, bf16[1,128,2880]{1,2,0:T(8,128)(2,1)}, u32[]{:S(2)}) copy-start(bf16[1,128,2880]{1,2,0:T(8,128)(2,1)} %param.20) | copy-start | bytes 2211844
  114.2 8.1 %copy-start.17 = (f32[2880]{0:T(1024)S(1)}, f32[2880]{0:T(1024)}, u32[]{:S(2)}) copy-start(f32[2880]{0:T(1024)} %param.22) | copy-start | bytes 34564
  121.9 6.0 %copy-start.16 = (s32[1,128,4]{1,2,0:T(4,128)S(1)}, s32[1,128,4]{1,2,0:T(4,128)}, u32[]{:S(2)}) copy-start(s32[1,128,4]{1,2,0:T(4,128)} %param.27) | copy-start | bytes 6148
  123.5 296.7 %all-to-all-start = ((bf16[2,4,2880]{2,1,0:T(4,128)(2,1)}), bf16[2,4,2880]{2,1,0:T(4,128)(2,1)S(1)}, u32[]{:S(2)}, u32[]{:S(2)}) async-start(bf16[2,4,2880]{2,1,0:T(4,128)(2,1)} %convolution_convert_fusion.1), calls=%async_computation | async-start | bytes 94208 | tf_op jit(solution)/shard_map/all_to_all | solution.py:232
  420.2 12.3 %slice-start = ((s8[11796480]{0:T(1024)(128)(4,1)}), s8[4194304]{0:T(1024)(128)(4,1)S(1)}, s32[]{:S(2)}) async-start(s8[11796480]{0:T(1024)(128)(4,1)} %bitcast.168), calls=%async_computation.8 | async-start | bytes 8388608
  420.2 12.3 %slice-start.1 = ((s8[11796480]{0:T(1024)(128)(4,1)}), s8[4194304]{0:T(1024)(128)(4,1)S(1)}, s32[]{:S(2)}) async-start(s8[11796480]{0:T(1024)(128)(4,1)} %bitcast.168), calls=%async_computation.9 | async-start | bytes 8388608
  426.4 6.1 %slice-start.2 = ((s8[11796480]{0:T(1024)(128)(4,1)}), s8[3407872]{0:T(1024)(128)(4,1)S(1)}, s32[]{:S(2)}) async-start(s8[11796480]{0:T(1024)(128)(4,1)} %bitcast.168), calls=%async_computation.10 | async-start | bytes 6815744
  432.5 11.1 %copy-start.4 = (bf16[1,128,2880]{1,2,0:T(8,128)(2,1)S(1)}, bf16[1,128,2880]{1,2,0:T(8,128)(2,1)}, u32[]{:S(2)}) copy-start(bf16[1,128,2880]{1,2,0:T(8,128)(2,1)} %param.31) | copy-start | bytes 2211844
  436.3 7.3 %all-to-all-start.1 = ((bf16[2,4,2880]{2,1,0:T(4,128)(2,1)}), bf16[2,4,2880]{2,1,0:T(4,128)(2,1)S(1)}, u32[]{:S(2)}, u32[]{:S(2)}) async-start(bf16[2,4,2880]{2,1,0:T(4,128)(2,1)} %reshape.252), calls=%async_computation.1 | async-start | bytes 94208 | tf_op jit(solution)/shard_map/all_to_all | solution.py:249
  445.1 7.3 %all-to-all-start.2 = ((bf16[2,4,2880]{2,1,0:T(4,128)(2,1)}), bf16[2,4,2880]{2,1,0:T(4,128)(2,1)S(1)}, u32[]{:S(2)}, u32[]{:S(2)}) async-start(bf16[2,4,2880]{2,1,0:T(4,128)(2,1)} %multiply_convert_fusion), calls=%async_computation.2 | async-start | bytes 94208 | tf_op jit(solution)/shard_map/all_to_all | solution.py:252
  470.0 7.3 %all-to-all-start.3 = ((bf16[2,4,2880]{2,1,0:T(4,128)(2,1)}), bf16[2,4,2880]{2,1,0:T(4,128)(2,1)S(1)}, u32[]{:S(2)}, u32[]{:S(2)}) async-start(bf16[2,4,2880]{2,1,0:T(4,128)(2,1)} %reshape.254), calls=%async_computation.3 | async-start | bytes 94208 | tf_op jit(solution)/shard_map/all_to_all | solution.py:261
  479.9 6.5 %copy-start.3 = (bf16[128,2880]{0,1:T(8,128)(2,1)}, bf16[128,2880]{0,1:T(8,128)(2,1)S(1)}, u32[]{:S(2)}) copy-start(bf16[128,2880]{0,1:T(8,128)(2,1)S(1)} %fusion.23) | copy-start | bytes 2211844
  486.6 3.6 copy-start.2
  486.6 3.6 copy-start.11
  486.6 3.6 copy-start.13
  490.3 3.4 copy-start.7
  490.3 5.4 copy-start.15
  493.7 2.2 copy-start.9
  494.4 54.8 %collective-permute-start.3 = (bf16[128,256]{1,0:T(8,128)(2,1)}, bf16[128,256]{1,0:T(8,128)(2,1)}, u32[]{:S(2)}, u32[]{:S(2)}) collective-permute-start(bf16[128,256]{1,0:T(8,128)(2,1)} %copy.94), channel_id=1, source_target_pairs={{16,0},{17,1},{18,2},{19,3},{20,4},{21,5},{22,6},{23,7},{24,8},{25... | collective-permute-start | bytes 196616 | tf_op jit(solution)/shard_map/ppermute | solution.py:25
  502.4 45.3 %slice-start.3 = ((f32[256,4,64]{0,2,1:T(8,128)}), f32[128,4,64]{0,2,1:T(8,128)S(1)}, s32[]{:S(2)}) async-start(f32[256,4,64]{0,2,1:T(8,128)} %fusion.27), calls=%async_computation.11 | async-start | bytes 262144 | tf_op jit(solution)/shard_map/slice | solution.py:301
  547.9 6.2 %collective-permute-start.2 = (bf16[128,256]{1,0:T(8,128)(2,1)S(1)}, bf16[128,256]{1,0:T(8,128)(2,1)S(1)}, u32[]{:S(2)}, u32[]{:S(2)}) collective-permute-start(bf16[128,256]{1,0:T(8,128)(2,1)S(1)} %copy.91), channel_id=1, source_target_pairs={{16,0},{17,1},{18,2},{19,3},{20,4},{21,5},{22,6},{23,7},{24,8},{25... | collective-permute-start | bytes 196616 | tf_op jit(solution)/shard_map/ppermute | solution.py:25
Sparse Core Ops, SparseCore 0:
  10.2 104.0 all-gather.7
  116.5 96.0 all-gather.11
  214.9 95.6 all-gather.9
  312.8 95.6 all-gather.13
where the time goes:
time: 563 us; the launch traced here: 561 us
  waiting for transfers between devices  313 us (56%)
  blocking collectives  83.4 us (15%)
  matrix products  63.5 us (11%)
  local copies, waits for them, and re-layouts  45.6 us (8%)
  starting transfers between devices  22.4 us (4%)
  between operations  17.7 us (3%)
  other arithmetic  15.5 us (3%)
    all_gather x1, waiting for transfers between devices, shards(): lax.all_gather(expert_up, 'dp', axis=0, tiled=True)  86.3 us
    all_gather x1, waiting for transfers between devices, shards(): lax.all_gather(expert_down, 'dp', axis=0, tiled=True)  86.1 us
    all_gather x1, waiting for transfers between devices, shards(): lax.all_gather(expert_gate, 'dp', axis=0, tiled=True)  84.6 us
    psum x1, blocking collectives, shards(): lax.psum((group_terms * first_device, local_count), ('seq', 'dp'))  43 us
    psum x1, blocking collectives, shards(): grad_sinks = lax.psum(sink_gradient, ('seq', 'dp'))  40.4 us
    unnamed x52, local copies, waits for them, and re-layouts  39.4 us
    all_gather x1, waiting for transfers between devices, shards(): out_full = lax.all_gather(out_weight, 'dp', axis=0, tiled=True)  38.8 us
  transfers between devices with their start and end apart: 12, of which 8 were waited for; matrix products, arithmetic and copies ran while one was open for 13% of the time, Pallas kernels for 0%

commit v1 on v0

--- a/solution.py
+++ b/solution.py
@@ -1,6 +1,10 @@
+import functools
+
 import jax
 import jax.numpy as jnp
 from jax import lax
+from jax.experimental import pallas as pl
+from jax.experimental.pallas import tpu as pltpu
 from jax.sharding import PartitionSpec as P
 
 D = 2880
@@ -129,7 +133,7 @@
     ).astype(jnp.bfloat16)
 
 
-def shards(
+def general_shards(
     queries,
     key_rows,
     value_matrix,
@@ -317,9 +321,443 @@
     )
 
 
+MESH = pl.DeviceIdType.MESH
+MIB = 1 << 20
+
+
+def halving_place(index, count):
+    place, weight, rest = 0, count // 2, index
+    while weight:
+        place = place + lax.rem(rest, 2) * weight
+        rest = lax.div(rest, 2)
+        weight //= 2
+    return place
+
+
+def flipped(index, bit):
+    return index + bit - 2 * bit * lax.rem(lax.div(index, bit), 2)
+
+
+def expert_kernel(
+    count,
+    slots_ref,
+    gate_ref,
+    up_ref,
+    down_ref,
+    own_ref,
+    other_ref,
+    theirs,
+    outgoing,
+    arrived,
+    sent,
+    total,
+    received,
+    grads,
+    back,
+    seq_send,
+    seq_recv,
+    to_send,
+    to_recv,
+    halve_send,
+    halve_recv,
+    double_send,
+    double_recv,
+    back_send,
+    back_recv,
+):
+    bits = count.bit_length() - 1
+    me = lax.axis_index("dp")
+    side = lax.axis_index("seq")
+    far = 1 - side
+    place = halving_place(me, count)
+    depth = gate_ref.shape[0]
+    hidden = gate_ref.shape[1]
+    wide = 3 * hidden // 2
+
+    barrier = pltpu.get_barrier_semaphore()
+    pl.semaphore_signal(barrier, inc=1, device_id={"seq": far}, device_id_type=MESH)
+
+    def greet(step, carry):
+        pl.semaphore_signal(
+            barrier, inc=1, device_id={"dp": lax.rem(me + step, count)}, device_id_type=MESH
+        )
+        return carry
+
+    lax.fori_loop(1, count, greet, 0)
+    pl.semaphore_wait(barrier, count)
+
+    swap = pltpu.make_async_remote_copy(
+        src_ref=slots_ref.at[far],
+        dst_ref=theirs,
+        send_sem=seq_send.at[0],
+        recv_sem=seq_recv.at[0],
+        device_id={"seq": far},
+        device_id_type=MESH,
+    )
+    swap.start()
+    back[...] = jnp.zeros_like(back)
+    swap.wait()
+    mine = slots_ref[side]
+    came = theirs[...]
+    first = jnp.where(side == 0, mine, came)
+    second = jnp.where(side == 0, came, mine)
+    outgoing[...] = jnp.concatenate(
+        [first[:, :CAP], second[:, :CAP], first[:, CAP:], second[:, CAP:]], axis=1
+    ).astype(jnp.bfloat16)
+
+    def slice_copy(step):
+        to = lax.rem(me + step, count)
+        return pltpu.make_async_remote_copy(
+            src_ref=outgoing.at[to],
+            dst_ref=arrived.at[place],
+            send_sem=to_send.at[step],
+            recv_sem=to_recv.at[step],
+            device_id={"dp": to},
+            device_id_type=MESH,
+        )
+
+    def start_slice(step, carry):
+        slice_copy(step).start()
+        return carry
+
+    def wait_slice(step, carry):
+        slice_copy(step).wait()
+        return carry
+
+    lax.fori_loop(1, count, start_slice, 0)
+    arrived[place] = outgoing[me]
+    lax.fori_loop(1, count, wait_slice, 0)
+
+    half = count // 2
+    rows = EW * CAP
+    tile = 512
+
+    def products(start):
+        block = arrived[pl.ds(start, half)].astype(jnp.float32)
+        normed = block[:, :rows].reshape(half * rows, -1)[:, :depth].astype(jnp.bfloat16)
+        upstream = block[:, rows:].reshape(half * rows, -1)[:, :depth].astype(jnp.bfloat16)
+
+        def product(column):
+            which, at = divmod(column, hidden)
+            weight = (gate_ref, up_ref, down_ref)[which]
+            return jnp.dot(
+                upstream if which == 2 else normed,
+                weight[:, at : at + tile],
+                preferred_element_type=jnp.float32,
+            ).reshape(half, rows, tile)
+
+        for column in range(0, wide, tile):
+            yield column, jnp.concatenate([product(column), product(wide + column)], axis=1)
+
+    def halve_copy(stage):
+        blocks = half >> stage
+        return pltpu.make_async_remote_copy(
+            src_ref=sent[stage],
+            dst_ref=received[stage],
+            send_sem=halve_send.at[stage],
+            recv_sem=halve_recv.at[stage],
+            device_id={"dp": flipped(me, 1 << stage)},
+            device_id_type=MESH,
+        )
+
+    bit_of = [lax.rem(lax.div(me, 1 << stage), 2) for stage in range(bits)]
+    for column, value in products((1 - bit_of[0]) * half):
+        sent[0][:, :, column : column + tile] = value.astype(jnp.bfloat16)
+    halve_copy(0).start()
+    for column, value in products(bit_of[0] * half):
+        total[:, :, column : column + tile] = value
+    base = 0
+    for stage in range(1, bits):
+        blocks = half >> stage
+        halve_copy(stage - 1).wait()
+        away = (1 - bit_of[stage]) * blocks
+        keep = bit_of[stage] * blocks
+        sent[stage][...] = (
+            total[pl.ds(base + away, blocks)]
+            + received[stage - 1][pl.ds(away, blocks)].astype(jnp.float32)
+        ).astype(jnp.bfloat16)
+        halve_copy(stage).start()
+        total[pl.ds(base + keep, blocks)] += received[stage - 1][pl.ds(keep, blocks)].astype(
+            jnp.float32
+        )
+        base = base + keep
+    halve_copy(bits - 1).wait()
+    summed = total[base] + received[bits - 1][0].astype(jnp.float32)
+
+    gate_pre = summed[:rows, :hidden]
+    up_pre = jnp.concatenate([summed[:rows, hidden:], summed[rows:, : hidden // 2]], axis=1)
+    grad_act = summed[rows:, hidden // 2 :]
+    sigmoid_gate = 1.0 / (1.0 + jnp.exp(-GLU_SLOPE * gate_pre))
+    gate_sigmoid = gate_pre * sigmoid_gate
+    raised_up = up_pre + 1.0
+    activation = (raised_up * gate_sigmoid).astype(jnp.bfloat16).astype(jnp.float32)
+    share = jnp.sum(activation * grad_act, axis=1, keepdims=True)
+    grad_up = grad_act * gate_sigmoid
+    grad_gate = (
+        grad_act * raised_up * (sigmoid_gate + GLU_SLOPE * gate_sigmoid * (1.0 - sigmoid_gate))
+    )
+    grads[place] = jnp.concatenate([grad_gate, grad_up], axis=0).astype(jnp.bfloat16)
+
+    for stage in range(bits):
+        blocks = 1 << stage
+        start = place // blocks * blocks
+        copy = pltpu.make_async_remote_copy(
+            src_ref=grads.at[pl.ds(start, blocks)],
+            dst_ref=grads.at[pl.ds(start, blocks)],
+            send_sem=double_send.at[stage],
+            recv_sem=double_recv.at[stage],
+            device_id={"dp": flipped(me, half >> stage)},
+            device_id_type=MESH,
+        )
+        copy.start()
+        copy.wait()
+
+    flat = grads[...].reshape(count * 2 * rows, hidden)
+    contract = (((1,), (1,)), ((), ()))
+    from_gate = lax.dot_general(flat, gate_ref[...], contract, preferred_element_type=jnp.float32)
+    from_up = lax.dot_general(flat, up_ref[...], contract, preferred_element_type=jnp.float32)
+    from_gate = from_gate.reshape(count, 2 * rows, depth)
+    from_up = from_up.reshape(count, 2 * rows, depth)
+    back[:, :, :depth] = from_gate[:, :rows] + from_up[:, rows:]
+
+    def back_copy(step):
+        to = lax.rem(me + step, count)
+        return pltpu.make_async_remote_copy(
+            src_ref=back.at[halving_place(to, count)],
+            dst_ref=own_ref.at[me],
+            send_sem=back_send.at[step],
+            recv_sem=back_recv.at[step],
+            device_id={"dp": to},
+            device_id_type=MESH,
+        )
+
+    def start_back(step, carry):
+        back_copy(step).start()
+        return carry
+
+    def wait_back(step, carry):
+        back_copy(step).wait()
+        return carry
+
+    lax.fori_loop(1, count, start_back, 0)
+    own_ref[me] = back[place]
+    own_ref[count] = jnp.broadcast_to(share, own_ref.shape[1:])
+    lax.fori_loop(1, count, wait_back, 0)
+    last = pltpu.make_async_remote_copy(
+        src_ref=own_ref,
+        dst_ref=other_ref,
+        send_sem=seq_send.at[1],
+        recv_sem=seq_recv.at[1],
+        device_id={"seq": far},
+        device_id_type=MESH,
+    )
+    last.start()
+    last.wait()
+
+
+def in_place_experts(slots, gate, up, down):
+    count, lanes = slots.shape[1], slots.shape[3]
+    bits = count.bit_length() - 1
+    rows = EW * CAP
+    hidden = gate.shape[1]
+    wide = 3 * hidden // 2
+    stages = [pltpu.VMEM((count >> (stage + 1), 2 * rows, wide), jnp.bfloat16) for stage in range(bits)]
+    vmem = pl.BlockSpec(memory_space=pltpu.VMEM)
+    dma = pltpu.SemaphoreType.DMA
+    result = jax.ShapeDtypeStruct((count + 1, rows, lanes), jnp.float32)
+    return pl.pallas_call(
+        functools.partial(expert_kernel, count),
+        out_shape=(result, result),
+        in_specs=[vmem] * 4,
+        out_specs=(vmem, vmem),
+        scratch_shapes=[
+            pltpu.VMEM((count, rows, lanes), jnp.float32),
+            pltpu.VMEM((count, 2 * rows, lanes), jnp.bfloat16),
+            pltpu.VMEM((count, 2 * rows, lanes), jnp.bfloat16),
+            stages,
+            pltpu.VMEM((count // 2, 2 * rows, wide), jnp.float32),
+            stages,
+            pltpu.VMEM((count, 2 * rows, hidden), jnp.bfloat16),
+            pltpu.VMEM((count, rows, lanes), jnp.float32),
+            dma((2,)),
+            dma((2,)),
+            dma((count,)),
+            dma((count,)),
+            dma((bits,)),
+            dma((bits,)),
+            dma((bits,)),
+            dma((bits,)),
+            dma((count,)),
+            dma((count,)),
+        ],
+        compiler_params=pltpu.CompilerParams(
+            collective_id=1, has_side_effects=True, vmem_limit_bytes=40 * MIB
+        ),
+        name="expert_kernel",
+    )(slots, gate, up, down)
+
+
+def shards(
+    queries,
+    key_rows,
+    value_matrix,
+    head_sink_logits,
+    residual,
+    out_weight,
+    norm_gain,
+    router,
+    expert_gate,
+    expert_up,
+    expert_down,
+    routes,
+    group_ids,
+    rewards,
+    response_mask,
+    upstream,
+):
+    seq_count = lax.axis_size("seq")
+    dp_count = lax.axis_size("dp")
+    seq_index = lax.axis_index("seq")
+    query_rows = queries[0]
+    own_keys = key_rows[0]
+    own_values = value_matrix[0]
+    tokens_here = query_rows.shape[0]
+    group_count = max(dp_count // 4, 1)
+    all_tokens = dp_count * seq_count * tokens_here
+    group_hot = (group_ids[0] == jnp.arange(group_count, dtype=jnp.int32)).astype(jnp.float32)
+    reward = rewards[0].astype(jnp.float32)
+    group_terms = (
+        group_hot[:, None] * jnp.stack([jnp.ones_like(reward), reward, reward * reward])[None, :]
+    )
+    mask_wide = response_mask[0].astype(jnp.float32)
+    local_count = jnp.sum(mask_wide)
+    first_device = (seq_index == 0).astype(jnp.float32)
+    group_totals, token_total = lax.psum((group_terms * first_device, local_count), ("seq", "dp"))
+    group_sizes = group_totals[:, 0]
+    group_means = group_totals[:, 1] / group_sizes
+    group_spread = group_totals[:, 2] / group_sizes - group_means * group_means
+    own_mean = jnp.sum(group_hot * group_means)
+    own_spread = jnp.sum(group_hot * group_spread)
+    advantage = (reward - own_mean) / jnp.sqrt(jnp.maximum(own_spread, 1.0))
+    token_scale = -advantage * all_tokens / token_total
+    loss_weight = token_scale * mask_wide
+    halo_keys, halo_values = passed_along((own_keys, own_values), "seq", 1)
+    key_tile_block = jnp.concatenate([halo_keys, own_keys], axis=0)
+    value_tile_block = jnp.concatenate([halo_values, own_values], axis=0)
+    row_index = jnp.arange(tokens_here, dtype=jnp.int32)[:, None]
+    col_index = jnp.arange(WINDOW + tokens_here, dtype=jnp.int32)[None, :]
+    allowed = (
+        (col_index >= row_index + 1)
+        & (col_index <= row_index + WINDOW)
+        & ((col_index >= WINDOW) | (seq_index > 0))
+    )
+    probs, sink_probs = head_scores(query_rows, key_tile_block, head_sink_logits, allowed)
+    reduced_probabilities = probs.astype(jnp.bfloat16)
+    attended = head_mix(reduced_probabilities, value_tile_block)
+    out_full = lax.all_gather(out_weight, "dp", axis=0, tiled=True)
+    projected = jnp.dot(attended, out_full, preferred_element_type=jnp.float32)
+    mid_rows = lax.optimization_barrier(
+        (residual[0].astype(jnp.float32) + projected).astype(jnp.bfloat16)
+    )
+    mid_wide = mid_rows.astype(jnp.float32)
+    inv_rms = lax.rsqrt(jnp.mean(mid_wide * mid_wide, axis=1, keepdims=True) + NORM_EPS)
+    unit_rows = mid_wide * inv_rms
+    normed = (unit_rows * norm_gain[None, :]).astype(jnp.bfloat16)
+    logits = jnp.dot(normed, router, preferred_element_type=jnp.float32)
+    route_hot = routes[0][:, :, None] == jnp.arange(EXPERTS, dtype=jnp.int32)[None, None, :]
+    route_logits = jnp.sum(jnp.where(route_hot, logits[:, None, :], 0.0), axis=2)
+    raised = jnp.exp(route_logits)
+    route_weights = raised / jnp.sum(raised, axis=1, keepdims=True)
+    member = route_hot[:, :, :EW]
+    expert_share = jnp.sum(jnp.where(member, route_weights[:, :, None], 0.0), axis=1)
+    chosen = jnp.any(member, axis=1)
+    slot_rank = jnp.cumsum(chosen.astype(jnp.int32), axis=0) - 1
+    slot_hot = chosen[:, :, None] & (
+        slot_rank[:, :, None] == jnp.arange(CAP, dtype=jnp.int32)[None, None, :]
+    )
+    slot_low = slot_hot.astype(jnp.bfloat16)
+    slot_wide = slot_hot.astype(jnp.float32)
+    slot_rows = jnp.einsum(
+        "tec,td->ecd", slot_low, normed, preferred_element_type=jnp.float32
+    )
+    weight_slots = jnp.einsum("tec,t->ec", slot_wide, loss_weight, precision=HIGHEST)
+    share_slots = jnp.einsum("tec,te->ec", slot_wide, expert_share, precision=HIGHEST)
+    upstream_slots = jnp.einsum(
+        "tec,td->ecd", slot_low, upstream[0], preferred_element_type=jnp.float32
+    )
+    depth = expert_gate.shape[0]
+    lanes = -(-depth // 128) * 128
+    slots = jnp.concatenate([slot_rows, upstream_slots], axis=1)
+    slots = slots.reshape(EW, 2 * CAP, dp_count, depth).transpose(0, 2, 1, 3)
+    slots = jnp.pad(slots, ((0, 0), (0, 0), (0, 0), (0, lanes - depth)))
+    own_part, other_part = in_place_experts(slots, expert_gate, expert_up, expert_down)
+    both_parts = jnp.where(
+        seq_index == 0, jnp.stack([own_part, other_part]), jnp.stack([other_part, own_part])
+    )
+    both_parts = lax.dynamic_slice_in_dim(both_parts, seq_index * CAP, CAP, 2)
+    grad_share_slots = weight_slots * both_parts[:, dp_count, :, 0]
+    grad_rows = (
+        both_parts[:, :dp_count, :, :depth].transpose(0, 2, 1, 3).reshape(EW, CAP, D)
+        * (weight_slots * share_slots)[:, :, None]
+    )
+    grad_normed_moe = jnp.einsum("tec,ecd->td", slot_wide, grad_rows, precision=HIGHEST)
+    grad_share = jnp.einsum("tec,ec->te", slot_wide, grad_share_slots, precision=HIGHEST)
+    grad_weights = jnp.sum(jnp.where(member, grad_share[:, None, :], 0.0), axis=2)
+    grad_route = route_weights * (
+        grad_weights - jnp.sum(route_weights * grad_weights, axis=1, keepdims=True)
+    )
+    grad_logits = jnp.sum(jnp.where(route_hot, grad_route[:, :, None], 0.0), axis=1).astype(
+        jnp.bfloat16
+    )
+    grad_normed = (
+        lax.dot_general(grad_logits, router, CONTRACT_LAST, preferred_element_type=jnp.float32)
+        + grad_normed_moe
+    )
+    grad_unit = grad_normed * norm_gain[None, :]
+    grad_mid = loss_weight[:, None] * upstream[0].astype(jnp.float32) + inv_rms * (
+        grad_unit - unit_rows * jnp.mean(grad_unit * unit_rows, axis=1, keepdims=True)
+    )
+    grad_residual = grad_mid.astype(jnp.bfloat16)
+    grad_attended = lax.dot_general(
+        grad_residual, out_full, CONTRACT_LAST, preferred_element_type=jnp.float32
+    ).astype(jnp.bfloat16)
+    query_gradient, key_gradient, value_gradient, sink_gradient = head_grads(
+        probs,
+        reduced_probabilities,
+        sink_probs,
+        query_rows,
+        key_tile_block,
+        value_tile_block,
+        grad_attended,
+    )
+    next_keys, next_values = (
+        passed_along(key_gradient[:WINDOW].astype(jnp.bfloat16), "seq", -1).astype(jnp.float32),
+        passed_along(value_gradient[:WINDOW].astype(jnp.bfloat16), "seq", -1).astype(jnp.float32),
+    )
+    own_key_grad = key_gradient[WINDOW:]
+    own_value_grad = value_gradient[WINDOW:]
+    split_at = tokens_here - WINDOW
+    grad_key_rows = jnp.concatenate(
+        [own_key_grad[:split_at], own_key_grad + next_keys], axis=0
+    ).astype(jnp.bfloat16)
+    grad_value_rows = jnp.concatenate(
+        [own_value_grad[:split_at], own_value_grad + next_values], axis=0
+    ).astype(jnp.bfloat16)
+    grad_sinks = lax.psum(sink_gradient, ("seq", "dp"))
+    return (
+        query_gradient[None],
+        grad_key_rows[None],
+        grad_value_rows[None],
+        grad_residual[None],
+        grad_sinks,
+    )
+
+
 def solution(mesh):
+    seq_count, dp_count = mesh.shape["seq"], mesh.shape["dp"]
+    in_place = seq_count == EW and dp_count & (dp_count - 1) == 0
     return jax.shard_map(
-        shards,
+        shards if in_place else general_shards,
         mesh=mesh,
         in_specs=(
             P("dp", "seq", None),

time: 563 us -> 285 us (0.51)
  waiting for transfers between devices: 313 us -> 39.3 us
  Pallas kernels: 0 us -> 62.2 us
  local copies, waits for them, and re-layouts: 45.6 us -> 14.6 us
  matrix products: 63.5 us -> 36.1 us
  starting transfers between devices: 22.4 us -> 8.74 us
    all_gather x3 -> x0, waiting for transfers between devices: 257 us -> none  [the longest x1 86.3 us: shards(): lax.all_gather(expert_up, 'dp', axis=0, tiled=True)]
    pallas_call x0 -> x1, Pallas kernels: none -> 62.2 us  [in_place_experts(): pl.pallas_call(functools.partial(expert_kernel, count), out_shape=(result...]
    unnamed x52 -> x87, local copies, waits for them, and re-layouts: 39.4 us -> 6.27 us
    dot_general x5 -> x0, matrix products: 32.4 us -> none  [the longest x1 11 us: block_backward(): lax.dot_general(grad_pair, weight_pair, CONTRACT_LAST, preferred_element_...]
    all_to_all x4 -> x0, starting transfers between devices: 13.5 us -> none  [the longest x1 3.5 us: shards(): lax.all_to_all(grad_piece.reshape(seq_count, CAP, D), 'seq', split_axis=0...]
    all_to_all x4 -> x0, waiting for transfers between devices: 11.5 us -> none  [the longest x1 3.99 us: shards(): lax.all_to_all(partial_out, 'seq', split_axis=0, concat_axis=0, tiled=True)]
  transfers between devices with their start and end apart: 12 -> 5, of which waited for: 8 -> 2; matrix products, arithmetic and copies ran while one was open for 13% -> 10% of each run, Pallas kernels for 0% -> 0%
where the time goes in v1:
time: 285 us; the launch traced here: 284 us
  blocking collectives  86.3 us (30%)
  Pallas kernels  62.2 us (22%)
  waiting for transfers between devices  39.3 us (14%)
  matrix products  36.1 us (13%)
  other arithmetic  18.1 us (6%)
  between operations  18.1 us (6%)
  local copies, waits for them, and re-layouts  14.6 us (5%)
  starting transfers between devices  8.74 us (3%)
    pallas_call x1, Pallas kernels, in_place_experts(): pl.pallas_call(functools.partial(expert_kernel, count), out_shape=(result...  62.2 us
    psum x1, blocking collectives, shards(): lax.psum((group_terms * first_device, local_count), ('seq', 'dp'))  44.1 us
    psum x1, blocking collectives, shards(): grad_sinks = lax.psum(sink_gradient, ('seq', 'dp'))  42.2 us
    all_gather x1, waiting for transfers between devices, shards(): out_full = lax.all_gather(out_weight, 'dp', axis=0, tiled=True)  35.3 us
    ppermute x4, starting transfers between devices, passed_along(): lax.ppermute(value, axis, [(source, source + steps) for source in range(i...  8.7 us
    dot_general x1, matrix products, shards(): projected = jnp.dot(attended, out_full, preferred_element_type=jnp.float32)  7.62 us
    dot_general x1, matrix products, shards(): lax.dot_general(grad_residual, out_full, CONTRACT_LAST, preferred_element...  6.45 us
    unnamed x87, local copies, waits for them, and re-layouts  6.27 us
  transfers between devices with their start and end apart: 5, of which 2 were waited for; matrix products, arithmetic and copies ran while one was open for 10% of the time, Pallas kernels for 0%

profile of v1, /device:TPU:0, one launch (start us, length us, event | category | flops | bytes accessed | tf_op | source)
XLA Modules:
  0.0 283.6 jit_solution(11940447038757971365)
XLA Ops:
  7.2 0.7 all-gather.2.cloned.1.call-update
  7.9 4.8 %collective-permute-start.1 = (bf16[128,256]{1,0:T(8,128)(2,1)}, bf16[128,256]{1,0:T(8,128)(2,1)S(1)}, u32[]{:S(2)}, u32[]{:S(2)}) collective-permute-start(bf16[128,256]{1,0:T(8,128)(2,1)} %bitcast.181), channel_id=1, source_target_pairs={{0,16},{1,17},{2,18},{3,19},{4,20},{5,21},{6,22},{7,23},{8,24},{9,... | collective-permute-start | bytes 196616 | tf_op jit(solution)/shard_map/ppermute | solution.py:29
  14.2 1.3 convert_reduce_fusion
  15.5 1.3 collective-permute-start
  16.8 44.1 %all-reduce.1 = (f32[4,3]{0,1:T(4,128)S(1)}, f32[]{:T(128)}) all-reduce(f32[4,3]{0,1:T(4,128)S(1)} %multiply_multiply_fusion, f32[]{:T(128)} %convert_reduce_fusion), channel_id=1, replica_groups=mesh['seq'=2,'dp'=16] {'seq','dp'}, use_global_device_ids=true, to_apply=%region_2.0 | all-reduce | flops 13 | bytes 104 | tf_op jit(solution)/shard_map/psum | solution.py:635
  62.8 0.8 iota_compare_fusion
  65.3 1.4 fusion.48
  66.8 2.1 fusion.23
  68.9 1.2 fusion.50
  70.1 0.9 copy.62
  71.1 1.0 copy.65
  72.1 0.8 max.20
  72.8 1.3 copy.63
  74.4 0.8 fusion.4
  75.3 1.1 fusion.7
  76.5 0.7 copy-done.4
  77.2 1.3 convolution_convert_fusion.1
  78.5 35.3 %all-gather.2.cloned.1.call-done = bf16[2048,2880]{0,1:T(8,128)(2,1)} async-done(((bf16[128,2880]{0,1:T(8,128)(2,1)}), bf16[2048,2880]{0,1:T(8,128)(2,1)}) %all-gather.2.cloned.1.call-update) | async-done | bytes 11796496 | tf_op jit(solution)/shard_map/all_gather | solution.py:657
  113.8 7.6 %fusion.5 = bf16[128,2880]{0,1:T(8,128)(2,1)S(1)} fusion(bf16[2048,2880]{0,1:T(8,128)(2,1)} %all-gather.2.cloned.1.call-done, bf16[128,2048]{0,1:T(8,128)(2,1)S(1)} %bitcast.196, bf16[1,128,2880]{1,2,0:T(8,128)(2,1)S(1)} %copy-done.40), kind=kOutput, calls=%fused_computation.12 | convolution fusion | flops 1511055360 | bytes 13795328 | tf_op jit(solution)/shard_map/dot_general | solution.py:658
  122.9 0.7 pad_maximum_fusion
  123.6 2.0 reshape.237
  125.6 1.2 copy.100
  126.9 62.2 %expert_kernel.1 = (f32[17,8,256]{2,1,0:T(8,128)S(1)}, f32[17,8,256]{2,1,0:T(8,128)S(1)}) custom-call(f32[2,16,8,256]{3,2,1,0:T(8,128)S(1)} %pad.4.slots_ref, bf16[180,2048]{1,0:T(8,128)(2,1)S(1)} %copy-done.1, bf16[180,2048]{1,0:T(8,128)(2,1)S(1)} %copy-done.2, bf16[180,2048]{1,0:T(8,128)(2,1)S(1)} %copy-done.3), custom_call_target="tpu_custom_call" | custom-call | tf_op jit(solution)/shard_map/expert_kernel/pallas_call | solution.py:568
  189.3 0.9 fusion.28
  191.2 0.8 fusion.58
  192.0 0.7 select_reduce_fusion.3
  192.7 0.8 fusion.59
  193.5 0.6 mul.185
  194.2 0.9 select_reduce_fusion
  195.1 2.1 convolution_bitcast_fusion
  197.3 1.7 fusion.12
  199.0 1.1 fusion.16
  200.1 6.4 %convolution_convert_fusion = bf16[128,2048]{1,0:T(8,128)(2,1)S(1)} fusion(bf16[128,2880]{0,1:T(8,128)(2,1)S(1)} %fusion.16, bf16[2048,2880]{0,1:T(8,128)(2,1)} %all-gather.2.cloned.1.call-done), kind=kOutput, calls=%fused_computation.15 | convolution fusion | flops 1510211584 | bytes 13058048 | tf_op jit(solution)/shard_map/dot_general | solution.py:721
  206.9 3.6 %convolution_bitcast_fusion.1 = f32[256,4,64]{0,2,1:T(8,128)S(1)} fusion(bf16[128,4,8,64]{0,3,2,1:T(8,128)(2,1)S(1)} %bitcast.176, f32[4,256,128,8]{2,1,3,0:T(8,128)} %copy-done.4, f32[4,8,128]{2,1,0:T(8,128)S(1)} %copy-done.25, f32[4,8,128]{2,1,0:T(8,128)S(1)} %copy-done.19, pred[128,256]{0,1:T(8,128)(4,1)S(1)} %fusion.34), kind=kOutput, calls=%fused_computation.31 | convolution fusion | flops 140509184 | bytes 5046272 | tf_op jit(solution)/shard_map/ujko,kujm->oum/dot_general | solution.py:114
  210.5 3.4 %fusion = (f32[4,8,128]{2,1,0:T(8,128)S(1)}, f32[4,256,128,8]{2,1,3,0:T(8,128)}) fusion(f32[4,8,128]{2,1,0:T(8,128)S(1)} %copy-done.25, f32[4,8,128]{2,1,0:T(8,128)S(1)} %copy-done.19, f32[4,256,128,8]{2,1,3,0:T(8,128)S(1)} %copy-done.5, pred[128,256]{0,1:T(8,128)(4,1)S(1)} %fusion.34, bf16[128,4,8,64]{0,3,2,1:T(8,128)(2,1)S(1)} %bitcast.177, ...), kind=kOutput, calls=%fused_computation.2 | convolution fusion | flops 141815808 | bytes 9125888 | tf_op jit(solution)/shard_map/baqj,eaj->aqbe/dot_general | solution.py:96
  213.9 0.7 copy.80
  214.7 1.3 collective-permute-start.3
  216.2 5.0 %fusion.2 = bf16[4,8,128,256]{2,3,1,0:T(8,128)(2,1)S(1)} fusion(f32[4,256,128,8]{2,1,3,0:T(8,128)} %get-tuple-element.35, f32[4,8,128]{2,1,0:T(8,128)S(1)} %get-tuple-element.34, f32[4,8,128]{2,1,0:T(8,128)S(1)} %copy-done.25, f32[4,8,128]{2,1,0:T(8,128)S(1)} %copy-done.19, f32[4,256,128,8]{2,1,3,0:T(8,128)} %copy-done.4, pred[128,256]{0,1:T(8,128)(4,1)} %copy-done.14), kind=kLoop, calls=%fused_computation.4 | loop fusion | flops 8388608 | bytes 10567680 | tf_op jit(solution)/shard_map/convert_element_type | solution.py:100
  221.2 1.4 fusion.20
  223.2 1.3 fusion.18
  224.5 42.2 %psum.23 = f32[32]{0:T(128)} all-reduce(f32[32]{0:T(128)} %neg.11), channel_id=1, replica_groups=mesh['seq'=2,'dp'=16] {'seq','dp'}, use_global_device_ids=true, to_apply=%region_19.20 | all-reduce | flops 32 | bytes 256 | tf_op jit(solution)/shard_map/psum | solution.py:746
  266.8 0.9 slice.57
  267.7 0.9 slice.73
  268.7 1.0 copy.82
  269.9 1.3 collective-permute-start.2
  271.2 1.5 fusion.39
  272.7 3.4 %collective-permute-done.2 = bf16[128,256]{1,0:T(8,128)(2,1)S(1)} collective-permute-done((bf16[128,256]{1,0:T(8,128)(2,1)S(1)}, bf16[128,256]{1,0:T(8,128)(2,1)S(1)}, u32[]{:S(2)}, u32[]{:S(2)}) %collective-permute-start.2) | collective-permute-done | bytes 65568 | tf_op jit(solution)/shard_map/ppermute | solution.py:29
  276.1 0.6 fusion.38
  (130 shorter events, 6.5 us)
Async XLA Ops:
  7.2 182.1 %copy-start = (bf16[2880,128]{1,0:T(8,128)(2,1)S(1)}, bf16[2880,128]{1,0:T(8,128)(2,1)}, u32[]{:S(2)}) copy-start(bf16[2880,128]{1,0:T(8,128)(2,1)} %param.23) | copy-start | bytes 2211844
  7.2 106.6 %all-gather.2.cloned.1.call-start = ((), (), s32[]{:S(2)}) async-start(), calls=%async_computation | async-start | bytes 12533760 | tf_op jit(solution)/shard_map/all_gather | solution.py:657
  7.9 66.2 %collective-permute-start.1 = (bf16[128,256]{1,0:T(8,128)(2,1)}, bf16[128,256]{1,0:T(8,128)(2,1)S(1)}, u32[]{:S(2)}, u32[]{:S(2)}) collective-permute-start(bf16[128,256]{1,0:T(8,128)(2,1)} %bitcast.181), channel_id=1, source_target_pairs={{0,16},{1,17},{2,18},{3,19},{4,20},{5,21},{6,22},{7,23},{8,24},{9,... | collective-permute-start | bytes 196616 | tf_op jit(solution)/shard_map/ppermute | solution.py:29
  15.5 58.8 %collective-permute-start = (bf16[128,256]{1,0:T(8,128)(2,1)}, bf16[128,256]{1,0:T(8,128)(2,1)S(1)}, u32[]{:S(2)}, u32[]{:S(2)}) collective-permute-start(bf16[128,256]{1,0:T(8,128)(2,1)} %bitcast.182), channel_id=1, source_target_pairs={{0,16},{1,17},{2,18},{3,19},{4,20},{5,21},{6,22},{7,23},{8,24},{9,... | collective-permute-start | bytes 196616 | tf_op jit(solution)/shard_map/ppermute | solution.py:29
  63.6 0.6 copy-start.23
  65.3 4.8 %copy-start.35 = (pred[128,2,4]{0,2,1:T(4,128)(4,1)}, pred[128,2,4]{0,2,1:T(4,128)(4,1)S(1)}, u32[]{:S(2)}) copy-start(pred[128,2,4]{0,2,1:T(4,128)(4,1)S(1)} %fusion.43) | copy-start | bytes 3076
  66.8 143.7 %copy-start.14 = (pred[128,256]{0,1:T(8,128)(4,1)}, pred[128,256]{0,1:T(8,128)(4,1)S(1)}, u32[]{:S(2)}) copy-start(pred[128,256]{0,1:T(8,128)(4,1)S(1)} %fusion.34) | copy-start | bytes 98308
  71.1 5.3 %copy-start.11 = (bf16[1,128,256]{1,2,0:T(8,128)(2,1)}, bf16[1,128,256]{1,2,0:T(8,128)(2,1)S(1)}, u32[]{:S(2)}) copy-start(bf16[1,128,256]{1,2,0:T(8,128)(2,1)S(1)} %copy.62) | copy-start | bytes 196612
  72.0 4.4 %copy-start.26 = (bf16[1,128,256]{1,2,0:T(8,128)(2,1)}, bf16[1,128,256]{1,2,0:T(8,128)(2,1)S(1)}, u32[]{:S(2)}) copy-start(bf16[1,128,256]{1,2,0:T(8,128)(2,1)S(1)} %copy.65) | copy-start | bytes 196612
  72.8 3.5 %copy-start.30 = (f32[4,8]{1,0:T(4,128)}, f32[4,8]{1,0:T(4,128)S(1)}, u32[]{:S(2)}) copy-start(f32[4,8]{1,0:T(4,128)S(1)} %max.20) | copy-start | bytes 388
  74.3 2.2 copy-start.28
  74.4 2.0 copy-start.13
  75.2 2.0 copy-start.4
  75.2 3.3 %copy-start.16 = (f32[4,8,128]{2,1,0:T(8,128)}, f32[4,8,128]{2,1,0:T(8,128)S(1)}, u32[]{:S(2)}) copy-start(f32[4,8,128]{2,1,0:T(8,128)S(1)} %get-tuple-element.30) | copy-start | bytes 49156
  75.3 3.2 %copy-start.18 = (f32[4,8,128]{2,1,0:T(8,128)}, f32[4,8,128]{2,1,0:T(8,128)S(1)}, u32[]{:S(2)}) copy-start(f32[4,8,128]{2,1,0:T(8,128)S(1)} %broadcast_maximum_fusion) | copy-start | bytes 49156
  76.4 2.1 copy-start.20
  76.5 2.1 copy-start.24
  77.2 36.6 %copy-start.40 = (bf16[1,128,2880]{1,2,0:T(8,128)(2,1)S(1)}, bf16[1,128,2880]{1,2,0:T(8,128)(2,1)}, u32[]{:S(2)}) copy-start(bf16[1,128,2880]{1,2,0:T(8,128)(2,1)} %param.20) | copy-start | bytes 2211844
  113.8 8.5 %copy-start.33 = (f32[2880]{0:T(1024)S(1)}, f32[2880]{0:T(1024)}, u32[]{:S(2)}) copy-start(f32[2880]{0:T(1024)} %param.22) | copy-start | bytes 34564
  113.8 8.5 %copy-start.36 = (pred[128,2,4]{0,2,1:T(4,128)(4,1)S(1)}, pred[128,2,4]{0,2,1:T(4,128)(4,1)}, u32[]{:S(2)}) copy-start(pred[128,2,4]{0,2,1:T(4,128)(4,1)} %copy-done.35) | copy-start | bytes 3076
  113.8 9.1 %copy-start.15 = (f32[2,4,2880]{2,1,0:T(4,128)S(1)}, f32[2,4,2880]{2,1,0:T(4,128)}, u32[]{:S(2)}) copy-start(f32[2,4,2880]{2,1,0:T(4,128)} %fusion.23) | copy-start | bytes 276484
  121.4 0.9 copy-start.6
  121.4 5.4 %copy-start.1 = (bf16[180,2048]{1,0:T(8,128)(2,1)S(1)}, bf16[180,2048]{1,0:T(8,128)(2,1)}, u32[]{:S(2)}) copy-start(bf16[180,2048]{1,0:T(8,128)(2,1)} %gate_ref.1) | copy-start | bytes 2211844
  121.5 5.4 %copy-start.2 = (bf16[180,2048]{1,0:T(8,128)(2,1)S(1)}, bf16[180,2048]{1,0:T(8,128)(2,1)}, u32[]{:S(2)}) copy-start(bf16[180,2048]{1,0:T(8,128)(2,1)} %up_ref.1) | copy-start | bytes 2211844
  121.5 5.4 %copy-start.3 = (bf16[180,2048]{1,0:T(8,128)(2,1)S(1)}, bf16[180,2048]{1,0:T(8,128)(2,1)}, u32[]{:S(2)}) copy-start(bf16[180,2048]{1,0:T(8,128)(2,1)} %down_ref.1) | copy-start | bytes 2211844
  122.3 0.6 copy-start.37
  125.6 63.7 %copy-start.7 = (bf16[128,2880]{0,1:T(8,128)(2,1)S(1)}, bf16[128,2880]{0,1:T(8,128)(2,1)}, u32[]{:S(2)}) copy-start(bf16[128,2880]{0,1:T(8,128)(2,1)} %copy-done.6) | copy-start | bytes 2211844
  125.6 63.7 %copy-start.34 = (f32[2880]{0:T(1024)S(1)}, f32[2880]{0:T(1024)}, u32[]{:S(2)}) copy-start(f32[2880]{0:T(1024)} %param.22) | copy-start | bytes 34564
  125.6 63.7 %copy-start.38 = (f32[128]{0:T(128)S(1)}, f32[128]{0:T(128)}, u32[]{:S(2)}) copy-start(f32[128]{0:T(128)} %copy-done.37) | copy-start | bytes 1540
  125.6 64.6 %copy-start.32 = (s32[1,128,4]{1,2,0:T(4,128)S(1)}, s32[1,128,4]{1,2,0:T(4,128)}, u32[]{:S(2)}) copy-start(s32[1,128,4]{1,2,0:T(4,128)} %param.27) | copy-start | bytes 6148
  189.3 9.7 %copy-start.8 = (bf16[128,2880]{0,1:T(8,128)(2,1)S(1)}, bf16[128,2880]{0,1:T(8,128)(2,1)}, u32[]{:S(2)}) copy-start(bf16[128,2880]{0,1:T(8,128)(2,1)} %copy-done.6) | copy-start | bytes 2211844
  189.3 9.7 %copy-start.10 = (bf16[1,128,2880]{1,2,0:T(8,128)(2,1)S(1)}, bf16[1,128,2880]{1,2,0:T(8,128)(2,1)}, u32[]{:S(2)}) copy-start(bf16[1,128,2880]{1,2,0:T(8,128)(2,1)} %param.31) | copy-start | bytes 2211844
  189.3 9.7 %copy-start.39 = (f32[128]{0:T(128)S(1)}, f32[128]{0:T(128)}, u32[]{:S(2)}) copy-start(f32[128]{0:T(128)} %copy-done.37) | copy-start | bytes 1540
  200.1 6.5 %copy-start.9 = (bf16[128,2880]{0,1:T(8,128)(2,1)}, bf16[128,2880]{0,1:T(8,128)(2,1)S(1)}, u32[]{:S(2)}) copy-start(bf16[128,2880]{0,1:T(8,128)(2,1)S(1)} %fusion.16) | copy-start | bytes 2211844
  200.1 6.8 %copy-start.19 = (f32[4,8,128]{2,1,0:T(8,128)S(1)}, f32[4,8,128]{2,1,0:T(8,128)}, u32[]{:S(2)}) copy-start(f32[4,8,128]{2,1,0:T(8,128)} %copy-done.18) | copy-start | bytes 49156
  200.1 6.8 %copy-start.25 = (f32[4,8,128]{2,1,0:T(8,128)S(1)}, f32[4,8,128]{2,1,0:T(8,128)}, u32[]{:S(2)}) copy-start(f32[4,8,128]{2,1,0:T(8,128)} %copy-done.24) | copy-start | bytes 49156
  206.8 3.6 %copy-start.5 = (f32[4,256,128,8]{2,1,3,0:T(8,128)S(1)}, f32[4,256,128,8]{2,1,3,0:T(8,128)}, u32[]{:S(2)}) copy-start(f32[4,256,128,8]{2,1,3,0:T(8,128)} %copy-done.4) | copy-start | bytes 12582916
  206.9 3.6 %copy-start.27 = (bf16[1,128,256]{1,2,0:T(8,128)(2,1)S(1)}, bf16[1,128,256]{1,2,0:T(8,128)(2,1)}, u32[]{:S(2)}) copy-start(bf16[1,128,256]{1,2,0:T(8,128)(2,1)} %copy-done.26) | copy-start | bytes 196612
  206.9 3.6 %copy-start.29 = (bf16[128,256]{0,1:T(8,128)(2,1)S(1)}, bf16[128,256]{0,1:T(8,128)(2,1)}, u32[]{:S(2)}) copy-start(bf16[128,256]{0,1:T(8,128)(2,1)} %copy-done.28) | copy-start | bytes 196612
  210.5 3.4 %copy-start.22 = (f32[256,4,64]{0,2,1:T(8,128)}, f32[256,4,64]{0,2,1:T(8,128)S(1)}, u32[]{:S(2)}) copy-start(f32[256,4,64]{0,2,1:T(8,128)S(1)} %convolution_bitcast_fusion.1) | copy-start | bytes 786436
  210.5 5.4 %copy-start.17 = (f32[4,8,128]{2,1,0:T(8,128)S(1)}, f32[4,8,128]{2,1,0:T(8,128)}, u32[]{:S(2)}) copy-start(f32[4,8,128]{2,1,0:T(8,128)} %copy-done.16) | copy-start | bytes 49156
  210.5 5.4 %copy-start.21 = (f32[4,8,128]{2,1,0:T(8,128)S(1)}, f32[4,8,128]{2,1,0:T(8,128)}, u32[]{:S(2)}) copy-start(f32[4,8,128]{2,1,0:T(8,128)} %copy-done.20) | copy-start | bytes 49156
  210.5 5.4 %copy-start.31 = (f32[4,8]{1,0:T(4,128)S(1)}, f32[4,8]{1,0:T(4,128)}, u32[]{:S(2)}) copy-start(f32[4,8]{1,0:T(4,128)} %copy-done.30) | copy-start | bytes 388
  214.7 56.6 %collective-permute-start.3 = (bf16[128,256]{1,0:T(8,128)(2,1)}, bf16[128,256]{1,0:T(8,128)(2,1)}, u32[]{:S(2)}, u32[]{:S(2)}) collective-permute-start(bf16[128,256]{1,0:T(8,128)(2,1)} %copy.80), channel_id=1, source_target_pairs={{16,0},{17,1},{18,2},{19,3},{20,4},{21,5},{22,6},{23,7},{24,8},{25... | collective-permute-start | bytes 196616 | tf_op jit(solution)/shard_map/ppermute | solution.py:29
  216.2 7.1 %copy-start.12 = (bf16[1,128,256]{1,2,0:T(8,128)(2,1)S(1)}, bf16[1,128,256]{1,2,0:T(8,128)(2,1)}, u32[]{:S(2)}) copy-start(bf16[1,128,256]{1,2,0:T(8,128)(2,1)} %copy-done.11) | copy-start | bytes 196612
  222.6 47.1 %slice-start = ((f32[256,4,64]{0,2,1:T(8,128)}), f32[128,4,64]{0,2,1:T(8,128)S(1)}, s32[]{:S(2)}) async-start(f32[256,4,64]{0,2,1:T(8,128)} %fusion.20), calls=%async_computation.1 | async-start | bytes 262144 | tf_op jit(solution)/shard_map/slice | solution.py:737
  269.9 6.2 %collective-permute-start.2 = (bf16[128,256]{1,0:T(8,128)(2,1)S(1)}, bf16[128,256]{1,0:T(8,128)(2,1)S(1)}, u32[]{:S(2)}, u32[]{:S(2)}) collective-permute-start(bf16[128,256]{1,0:T(8,128)(2,1)S(1)} %copy.77), channel_id=1, source_target_pairs={{16,0},{17,1},{18,2},{19,3},{20,4},{21,5},{22,6},{23,7},{24,8},{25... | collective-permute-start | bytes 196616 | tf_op jit(solution)/shard_map/ppermute | solution.py:29
Sparse Core Ops, SparseCore 0:
  10.2 103.5 all-gather.1

commit v2 on v1

--- a/solution.py
+++ b/solution.py
@@ -341,6 +341,7 @@
 def expert_kernel(
     count,
     slots_ref,
+    facts_ref,
     gate_ref,
     up_ref,
     down_ref,
@@ -395,7 +396,7 @@
         device_id_type=MESH,
     )
     swap.start()
-    back[...] = jnp.zeros_like(back)
+    back[...] = jnp.broadcast_to(facts_ref[...], back.shape)
     swap.wait()
     mine = slots_ref[side]
     came = theirs[...]
@@ -555,7 +556,7 @@
     last.wait()
 
 
-def in_place_experts(slots, gate, up, down):
+def in_place_experts(slots, facts, gate, up, down):
     count, lanes = slots.shape[1], slots.shape[3]
     bits = count.bit_length() - 1
     rows = EW * CAP
@@ -568,7 +569,7 @@
     return pl.pallas_call(
         functools.partial(expert_kernel, count),
         out_shape=(result, result),
-        in_specs=[vmem] * 4,
+        in_specs=[vmem] * 5,
         out_specs=(vmem, vmem),
         scratch_shapes=[
             pltpu.VMEM((count, rows, lanes), jnp.float32),
@@ -594,7 +595,347 @@
             collective_id=1, has_side_effects=True, vmem_limit_bytes=40 * MIB
         ),
         name="expert_kernel",
-    )(slots, gate, up, down)
+    )(slots, facts, gate, up, down)
+
+
+def gather_kernel(
+    count,
+    weight_ref,
+    full_ref,
+    own_sem,
+    line_send,
+    line_recv,
+    pair_send,
+    pair_recv,
+    side_send,
+    side_recv,
+    core_send,
+    core_recv,
+):
+    line = count // 4
+    waves = line - 1
+    me = lax.axis_index("dp")
+    side = lax.axis_index("seq")
+    core, pair, spot = lax.rem(me, 2), lax.rem(lax.div(me, 2), 2), lax.div(me, 4)
+    rows = weight_ref.shape[0]
+    lone = rows * 3 // 128 * 16
+    shared = rows - 2 * lone
+    lone_start = pl.multiple_of(side * (lone + shared), 16)
+    plane_start = pl.multiple_of(side * lone, 16)
+    far_start = pl.multiple_of((1 - side) * (lone + shared), 16)
+    chunks = ((lone_start, lone), (lone, shared))
+
+    def index(spot, pair, core):
+        return (spot * 2 + pair) * 2 + core
+
+    def part(owner, start, size, own=False):
+        if own:
+            return weight_ref.at[pl.ds(start, size)]
+        return full_ref.at[owner, pl.ds(start, size)]
+
+    def remote(owner, own, start, size, send, recv, target):
+        return pltpu.make_async_remote_copy(
+            src_ref=part(owner, start, size, own),
+            dst_ref=part(owner, start, size),
+            send_sem=send,
+            recv_sem=recv,
+            device_id=target,
+            device_id_type=MESH,
+        )
+
+    def shard_spot(way, wave):
+        return spot - 1 - wave if way == 0 else spot + 1 + wave
+
+    def arrives(way, wave):
+        return spot - 1 - wave >= 0 if way == 0 else spot + 1 + wave < line
+
+    def leaves(way, wave):
+        if way == 0:
+            return (spot + 1 < line) & (spot - wave >= 0)
+        return (spot >= 1) & (spot + wave < line)
+
+    def line_copy(way, wave, chunk):
+        step = 1 if way == 0 else -1
+        owner = index(spot - step * wave, pair, core)
+        return remote(
+            owner,
+            wave == 0,
+            *chunks[chunk],
+            line_send.at[way, wave, chunk],
+            line_recv.at[way, wave, chunk],
+            {"dp": index(spot + step, pair, core)},
+        )
+
+    def slot(piece):
+        return 0 if piece is None else 1 + 2 * piece[1] + piece[0]
+
+    def owner_of(piece, other_pair):
+        at = spot if piece is None else shard_spot(*piece)
+        return index(at, 1 - pair if other_pair else pair, core)
+
+    def pair_copy(piece, chunk):
+        at = slot(piece)
+        return remote(
+            owner_of(piece, False),
+            piece is None,
+            *chunks[chunk],
+            pair_send.at[at, chunk],
+            pair_recv.at[at, chunk],
+            {"dp": index(spot, 1 - pair, core)},
+        )
+
+    def side_copy(piece, other_pair):
+        at = slot(piece)
+        return remote(
+            owner_of(piece, other_pair),
+            False,
+            lone_start,
+            lone,
+            side_send.at[other_pair, at],
+            side_recv.at[other_pair, at],
+            {"seq": 1 - side},
+        )
+
+    def core_copy(piece, other_pair, from_side):
+        at = slot(piece)
+        if piece is None and other_pair == 0:
+            start, size = 0, rows
+        elif from_side:
+            start, size = far_start, lone
+        else:
+            start, size = plane_start, lone + shared
+        return remote(
+            owner_of(piece, other_pair),
+            piece is None and other_pair == 0,
+            start,
+            size,
+            core_send.at[from_side, other_pair, at],
+            core_recv.at[from_side, other_pair, at],
+            {"dp": index(spot, pair, 1 - core)},
+        )
+
+    def held(piece, action):
+        if piece is None:
+            action()
+        else:
+            pl.when(arrives(*piece))(action)
+
+    barrier = pltpu.get_barrier_semaphore()
+
+    def greet(target):
+        pl.semaphore_signal(barrier, inc=1, device_id=target, device_id_type=MESH)
+
+    greet({"seq": 1 - side})
+    greet({"dp": index(spot, 1 - pair, core)})
+    greet({"dp": index(spot, pair, 1 - core)})
+    for way, step in ((0, 1), (1, -1)):
+
+        @pl.when(leaves(way, 0))
+        def _(step=step):
+            greet({"dp": index(spot + step, pair, core)})
+
+    neighbours = leaves(0, 0).astype(jnp.int32) + leaves(1, 0).astype(jnp.int32)
+    pl.semaphore_wait(barrier, 3 + neighbours)
+
+    keep = pltpu.make_async_copy(weight_ref, full_ref.at[me], own_sem)
+    for chunk in (0, 1):
+        for way in (0, 1):
+
+            @pl.when(leaves(way, 0))
+            def _(way=way, chunk=chunk):
+                line_copy(way, 0, chunk).start()
+
+        pair_copy(None, chunk).start()
+    core_copy(None, 0, 0).start()
+    keep.start()
+
+    def line_step(wave):
+        for chunk in (0, 1):
+            for way in (0, 1):
+
+                @pl.when(arrives(way, wave))
+                def _(way=way, chunk=chunk):
+                    piece = (way, wave)
+                    line_copy(way, wave, chunk).wait_recv()
+                    if wave + 1 < waves:
+
+                        @pl.when(leaves(way, wave + 1))
+                        def _():
+                            line_copy(way, wave + 1, chunk).start()
+
+                    pair_copy(piece, chunk).start()
+                    if chunk == 0:
+                        side_copy(piece, 0).start()
+                    else:
+                        core_copy(piece, 0, 0).start()
+
+    def pair_step(pieces):
+        for chunk in (0, 1):
+            for piece in pieces:
+
+                def arrive(piece=piece, chunk=chunk):
+                    pair_copy(piece, chunk).wait_recv()
+                    if chunk == 0:
+                        side_copy(piece, 1).start()
+                    else:
+                        core_copy(piece, 1, 0).start()
+
+                held(piece, arrive)
+
+    def side_step(pieces, other_pair):
+        for piece in pieces:
+
+            def arrive(piece=piece):
+                side_copy(piece, other_pair).wait_recv()
+                core_copy(piece, other_pair, 1).start()
+
+            held(piece, arrive)
+
+    waved = [[(0, wave), (1, wave)] for wave in range(waves)]
+    ordered = [[None]] + waved
+    for wave in range(waves):
+        line_step(wave)
+        pair_step(ordered[wave])
+        if wave:
+            side_step(waved[wave - 1], 0)
+            side_step(ordered[wave - 1], 1)
+    pair_step(ordered[waves])
+    side_step(waved[waves - 1], 0)
+    side_step(ordered[waves - 1], 1)
+    side_step(ordered[waves], 1)
+
+    keep.wait()
+    for piece in [None] + sum(waved, []):
+
+        def finish(piece=piece):
+            for chunk in (0, 1):
+                pair_copy(piece, chunk).wait_send()
+            for other_pair in (0, 1):
+                core_copy(piece, other_pair, 0).wait()
+                if piece is not None or other_pair:
+                    side_copy(piece, other_pair).wait_send()
+                    core_copy(piece, other_pair, 1).wait()
+
+        held(piece, finish)
+    for wave in range(waves):
+        for way in (0, 1):
+
+            @pl.when(leaves(way, wave))
+            def _(way=way, wave=wave):
+                for chunk in (0, 1):
+                    line_copy(way, wave, chunk).wait_send()
+
+
+def gathered(weight, count):
+    waves = count // 4 - 1
+    slots = 1 + 2 * waves
+    dma = pltpu.SemaphoreType.DMA
+    full = pl.pallas_call(
+        functools.partial(gather_kernel, count),
+        out_shape=jax.ShapeDtypeStruct((count,) + weight.shape, weight.dtype),
+        in_specs=[pl.BlockSpec(memory_space=pl.ANY)],
+        out_specs=pl.BlockSpec(memory_space=pl.ANY),
+        scratch_shapes=[
+            dma,
+            dma((2, waves, 2)),
+            dma((2, waves, 2)),
+            dma((slots, 2)),
+            dma((slots, 2)),
+            dma((2, slots)),
+            dma((2, slots)),
+            dma((2, 2, slots)),
+            dma((2, 2, slots)),
+        ],
+        compiler_params=pltpu.CompilerParams(collective_id=2, has_side_effects=True),
+        name="gather_kernel",
+    )(weight)
+    return full.reshape(count * weight.shape[0], weight.shape[1])
+
+
+def tail_kernel(
+    count, sinks_ref, halo_ref, sums_ref, came_ref, parts, half, far_half, dp_send, dp_recv, seq_send, seq_recv
+):
+    me = lax.axis_index("dp")
+    far = 1 - lax.axis_index("seq")
+    barrier = pltpu.get_barrier_semaphore()
+    pl.semaphore_signal(barrier, inc=1, device_id={"seq": far}, device_id_type=MESH)
+
+    def greet(step, carry):
+        pl.semaphore_signal(
+            barrier, inc=1, device_id={"dp": lax.rem(me + step, count)}, device_id_type=MESH
+        )
+        return carry
+
+    lax.fori_loop(1, count, greet, 0)
+    pl.semaphore_wait(barrier, count)
+
+    def across(source, target, at):
+        return pltpu.make_async_remote_copy(
+            src_ref=source,
+            dst_ref=target,
+            send_sem=seq_send.at[at],
+            recv_sem=seq_recv.at[at],
+            device_id={"seq": far},
+            device_id_type=MESH,
+        )
+
+    def part_copy(step):
+        return pltpu.make_async_remote_copy(
+            src_ref=sinks_ref,
+            dst_ref=parts.at[me],
+            send_sem=dp_send.at[step],
+            recv_sem=dp_recv.at[step],
+            device_id={"dp": lax.rem(me + step, count)},
+            device_id_type=MESH,
+        )
+
+    def start_part(step, carry):
+        part_copy(step).start()
+        return carry
+
+    def wait_part(step, carry):
+        part_copy(step).wait()
+        return carry
+
+    lax.fori_loop(1, count, start_part, 0)
+    halo = across(halo_ref, came_ref, 0)
+    halo.start()
+    parts[me] = sinks_ref[...]
+    lax.fori_loop(1, count, wait_part, 0)
+    half[...] = jnp.sum(parts[...], axis=0)
+    swap = across(half, far_half, 1)
+    swap.start()
+    swap.wait()
+    sums_ref[...] = half[...] + far_half[...]
+    halo.wait()
+
+
+def tail_exchange(sinks, halo, count):
+    vmem = pl.BlockSpec(memory_space=pltpu.VMEM)
+    dma = pltpu.SemaphoreType.DMA
+    tile = (8, 128)
+    row = jnp.zeros(tile, jnp.float32).at[0, : sinks.shape[0]].set(sinks)
+    sums, came = pl.pallas_call(
+        functools.partial(tail_kernel, count),
+        out_shape=(
+            jax.ShapeDtypeStruct(tile, jnp.float32),
+            jax.ShapeDtypeStruct(halo.shape, halo.dtype),
+        ),
+        in_specs=[vmem] * 2,
+        out_specs=(vmem, vmem),
+        scratch_shapes=[
+            pltpu.VMEM((count,) + tile, jnp.float32),
+            pltpu.VMEM(tile, jnp.float32),
+            pltpu.VMEM(tile, jnp.float32),
+            dma((count,)),
+            dma((count,)),
+            dma((2,)),
+            dma((2,)),
+        ],
+        compiler_params=pltpu.CompilerParams(collective_id=3, has_side_effects=True),
+        name="tail_kernel",
+    )(row, halo)
+    return sums[0, : sinks.shape[0]], came
 
 
 def shards(
@@ -632,15 +973,6 @@
     mask_wide = response_mask[0].astype(jnp.float32)
     local_count = jnp.sum(mask_wide)
     first_device = (seq_index == 0).astype(jnp.float32)
-    group_totals, token_total = lax.psum((group_terms * first_device, local_count), ("seq", "dp"))
-    group_sizes = group_totals[:, 0]
-    group_means = group_totals[:, 1] / group_sizes
-    group_spread = group_totals[:, 2] / group_sizes - group_means * group_means
-    own_mean = jnp.sum(group_hot * group_means)
-    own_spread = jnp.sum(group_hot * group_spread)
-    advantage = (reward - own_mean) / jnp.sqrt(jnp.maximum(own_spread, 1.0))
-    token_scale = -advantage * all_tokens / token_total
-    loss_weight = token_scale * mask_wide
     halo_keys, halo_values = passed_along((own_keys, own_values), "seq", 1)
     key_tile_block = jnp.concatenate([halo_keys, own_keys], axis=0)
     value_tile_block = jnp.concatenate([halo_values, own_values], axis=0)
@@ -654,7 +986,7 @@
     probs, sink_probs = head_scores(query_rows, key_tile_block, head_sink_logits, allowed)
     reduced_probabilities = probs.astype(jnp.bfloat16)
     attended = head_mix(reduced_probabilities, value_tile_block)
-    out_full = lax.all_gather(out_weight, "dp", axis=0, tiled=True)
+    out_full = gathered(out_weight, dp_count)
     projected = jnp.dot(attended, out_full, preferred_element_type=jnp.float32)
     mid_rows = lax.optimization_barrier(
         (residual[0].astype(jnp.float32) + projected).astype(jnp.bfloat16)
@@ -680,7 +1012,6 @@
     slot_rows = jnp.einsum(
         "tec,td->ecd", slot_low, normed, preferred_element_type=jnp.float32
     )
-    weight_slots = jnp.einsum("tec,t->ec", slot_wide, loss_weight, precision=HIGHEST)
     share_slots = jnp.einsum("tec,te->ec", slot_wide, expert_share, precision=HIGHEST)
     upstream_slots = jnp.einsum(
         "tec,td->ecd", slot_low, upstream[0], preferred_element_type=jnp.float32
@@ -689,8 +1020,24 @@
     lanes = -(-depth // 128) * 128
     slots = jnp.concatenate([slot_rows, upstream_slots], axis=1)
     slots = slots.reshape(EW, 2 * CAP, dp_count, depth).transpose(0, 2, 1, 3)
+    facts = jnp.concatenate([(group_terms * first_device).reshape(-1), local_count[None]])
+    lanes = max(lanes, -(-(depth + facts.shape[0]) // 128) * 128)
     slots = jnp.pad(slots, ((0, 0), (0, 0), (0, 0), (0, lanes - depth)))
-    own_part, other_part = in_place_experts(slots, expert_gate, expert_up, expert_down)
+    facts = jnp.pad(facts, (depth, lanes - depth - facts.shape[0]))
+    facts = jnp.broadcast_to(facts, (EW * CAP, lanes))
+    own_part, other_part = in_place_experts(slots, facts, expert_gate, expert_up, expert_down)
+    totals = jnp.sum(own_part[:dp_count, 0] + other_part[:dp_count, 0], axis=0)[depth:]
+    group_totals = totals[: group_terms.size].reshape(group_terms.shape)
+    token_total = totals[group_terms.size]
+    group_sizes = group_totals[:, 0]
+    group_means = group_totals[:, 1] / group_sizes
+    group_spread = group_totals[:, 2] / group_sizes - group_means * group_means
+    own_mean = jnp.sum(group_hot * group_means)
+    own_spread = jnp.sum(group_hot * group_spread)
+    advantage = (reward - own_mean) / jnp.sqrt(jnp.maximum(own_spread, 1.0))
+    token_scale = -advantage * all_tokens / token_total
+    loss_weight = token_scale * mask_wide
+    weight_slots = jnp.einsum("tec,t->ec", slot_wide, loss_weight, precision=HIGHEST)
     both_parts = jnp.where(
         seq_index == 0, jnp.stack([own_part, other_part]), jnp.stack([other_part, own_part])
     )
@@ -730,10 +1077,10 @@
         value_tile_block,
         grad_attended,
     )
-    next_keys, next_values = (
-        passed_along(key_gradient[:WINDOW].astype(jnp.bfloat16), "seq", -1).astype(jnp.float32),
-        passed_along(value_gradient[:WINDOW].astype(jnp.bfloat16), "seq", -1).astype(jnp.float32),
-    )
+    halo = jnp.concatenate([key_gradient[:WINDOW], value_gradient[:WINDOW]], axis=0)
+    grad_sinks, came = tail_exchange(sink_gradient, halo.astype(jnp.bfloat16), dp_count)
+    came = jnp.where(seq_index + 1 < seq_count, came.astype(jnp.float32), 0.0)
+    next_keys, next_values = came[:WINDOW], came[WINDOW:]
     own_key_grad = key_gradient[WINDOW:]
     own_value_grad = value_gradient[WINDOW:]
     split_at = tokens_here - WINDOW
@@ -743,7 +1090,6 @@
     grad_value_rows = jnp.concatenate(
         [own_value_grad[:split_at], own_value_grad + next_values], axis=0
     ).astype(jnp.bfloat16)
-    grad_sinks = lax.psum(sink_gradient, ("seq", "dp"))
     return (
         query_gradient[None],
         grad_key_rows[None],
@@ -755,7 +1101,7 @@
 
 def solution(mesh):
     seq_count, dp_count = mesh.shape["seq"], mesh.shape["dp"]
-    in_place = seq_count == EW and dp_count & (dp_count - 1) == 0
+    in_place = seq_count == EW and dp_count >= 8 and dp_count & (dp_count - 1) == 0
     return jax.shard_map(
         shards if in_place else general_shards,
         mesh=mesh,

time: 285 us -> 206 us (0.72)
  blocking collectives: 86.3 us -> 0 us
  Pallas kernels: 62.2 us -> 131 us
  waiting for transfers between devices: 39.3 us -> 0.01 us
  between operations: 18.1 us -> 4.79 us
  other arithmetic: 18.1 us -> 12.8 us
    psum x2 -> x0, blocking collectives: 86.3 us -> none  [the longest x1 44.1 us: shards(): lax.psum((group_terms * first_device, local_count), ('seq', 'dp'))]
    pallas_call x0 -> x2, Pallas kernels: none -> 67.1 us  [the longest x1 55.6 us: gathered(): pl.pallas_call(functools.partial(gather_kernel, count), out_shape=jax.Sha...]
    all_gather x1 -> x0, waiting for transfers between devices: 35.3 us -> none  [shards(): out_full = lax.all_gather(out_weight, 'dp', axis=0, tiled=True)]
    unnamed x87 -> x84, local copies, waits for them, and re-layouts: 6.27 us -> 9.93 us
    ppermute x4 -> x2, waiting for transfers between devices: 3.37 us -> 0.01 us  [passed_along(): lax.ppermute(value, axis, [(source, source + steps) for source in range(i...]
    convert_element_type x1, other arithmetic: 5 us -> 1.67 us  [head_grads(): (probs * (probability_gradient - spread[..., None])).astype(jnp.bfloat16)]
    ppermute x4 -> x2, starting transfers between devices: 8.7 us -> 6.27 us  [passed_along(): lax.ppermute(value, axis, [(source, source + steps) for source in range(i...]
  transfers between devices with their start and end apart: 5 -> 2, of which waited for: 2 -> 0; matrix products, arithmetic and copies ran while one was open for 10% -> 7% of each run, Pallas kernels for 0% -> 27%
where the time goes in v2:
time: 206 us; the launch traced here: 205 us
  Pallas kernels  131 us (64%)
  matrix products  35.4 us (17%)
  local copies, waits for them, and re-layouts  15.3 us (7%)
  other arithmetic  12.8 us (6%)
  starting transfers between devices  6.27 us (3%)
  between operations  4.79 us (2%)
    pallas_call x1, Pallas kernels, in_place_experts(): pl.pallas_call(functools.partial(expert_kernel, count), out_shape=(result...  63.6 us
    pallas_call x1, Pallas kernels, gathered(): pl.pallas_call(functools.partial(gather_kernel, count), out_shape=jax.Sha...  55.6 us
    pallas_call x1, Pallas kernels, tail_exchange(): pl.pallas_call(functools.partial(tail_kernel, count), out_shape=(jax.Shap...  11.5 us
    unnamed x84, local copies, waits for them, and re-layouts  9.93 us
    dot_general x1, matrix products, shards(): lax.dot_general(grad_residual, out_full, CONTRACT_LAST, preferred_element...  8.75 us
    dot_general x1, matrix products, shards(): projected = jnp.dot(attended, out_full, preferred_element_type=jnp.float32)  8.34 us
    ppermute x2, starting transfers between devices, passed_along(): lax.ppermute(value, axis, [(source, source + steps) for source in range(i...  6.27 us
  transfers between devices with their start and end apart: 2, of which 0 were waited for; matrix products, arithmetic and copies ran while one was open for 7% of the time, Pallas kernels for 27%

profile of v2, /device:TPU:0, one launch (start us, length us, event | category | flops | bytes accessed | tf_op | source)
XLA Modules:
  0.0 205.3 jit_solution(3079295835677371035)
XLA Ops:
  0.6 5.0 %collective-permute-start.1 = (bf16[128,256]{1,0:T(8,128)(2,1)}, bf16[128,256]{1,0:T(8,128)(2,1)S(1)}, u32[]{:S(2)}, u32[]{:S(2)}) collective-permute-start(bf16[128,256]{1,0:T(8,128)(2,1)} %bitcast.177), channel_id=1, source_target_pairs={{0,16},{1,17},{2,18},{3,19},{4,20},{5,21},{6,22},{7,23},{8,24},{9,... | collective-permute-start | bytes 196616 | tf_op jit(solution)/shard_map/ppermute | solution.py:29
  5.6 1.3 collective-permute-start
  7.0 1.0 copy.64
  7.9 1.0 copy.67
  10.2 1.3 convert_reduce_fusion
  11.8 0.7 max.20
  12.5 0.8 iota_compare_fusion
  13.3 0.6 copy-done.24
  14.3 1.3 copy.65
  15.6 2.5 %copy.71.weight_ref = bf16[128,2880]{1,0:T(8,128)(2,1)} copy(bf16[128,2880]{0,1:T(8,128)(2,1)} %param.23) | data formatting | bytes 1474560 | tf_op args[5]
  18.1 55.6 %gather_kernel.1 = bf16[16,128,2880]{2,1,0:T(8,128)(2,1)} custom-call(bf16[128,2880]{1,0:T(8,128)(2,1)} %copy.71.weight_ref), custom_call_target="tpu_custom_call" | custom-call | tf_op jit(solution)/shard_map/gather_kernel/pallas_call | solution.py:833
  73.7 0.9 fusion.23
  74.8 1.3 select_maximum_fusion
  76.2 0.8 fusion.4
  77.1 1.9 copy-done.4
  79.0 1.1 fusion.7
  80.3 3.5 %convolution_convert_fusion.1 = bf16[4,64,8,128]{3,1,2,0:T(8,128)(2,1)S(1)} fusion(bf16[128,4,64]{0,2,1:T(8,128)(2,1)S(1)} %bitcast.178, bf16[128,4,64]{0,2,1:T(8,128)(2,1)S(1)} %bitcast.180, f32[4,256,128,8]{2,1,3,0:T(8,128)} %copy-done.4, f32[4,8,128]{2,1,0:T(8,128)S(1)} %fusion.44, f32[4,8,128]{2,1,0:T(8,128)S(1)} %broadcast_maximum_fusion, ...), kind=kOutput, calls=%fused_computation.30 | convolution fusion | flops 141033472 | bytes 4915200 | tf_op jit(solution)/shard_map/amlh,hai->lami/dot_general | solution.py:71
  83.9 8.3 %fusion.5 = bf16[128,2880]{0,1:T(8,128)(2,1)S(1)} fusion(bf16[128,2048]{0,1:T(8,128)(2,1)S(1)} %bitcast.173, bf16[2048,2880]{1,0:T(8,128)(2,1)} %bitcast.158, bf16[1,128,2880]{1,2,0:T(8,128)(2,1)S(1)} %copy-done.13), kind=kOutput, calls=%fused_computation.12 | convolution fusion | flops 1511055360 | bytes 13795328 | tf_op jit(solution)/shard_map/dot_general | solution.py:990
  92.3 0.4 fusion.17
  92.7 0.4 copy-done.6
  93.1 0.6 fusion.25
  93.8 0.3 reshape.286
  94.4 63.6 %expert_kernel.1 = (f32[17,8,256]{2,1,0:T(8,128)S(1)}, f32[17,8,256]{2,1,0:T(8,128)S(1)}) custom-call(f32[2,16,8,256]{3,2,1,0:T(8,128)S(1)} %pad.13.slots_ref, f32[8,256]{1,0:T(8,128)S(1)} %broadcast_in_dim.112.facts_ref, bf16[180,2048]{1,0:T(8,128)(2,1)S(1)} %copy-done.1, bf16[180,2048]{1,0:T(8,128)(2,1)S(1)} %copy-done.2, bf16[180,2048]{1,0:T(8,128)(2,1)S(1)} %copy-done.3), custom_call_target="tpu_custom_call" | custom-call | tf_op jit(solution)/shard_map/expert_kernel/pallas_call | solution.py:569
  158.0 0.7 slice.91
  158.8 0.2 fusion.47
  159.0 0.6 select_reduce_fusion.4
  161.6 0.7 fusion.51
  162.3 0.8 fusion.49
  163.3 2.1 %fusion.27 = f32[128,128]{0,1:T(8,128)S(1)} fusion(bf16[2880,128]{1,0:T(8,128)(2,1)S(1)} %copy-done, bf16[128,2880]{0,1:T(8,128)(2,1)} %copy-done.6, f32[2880]{0:T(1024)} %param.24, f32[128]{0:T(128)} %copy-done.37), kind=kOutput, calls=%fused_computation.50 | convolution fusion | flops 95846400 | bytes 1552128 | tf_op jit(solution)/shard_map/dot_general | solution.py:998
  166.0 0.7 select_reduce_fusion.3
  166.8 0.2 select_reduce_fusion
  167.1 1.4 convolution_bitcast_fusion
  168.6 1.7 fusion.12
  170.3 0.5 fusion.16
  170.8 8.7 %convolution_convert_fusion = bf16[128,2048]{1,0:T(8,128)(2,1)S(1)} fusion(bf16[128,2880]{0,1:T(8,128)(2,1)S(1)} %fusion.16, bf16[2048,2880]{1,0:T(8,128)(2,1)} %bitcast.159), kind=kOutput, calls=%fused_computation.15 | convolution fusion | flops 1510211584 | bytes 13058048 | tf_op jit(solution)/shard_map/dot_general | solution.py:1068
  179.6 0.3 copy.77
  179.9 3.6 %convolution_bitcast_fusion.1 = f32[256,4,64]{0,2,1:T(8,128)S(1)} fusion(bf16[128,4,8,64]{0,3,2,1:T(8,128)(2,1)S(1)} %bitcast.169, f32[4,256,128,8]{2,1,3,0:T(8,128)} %copy-done.4, f32[4,8,128]{2,1,0:T(8,128)S(1)} %copy-done.26, f32[4,8,128]{2,1,0:T(8,128)S(1)} %copy-done.21, pred[128,256]{0,1:T(8,128)(4,1)S(1)} %copy-done.17), kind=kOutput, calls=%fused_computation.31 | convolution fusion | flops 140509184 | bytes 5046272 | tf_op jit(solution)/shard_map/ujko,kujm->oum/dot_general | solution.py:114
  183.6 1.5 fusion
  185.2 1.7 fusion.2
  186.9 0.7 fusion.20
  187.7 0.5 fusion.18
  188.4 1.0 copy.85
  189.5 0.6 scatter.4.sinks_ref
  190.3 0.6 pad_maximum_fusion.1.halo_ref
  191.0 11.5 %tail_kernel.1 = (f32[8,128]{1,0:T(8,128)}, bf16[256,256]{1,0:T(8,128)(2,1)}) custom-call(f32[8,128]{1,0:T(8,128)} %scatter.4.sinks_ref, bf16[256,256]{1,0:T(8,128)(2,1)} %pad_maximum_fusion.1.halo_ref), custom_call_target="tpu_custom_call" | custom-call | tf_op jit(solution)/shard_map/tail_kernel/pallas_call | solution.py:918
  202.5 1.2 slice_bitcast_fusion.1
  203.7 0.9 convert_select_fusion
  204.6 0.7 fusion.41
  (131 shorter events, 3.4 us)
Async XLA Ops:
  0.6 162.7 %copy-start = (bf16[2880,128]{1,0:T(8,128)(2,1)S(1)}, bf16[2880,128]{1,0:T(8,128)(2,1)}, u32[]{:S(2)}) copy-start(bf16[2880,128]{1,0:T(8,128)(2,1)} %param.25) | copy-start | bytes 2211844
  0.6 79.5 %collective-permute-start.1 = (bf16[128,256]{1,0:T(8,128)(2,1)}, bf16[128,256]{1,0:T(8,128)(2,1)S(1)}, u32[]{:S(2)}, u32[]{:S(2)}) collective-permute-start(bf16[128,256]{1,0:T(8,128)(2,1)} %bitcast.177), channel_id=1, source_target_pairs={{0,16},{1,17},{2,18},{3,19},{4,20},{5,21},{6,22},{7,23},{8,24},{9,... | collective-permute-start | bytes 196616 | tf_op jit(solution)/shard_map/ppermute | solution.py:29
  5.6 70.5 %collective-permute-start = (bf16[128,256]{1,0:T(8,128)(2,1)}, bf16[128,256]{1,0:T(8,128)(2,1)S(1)}, u32[]{:S(2)}, u32[]{:S(2)}) collective-permute-start(bf16[128,256]{1,0:T(8,128)(2,1)} %bitcast.176), channel_id=1, source_target_pairs={{0,16},{1,17},{2,18},{3,19},{4,20},{5,21},{6,22},{7,23},{8,24},{9,... | collective-permute-start | bytes 196616 | tf_op jit(solution)/shard_map/ppermute | solution.py:29
  8.9 71.4 %copy-start.27 = (bf16[1,128,256]{1,2,0:T(8,128)(2,1)}, bf16[1,128,256]{1,2,0:T(8,128)(2,1)S(1)}, u32[]{:S(2)}) copy-start(bf16[1,128,256]{1,2,0:T(8,128)(2,1)S(1)} %copy.67) | copy-start | bytes 196612
  13.3 0.6 copy-start.24
  14.3 78.5 %copy-start.34 = (pred[128,2,4]{0,2,1:T(4,128)(4,1)}, pred[128,2,4]{0,2,1:T(4,128)(4,1)S(1)}, u32[]{:S(2)}) copy-start(pred[128,2,4]{0,2,1:T(4,128)(4,1)S(1)} %fusion.45) | copy-start | bytes 3076
  15.6 60.6 %copy-start.8 = (bf16[1,128,2048]{1,2,0:T(8,128)(2,1)}, bf16[1,128,2048]{1,2,0:T(8,128)(2,1)S(1)}, u32[]{:S(2)}) copy-start(bf16[1,128,2048]{1,2,0:T(8,128)(2,1)S(1)} %copy.65) | copy-start | bytes 1572868
  18.1 55.6 %copy-start.10 = (bf16[1,128,2880]{1,2,0:T(8,128)(2,1)S(1)}, bf16[1,128,2880]{1,2,0:T(8,128)(2,1)}, u32[]{:S(2)}) copy-start(bf16[1,128,2880]{1,2,0:T(8,128)(2,1)} %param.33) | copy-start | bytes 2211844
  74.8 5.5 %copy-start.16 = (pred[128,256]{0,1:T(8,128)(4,1)}, pred[128,256]{0,1:T(8,128)(4,1)S(1)}, u32[]{:S(2)}) copy-start(pred[128,256]{0,1:T(8,128)(4,1)S(1)} %fusion.36) | copy-start | bytes 98308
  76.2 3.8 %copy-start.14 = (bf16[128,256]{0,1:T(8,128)(2,1)}, bf16[128,256]{0,1:T(8,128)(2,1)S(1)}, u32[]{:S(2)}) copy-start(bf16[128,256]{0,1:T(8,128)(2,1)S(1)} %copy.63) | copy-start | bytes 196612
  77.0 2.0 copy-start.4
  77.1 6.8 %copy-start.20 = (f32[4,8,128]{2,1,0:T(8,128)}, f32[4,8,128]{2,1,0:T(8,128)S(1)}, u32[]{:S(2)}) copy-start(f32[4,8,128]{2,1,0:T(8,128)S(1)} %broadcast_maximum_fusion) | copy-start | bytes 49156
  80.0 3.8 %copy-start.22 = (f32[4,8,128]{2,1,0:T(8,128)}, f32[4,8,128]{2,1,0:T(8,128)S(1)}, u32[]{:S(2)}) copy-start(f32[4,8,128]{2,1,0:T(8,128)S(1)} %fusion.7) | copy-start | bytes 49156
  80.1 3.7 %copy-start.25 = (f32[4,8,128]{2,1,0:T(8,128)}, f32[4,8,128]{2,1,0:T(8,128)S(1)}, u32[]{:S(2)}) copy-start(f32[4,8,128]{2,1,0:T(8,128)S(1)} %fusion.44) | copy-start | bytes 49156
  80.3 3.6 %copy-start.29 = (bf16[128,256]{0,1:T(8,128)(2,1)}, bf16[128,256]{0,1:T(8,128)(2,1)S(1)}, u32[]{:S(2)}) copy-start(bf16[128,256]{0,1:T(8,128)(2,1)S(1)} %copy.66) | copy-start | bytes 196612
  80.3 3.6 %copy-start.13 = (bf16[1,128,2880]{1,2,0:T(8,128)(2,1)S(1)}, bf16[1,128,2880]{1,2,0:T(8,128)(2,1)}, u32[]{:S(2)}) copy-start(bf16[1,128,2880]{1,2,0:T(8,128)(2,1)} %param.22) | copy-start | bytes 2211844
  83.9 9.2 %copy-start.32 = (f32[2880]{0:T(1024)S(1)}, f32[2880]{0:T(1024)}, u32[]{:S(2)}) copy-start(f32[2880]{0:T(1024)} %param.24) | copy-start | bytes 34564
  83.9 9.8 %copy-start.19 = (f32[2,4,2880]{2,1,0:T(4,128)S(1)}, f32[2,4,2880]{2,1,0:T(4,128)}, u32[]{:S(2)}) copy-start(f32[2,4,2880]{2,1,0:T(4,128)} %fusion.23) | copy-start | bytes 276484
  83.9 10.4 %copy-start.36 = (f32[256]{0:T(256)S(1)}, f32[256]{0:T(256)}, u32[]{:S(2)}) copy-start(f32[256]{0:T(256)} %select_maximum_fusion) | copy-start | bytes 3076
  92.3 0.9 copy-start.6
  92.3 2.1 %copy-start.1 = (bf16[180,2048]{1,0:T(8,128)(2,1)S(1)}, bf16[180,2048]{1,0:T(8,128)(2,1)}, u32[]{:S(2)}) copy-start(bf16[180,2048]{1,0:T(8,128)(2,1)} %gate_ref.1) | copy-start | bytes 2211844
  92.3 2.1 %copy-start.2 = (bf16[180,2048]{1,0:T(8,128)(2,1)S(1)}, bf16[180,2048]{1,0:T(8,128)(2,1)}, u32[]{:S(2)}) copy-start(bf16[180,2048]{1,0:T(8,128)(2,1)} %up_ref.1) | copy-start | bytes 2211844
  92.3 2.1 %copy-start.3 = (bf16[180,2048]{1,0:T(8,128)(2,1)S(1)}, bf16[180,2048]{1,0:T(8,128)(2,1)}, u32[]{:S(2)}) copy-start(bf16[180,2048]{1,0:T(8,128)(2,1)} %down_ref.1) | copy-start | bytes 2211844
  93.1 1.2 copy-start.37
  93.1 72.3 %copy-start.31 = (s32[1,128,4]{1,2,0:T(4,128)S(1)}, s32[1,128,4]{1,2,0:T(4,128)}, u32[]{:S(2)}) copy-start(s32[1,128,4]{1,2,0:T(4,128)} %param.29) | copy-start | bytes 6148
  94.1 71.7 %copy-start.35 = (pred[128,2,4]{0,2,1:T(4,128)(4,1)S(1)}, pred[128,2,4]{0,2,1:T(4,128)(4,1)}, u32[]{:S(2)}) copy-start(pred[128,2,4]{0,2,1:T(4,128)(4,1)} %copy-done.34) | copy-start | bytes 3076
  94.3 74.3 %copy-start.33 = (f32[2880]{0:T(1024)S(1)}, f32[2880]{0:T(1024)}, u32[]{:S(2)}) copy-start(f32[2880]{0:T(1024)} %param.24) | copy-start | bytes 34564
  94.4 74.2 %copy-start.38 = (f32[128]{0:T(128)S(1)}, f32[128]{0:T(128)}, u32[]{:S(2)}) copy-start(f32[128]{0:T(128)} %copy-done.37) | copy-start | bytes 1540
  163.3 7.0 %copy-start.7 = (bf16[128,2880]{0,1:T(8,128)(2,1)S(1)}, bf16[128,2880]{0,1:T(8,128)(2,1)}, u32[]{:S(2)}) copy-start(bf16[128,2880]{0,1:T(8,128)(2,1)} %copy-done.6) | copy-start | bytes 2211844
  163.3 7.0 %copy-start.11 = (bf16[1,128,2880]{1,2,0:T(8,128)(2,1)S(1)}, bf16[1,128,2880]{1,2,0:T(8,128)(2,1)}, u32[]{:S(2)}) copy-start(bf16[1,128,2880]{1,2,0:T(8,128)(2,1)} %param.33) | copy-start | bytes 2211844
  170.8 8.8 %copy-start.12 = (bf16[128,2880]{0,1:T(8,128)(2,1)}, bf16[128,2880]{0,1:T(8,128)(2,1)S(1)}, u32[]{:S(2)}) copy-start(bf16[128,2880]{0,1:T(8,128)(2,1)S(1)} %fusion.16) | copy-start | bytes 2211844
  170.8 9.1 %copy-start.17 = (pred[128,256]{0,1:T(8,128)(4,1)S(1)}, pred[128,256]{0,1:T(8,128)(4,1)}, u32[]{:S(2)}) copy-start(pred[128,256]{0,1:T(8,128)(4,1)} %copy-done.16) | copy-start | bytes 98308
  170.8 9.1 %copy-start.21 = (f32[4,8,128]{2,1,0:T(8,128)S(1)}, f32[4,8,128]{2,1,0:T(8,128)}, u32[]{:S(2)}) copy-start(f32[4,8,128]{2,1,0:T(8,128)} %copy-done.20) | copy-start | bytes 49156
  170.8 9.1 %copy-start.26 = (f32[4,8,128]{2,1,0:T(8,128)S(1)}, f32[4,8,128]{2,1,0:T(8,128)}, u32[]{:S(2)}) copy-start(f32[4,8,128]{2,1,0:T(8,128)} %copy-done.25) | copy-start | bytes 49156
  179.9 3.6 %copy-start.5 = (f32[4,256,128,8]{2,1,3,0:T(8,128)S(1)}, f32[4,256,128,8]{2,1,3,0:T(8,128)}, u32[]{:S(2)}) copy-start(f32[4,256,128,8]{2,1,3,0:T(8,128)} %copy-done.4) | copy-start | bytes 12582916
  179.9 3.6 %copy-start.28 = (bf16[1,128,256]{1,2,0:T(8,128)(2,1)S(1)}, bf16[1,128,256]{1,2,0:T(8,128)(2,1)}, u32[]{:S(2)}) copy-start(bf16[1,128,256]{1,2,0:T(8,128)(2,1)} %copy-done.27) | copy-start | bytes 196612
  179.9 3.6 %copy-start.30 = (bf16[128,256]{0,1:T(8,128)(2,1)S(1)}, bf16[128,256]{0,1:T(8,128)(2,1)}, u32[]{:S(2)}) copy-start(bf16[128,256]{0,1:T(8,128)(2,1)} %copy-done.29) | copy-start | bytes 196612
  183.5 1.5 copy-start.18
  183.5 1.5 copy-start.23
  185.2 1.7 copy-start.9
  185.2 2.5 %copy-start.15 = (bf16[128,256]{0,1:T(8,128)(2,1)S(1)}, bf16[128,256]{0,1:T(8,128)(2,1)}, u32[]{:S(2)}) copy-start(bf16[128,256]{0,1:T(8,128)(2,1)} %copy-done.14) | copy-start | bytes 196612
  186.9 1.3 slice-start

commit v3 on v2

--- a/solution.py
+++ b/solution.py
@@ -598,10 +598,65 @@
     )(slots, facts, gate, up, down)
 
 
+def attend(
+    side, queries_ref, key_block, value_block, sinks_ref, attended_ref, probs_ref, sink_probs_ref
+):
+    tokens = queries_ref.shape[0]
+    span = 2 * tokens
+    shared_heads = QUERY_HEADS // KEY_VALUE_HEADS
+    stacked = (tokens, span)
+    row = lax.broadcasted_iota(jnp.int32, stacked, 0)
+    col = lax.broadcasted_iota(jnp.int32, stacked, 1)
+    allowed = (col >= row + 1) & (col <= row + tokens) & (col + side * tokens >= tokens)
+    for group in range(KEY_VALUE_HEADS):
+        lanes = slice(group * HEAD_SIZE, (group + 1) * HEAD_SIZE)
+        group_keys = key_block[:, :, lanes].reshape(span, HEAD_SIZE)
+        group_values = value_block[:, :, lanes].reshape(span, HEAD_SIZE)
+        mixed = []
+        for head in range(group * shared_heads, (group + 1) * shared_heads):
+            scores = lax.dot_general(
+                queries_ref[:, head * HEAD_SIZE : (head + 1) * HEAD_SIZE],
+                group_keys,
+                (((1,), (1,)), ((), ())),
+                preferred_element_type=jnp.float32,
+            )
+            scores = jnp.where(allowed, scores * HEAD_SIZE ** (-0.5), -1e30)
+            sink = sinks_ref[head : head + 1, :1]
+            largest = jnp.maximum(jnp.max(scores, axis=1, keepdims=True), sink)
+            raised = jnp.where(allowed, jnp.exp(scores - largest), 0.0)
+            sink_raised = jnp.exp(sink - largest)
+            denominator = jnp.sum(raised, axis=1, keepdims=True) + sink_raised
+            probs = raised / denominator
+            probs_ref[head] = probs
+            sink_probs_ref[head] = sink_raised / denominator
+            mixed.append(
+                jnp.dot(
+                    probs.astype(jnp.bfloat16), group_values, preferred_element_type=jnp.float32
+                )
+            )
+            if len(mixed) * HEAD_SIZE == 128:
+                end = (head + 1) * HEAD_SIZE
+                attended_ref[:, end - 128 : end] = jnp.concatenate(mixed, axis=1).astype(
+                    jnp.bfloat16
+                )
+                mixed = []
+
+
 def gather_kernel(
     count,
     weight_ref,
+    queries_ref,
+    keys_ref,
+    values_ref,
+    sinks_ref,
     full_ref,
+    attended_ref,
+    probs_ref,
+    sink_probs_ref,
+    key_block,
+    value_block,
+    halo_send,
+    halo_recv,
     own_sem,
     line_send,
     line_recv,
@@ -748,6 +803,26 @@
         pair_copy(None, chunk).start()
     core_copy(None, 0, 0).start()
     keep.start()
+    halos = [
+        pltpu.make_async_remote_copy(
+            src_ref=source,
+            dst_ref=block.at[0],
+            send_sem=halo_send.at[at],
+            recv_sem=halo_recv.at[at],
+            device_id={"seq": 1 - side},
+            device_id_type=MESH,
+        )
+        for at, (source, block) in enumerate(((keys_ref, key_block), (values_ref, value_block)))
+    ]
+    for halo in halos:
+        halo.start()
+    key_block[1] = keys_ref[...]
+    value_block[1] = values_ref[...]
+    for halo in halos:
+        halo.wait()
+    attend(
+        side, queries_ref, key_block, value_block, sinks_ref, attended_ref, probs_ref, sink_probs_ref
+    )
 
     def line_step(wave):
         for chunk in (0, 1):
@@ -826,16 +901,29 @@
                     line_copy(way, wave, chunk).wait_send()
 
 
-def gathered(weight, count):
+def gather_and_attend(weight, queries, keys, values, sinks, count):
     waves = count // 4 - 1
     slots = 1 + 2 * waves
     dma = pltpu.SemaphoreType.DMA
-    full = pl.pallas_call(
+    hbm = pl.BlockSpec(memory_space=pl.ANY)
+    vmem = pl.BlockSpec(memory_space=pltpu.VMEM)
+    tokens = queries.shape[0]
+    sink_rows = jnp.broadcast_to(sinks[:, None], (QUERY_HEADS, 128))
+    full, attended, probs, sink_probs, key_block, value_block = pl.pallas_call(
         functools.partial(gather_kernel, count),
-        out_shape=jax.ShapeDtypeStruct((count,) + weight.shape, weight.dtype),
-        in_specs=[pl.BlockSpec(memory_space=pl.ANY)],
-        out_specs=pl.BlockSpec(memory_space=pl.ANY),
+        out_shape=(
+            jax.ShapeDtypeStruct((count,) + weight.shape, weight.dtype),
+            jax.ShapeDtypeStruct(queries.shape, jnp.bfloat16),
+            jax.ShapeDtypeStruct((QUERY_HEADS, tokens, 2 * tokens), jnp.float32),
+            jax.ShapeDtypeStruct((QUERY_HEADS, tokens, 1), jnp.float32),
+            jax.ShapeDtypeStruct((2,) + keys.shape, keys.dtype),
+            jax.ShapeDtypeStruct((2,) + values.shape, values.dtype),
+        ),
+        in_specs=[vmem] * 5,
+        out_specs=(hbm,) + (vmem,) * 5,
         scratch_shapes=[
+            dma((2,)),
+            dma((2,)),
             dma,
             dma((2, waves, 2)),
             dma((2, waves, 2)),
@@ -846,10 +934,20 @@
             dma((2, 2, slots)),
             dma((2, 2, slots)),
         ],
-        compiler_params=pltpu.CompilerParams(collective_id=2, has_side_effects=True),
+        compiler_params=pltpu.CompilerParams(
+            collective_id=2, has_side_effects=True, vmem_limit_bytes=40 * MIB
+        ),
         name="gather_kernel",
-    )(weight)
-    return full.reshape(count * weight.shape[0], weight.shape[1])
+    )(weight, queries, keys, values, sink_rows)
+    heads = (KEY_VALUE_HEADS, QUERY_HEADS // KEY_VALUE_HEADS, tokens)
+    return (
+        full.reshape(count * weight.shape[0], weight.shape[1]),
+        attended,
+        probs.reshape(heads + (2 * tokens,)),
+        sink_probs.reshape(heads),
+        key_block.reshape(2 * tokens, keys.shape[1]),
+        value_block.reshape(2 * tokens, values.shape[1]),
+    )
 
 
 def tail_kernel(
@@ -973,20 +1071,10 @@
     mask_wide = response_mask[0].astype(jnp.float32)
     local_count = jnp.sum(mask_wide)
     first_device = (seq_index == 0).astype(jnp.float32)
-    halo_keys, halo_values = passed_along((own_keys, own_values), "seq", 1)
-    key_tile_block = jnp.concatenate([halo_keys, own_keys], axis=0)
-    value_tile_block = jnp.concatenate([halo_values, own_values], axis=0)
-    row_index = jnp.arange(tokens_here, dtype=jnp.int32)[:, None]
-    col_index = jnp.arange(WINDOW + tokens_here, dtype=jnp.int32)[None, :]
-    allowed = (
-        (col_index >= row_index + 1)
-        & (col_index <= row_index + WINDOW)
-        & ((col_index >= WINDOW) | (seq_index > 0))
-    )
-    probs, sink_probs = head_scores(query_rows, key_tile_block, head_sink_logits, allowed)
+    out_full, attended, probs, sink_probs, key_tile_block, value_tile_block = gather_and_attend(
+        out_weight, query_rows, own_keys, own_values, head_sink_logits, dp_count
+    )
     reduced_probabilities = probs.astype(jnp.bfloat16)
-    attended = head_mix(reduced_probabilities, value_tile_block)
-    out_full = gathered(out_weight, dp_count)
     projected = jnp.dot(attended, out_full, preferred_element_type=jnp.float32)
     mid_rows = lax.optimization_barrier(
         (residual[0].astype(jnp.float32) + projected).astype(jnp.bfloat16)

time: 206 us -> 217 us (1.053)
  Pallas kernels: 131 us -> 144 us
  local copies, waits for them, and re-layouts: 15.3 us -> 27 us
  starting transfers between devices: 6.27 us -> 0 us
  matrix products: 35.4 us -> 31.5 us
  other arithmetic: 12.8 us -> 9.33 us
    pallas_call x1, Pallas kernels: 55.6 us -> 68.4 us  [gather_and_attend(): pl.pallas_call(functools.partial(gather_kernel, count), out_shape=(jax.Sh...]
    ppermute x2 -> x0, starting transfers between devices: 6.27 us -> none  [passed_along(): lax.ppermute(value, axis, [(source, source + steps) for source in range(i...]
    reshape x0 -> x1, local copies, waits for them, and re-layouts: none -> 5.4 us  [gather_and_attend(): probs.reshape(heads + (2 * tokens,))]
    dot_general x2 -> x0, matrix products: 4.28 us -> none  [the longest x1 3.53 us: head_mix(): jnp.einsum('amlh,hai->lami', reduced_probabilities, value_head_rows, pref...]
    unnamed x84 -> x60, local copies, waits for them, and re-layouts: 9.93 us -> 12.4 us
    slice x2, local copies, waits for them, and re-layouts: 0.1 us -> 2.57 us  [shards(): own_key_grad = key_gradient[WINDOW:]]
  transfers between devices with their start and end apart: 2 -> 0, of which waited for: 0 -> 0; matrix products, arithmetic and copies ran while one was open for 7% -> 0% of each run, Pallas kernels for 27% -> 0%
where the time goes in v3:
time: 217 us
  Pallas kernels  144 us (66%)
  matrix products  31.5 us (15%)
  local copies, waits for them, and re-layouts  27 us (12%)
  other arithmetic  9.33 us (4%)
  between operations  4.52 us (2%)
    pallas_call x1, Pallas kernels, gather_and_attend(): pl.pallas_call(functools.partial(gather_kernel, count), out_shape=(jax.Sh...  68.4 us
    pallas_call x1, Pallas kernels, in_place_experts(): pl.pallas_call(functools.partial(expert_kernel, count), out_shape=(result...  64.5 us
    unnamed x60, local copies, waits for them, and re-layouts  12.4 us
    pallas_call x1, Pallas kernels, tail_exchange(): pl.pallas_call(functools.partial(tail_kernel, count), out_shape=(jax.Shap...  11.4 us
    dot_general x1, matrix products, shards(): projected = jnp.dot(attended, out_full, preferred_element_type=jnp.float32)  8.54 us
    dot_general x1, matrix products, shards(): lax.dot_general(grad_residual, out_full, CONTRACT_LAST, preferred_element...  8.51 us
    reshape x1, local copies, waits for them, and re-layouts, gather_and_attend(): probs.reshape(heads + (2 * tokens,))  5.4 us

profile of v3, /device:TPU:0, one launch (start us, length us, event | category | flops | bytes accessed | tf_op | source)
XLA Modules:
  0.0 216.6 jit_solution(15401038357900931877)
XLA Ops:
  0.7 1.6 copy.59.weight_ref
  2.4 68.4 %gather_kernel.1 = (bf16[16,128,2880]{2,1,0:T(8,128)(2,1)}, bf16[128,2048]{1,0:T(8,128)(2,1)S(1)}, f32[32,128,256]{2,1,0:T(8,128)S(1)}, f32[32,128,1]{2,1,0:T(8,...) custom-call(bf16[128,2880]{1,0:T(8,128)(2,1)S(1)} %copy.59.weight_ref, ...), custom_call_target="tpu_custom_call" | custom-call | tf_op jit(solution)/shard_map/gather_kernel/pallas_call | solution.py:912
  70.8 2.0 copy-done.1
  72.7 1.3 copy-done.2
  74.1 0.6 copy-done.8
  74.7 0.7 copy-done.10
  75.4 8.5 %fusion.4 = bf16[128,2880]{0,1:T(8,128)(2,1)S(1)} fusion(bf16[128,2048]{1,0:T(8,128)(2,1)S(1)} %get-tuple-element.30, bf16[2048,2880]{1,0:T(8,128)(2,1)} %bitcast.136, bf16[1,128,2880]{1,2,0:T(8,128)(2,1)S(1)} %copy-done.23), kind=kOutput, calls=%fused_computation.9 | convolution fusion | flops 1511055360 | bytes 13795328 | tf_op jit(solution)/shard_map/dot_general | solution.py:1078
  83.9 0.4 fusion.16
  84.8 0.6 fusion.25
  85.4 1.5 fusion.23
  87.0 0.3 reshape.199
  89.1 0.6 convert_reduce_fusion
  89.7 0.7 select_maximum_fusion
  90.4 1.1 copy-done.7
  91.6 64.5 %expert_kernel.1 = (f32[17,8,256]{2,1,0:T(8,128)S(1)}, f32[17,8,256]{2,1,0:T(8,128)S(1)}) custom-call(f32[2,16,8,256]{3,2,1,0:T(8,128)S(1)} %pad.13.slots_ref, f32[8,256]{1,0:T(8,128)S(1)} %broadcast_in_dim.62.facts_ref, bf16[180,2048]{1,0:T(8,128)(2,1)S(1)} %copy-done.5, bf16[180,2048]{1,0:T(8,128)(2,1)S(1)} %copy-done.6, bf16[180,2048]{1,0:T(8,128)(2,1)S(1)} %copy-done.7), custom_call_target="tpu_custom_call" | custom-call | tf_op jit(solution)/shard_map/expert_kernel/pallas_call | solution.py:569
  156.2 0.2 fusion.45
  156.4 0.7 select_reduce_fusion.4
  158.5 0.6 slice.91
  160.2 2.0 fusion.27
  162.5 0.2 select_reduce_fusion
  163.1 1.4 convolution_bitcast_fusion
  164.6 0.6 fusion.11
  165.1 0.5 copy-done.19
  165.7 0.4 fusion.15
  166.1 0.9 copy-done.20
  167.0 8.5 %convolution_convert_fusion = bf16[128,2048]{1,0:T(8,128)(2,1)S(1)} fusion(bf16[128,2880]{0,1:T(8,128)(2,1)S(1)} %fusion.15, bf16[2048,2880]{1,0:T(8,128)(2,1)} %bitcast.137), kind=kOutput, calls=%fused_computation.10 | convolution fusion | flops 1510211584 | bytes 13058048 | tf_op jit(solution)/shard_map/dot_general | solution.py:1156
  175.5 0.3 copy.69
  175.8 2.7 %fusion.18 = f32[256,4,64]{0,2,1:T(8,128)S(1)} fusion(bf16[128,4,8,64]{0,3,2,1:T(8,128)(2,1)S(1)} %bitcast.138, f32[4,8,128,256]{3,2,1,0:T(8,128)} %bitcast.129), kind=kOutput, calls=%fused_computation.28 | convolution fusion | flops 135266304 | bytes 4980736 | tf_op jit(solution)/shard_map/ujko,kujm->oum/dot_general | solution.py:114
  178.5 0.7 copy-done.21
  179.3 5.4 %copy.71 = f32[4,8,128,256]{2,3,1,0:T(8,128)} copy(f32[4,8,128,256]{3,2,1,0:T(8,128)} %bitcast.130) | data formatting | bytes 8388608 | tf_op jit(solution)/shard_map/reshape | solution.py:946
  184.9 3.1 %fusion = (f32[4,8,128]{2,1,0:T(8,128)S(1)}, f32[4,256,128,8]{2,1,3,0:T(8,128)S(1)}) fusion(f32[4,8,128,256]{2,3,1,0:T(8,128)} %copy.71, bf16[128,4,8,64]{0,3,2,1:T(8,128)(2,1)S(1)} %bitcast.139, bf16[256,4,64,1]{0,2,1,3:T(8,128)(2,1)S(1)} %reshape.213), kind=kOutput, calls=%fused_computation.2 | convolution fusion | flops 136310784 | bytes 9060352 | tf_op jit(solution)/shard_map/baqj,eaj->aqbe/dot_general | solution.py:96
  188.0 0.3 copy-done.14
  188.4 0.9 fusion.2
  189.3 1.2 copy.73
  190.4 0.4 copy-done.15
  190.8 1.8 fusion.22
  192.8 0.7 pad_maximum_fusion.1.halo_ref
  193.4 1.9 copy.75
  195.4 2.0 multiply_reduce_fusion
  197.4 0.6 scatter.4.sinks_ref
  198.0 11.4 %tail_kernel.1 = (f32[8,128]{1,0:T(8,128)}, bf16[256,256]{1,0:T(8,128)(2,1)}) custom-call(f32[8,128]{1,0:T(8,128)} %scatter.4.sinks_ref, bf16[256,256]{1,0:T(8,128)(2,1)} %pad_maximum_fusion.1.halo_ref), custom_call_target="tpu_custom_call" | custom-call | tf_op jit(solution)/shard_map/tail_kernel/pallas_call | solution.py:1016
  209.4 0.9 convert_select_fusion
  210.5 1.6 slice.108
  212.0 1.0 copy.78
  213.0 0.7 fusion.40
  213.7 1.2 slice_bitcast_fusion.1
  215.2 0.5 fusion.17
  215.6 1.0 copy.80
  (98 shorter events, 3.2 us)
Async XLA Ops:
  0.6 159.6 %copy-start = (bf16[2880,128]{1,0:T(8,128)(2,1)S(1)}, bf16[2880,128]{1,0:T(8,128)(2,1)}, u32[]{:S(2)}) copy-start(bf16[2880,128]{1,0:T(8,128)(2,1)} %param.25) | copy-start | bytes 2211844
  0.6 1.6 copy-start.26
  0.7 1.7 copy-start.4
  0.7 1.7 copy-start.12
  0.7 1.7 copy-start.13
  0.7 74.7 %copy-start.23 = (bf16[1,128,2880]{1,2,0:T(8,128)(2,1)S(1)}, bf16[1,128,2880]{1,2,0:T(8,128)(2,1)}, u32[]{:S(2)}) copy-start(bf16[1,128,2880]{1,2,0:T(8,128)(2,1)} %param.22) | copy-start | bytes 2211844
  70.8 2.0 copy-start.1
  72.7 1.3 copy-start.2
  74.1 0.6 copy-start.8
  74.7 0.7 copy-start.10
  75.4 9.0 %copy-start.24 = (s32[1,128,4]{1,2,0:T(4,128)S(1)}, s32[1,128,4]{1,2,0:T(4,128)}, u32[]{:S(2)}) copy-start(s32[1,128,4]{1,2,0:T(4,128)} %param.29) | copy-start | bytes 6148
  75.4 9.5 %copy-start.25 = (f32[2880]{0:T(1024)S(1)}, f32[2880]{0:T(1024)}, u32[]{:S(2)}) copy-start(f32[2880]{0:T(1024)} %param.24) | copy-start | bytes 34564
  83.9 0.9 copy-start.17
  85.4 3.7 %copy-start.27 = (s32[1,128]{1,0:T(1,128)S(1)}, s32[1,128]{1,0:T(1,128)}, u32[]{:S(2)}) copy-start(s32[1,128]{1,0:T(1,128)} %param.32) | copy-start | bytes 1540
  85.4 5.0 %copy-start.5 = (bf16[180,2048]{1,0:T(8,128)(2,1)S(1)}, bf16[180,2048]{1,0:T(8,128)(2,1)}, u32[]{:S(2)}) copy-start(bf16[180,2048]{1,0:T(8,128)(2,1)} %gate_ref.1) | copy-start | bytes 2211844
  85.4 5.0 %copy-start.6 = (bf16[180,2048]{1,0:T(8,128)(2,1)S(1)}, bf16[180,2048]{1,0:T(8,128)(2,1)}, u32[]{:S(2)}) copy-start(bf16[180,2048]{1,0:T(8,128)(2,1)} %up_ref.1) | copy-start | bytes 2211844
  90.4 1.1 copy-start.7
  162.2 2.3 %copy-start.18 = (bf16[128,2880]{0,1:T(8,128)(2,1)S(1)}, bf16[128,2880]{0,1:T(8,128)(2,1)}, u32[]{:S(2)}) copy-start(bf16[128,2880]{0,1:T(8,128)(2,1)} %copy-done.17) | copy-start | bytes 2211844
  164.5 1.1 copy-start.19
  166.1 0.9 copy-start.20
  178.4 0.7 copy-start.21
  179.3 5.4 %copy-start.11 = (bf16[2,128,256]{2,1,0:T(8,128)(2,1)S(1)}, bf16[2,128,256]{2,1,0:T(8,128)(2,1)}, u32[]{:S(2)}) copy-start(bf16[2,128,256]{2,1,0:T(8,128)(2,1)} %copy-done.10) | copy-start | bytes 393220
  184.9 3.5 %copy-start.14 = (f32[4,8,128,256]{2,3,1,0:T(8,128)S(1)}, f32[4,8,128,256]{2,3,1,0:T(8,128)}, u32[]{:S(2)}) copy-start(f32[4,8,128,256]{2,3,1,0:T(8,128)} %copy.71) | copy-start | bytes 12582916
  189.3 1.5 copy-start.15
  192.6 2.8 %copy-start.22 = (f32[256,4,64]{0,2,1:T(8,128)}, f32[256,4,64]{0,2,1:T(8,128)S(1)}, u32[]{:S(2)}) copy-start(f32[256,4,64]{0,2,1:T(8,128)S(1)} %fusion.22) | copy-start | bytes 786436
  192.6 2.8 %copy-start.3 = (f32[32,128,1]{2,1,0:T(8,128)S(1)}, f32[32,128,1]{2,1,0:T(8,128)}, u32[]{:S(2)}) copy-start(f32[32,128,1]{2,1,0:T(8,128)} %copy-done.2) | copy-start | bytes 49156
  195.4 15.0 %slice-start = ((f32[256,4,64]{0,2,1:T(8,128)}), f32[128,4,64]{0,2,1:T(8,128)S(1)}, s32[]{:S(2)}) async-start(f32[256,4,64]{0,2,1:T(8,128)} %copy-done.21), calls=%async_computation | async-start | bytes 262144 | tf_op jit(solution)/shard_map/slice | solution.py:1173
  197.4 17.6 %copy-start.9 = (bf16[2,128,256]{2,1,0:T(8,128)(2,1)S(1)}, bf16[2,128,256]{2,1,0:T(8,128)(2,1)}, u32[]{:S(2)}) copy-start(bf16[2,128,256]{2,1,0:T(8,128)(2,1)} %copy-done.8) | copy-start | bytes 393220
  197.4 17.8 %copy-start.16 = (bf16[4,8,128,256]{2,3,1,0:T(8,128)(2,1)S(1)}, bf16[4,8,128,256]{2,3,1,0:T(8,128)(2,1)}, u32[]{:S(2)}) copy-start(bf16[4,8,128,256]{2,3,1,0:T(8,128)(2,1)} %copy-done.15) | copy-start | bytes 6291460

commit v4 on v3

--- a/solution.py
+++ b/solution.py
@@ -599,7 +599,7 @@
 
 
 def attend(
-    side, queries_ref, key_block, value_block, sinks_ref, attended_ref, probs_ref, sink_probs_ref
+    group, side, queries_ref, key_block, value_block, sinks_ref, attended_ref, probs_ref, sink_probs_ref
 ):
     tokens = queries_ref.shape[0]
     span = 2 * tokens
@@ -608,38 +608,37 @@
     row = lax.broadcasted_iota(jnp.int32, stacked, 0)
     col = lax.broadcasted_iota(jnp.int32, stacked, 1)
     allowed = (col >= row + 1) & (col <= row + tokens) & (col + side * tokens >= tokens)
-    for group in range(KEY_VALUE_HEADS):
-        lanes = slice(group * HEAD_SIZE, (group + 1) * HEAD_SIZE)
-        group_keys = key_block[:, :, lanes].reshape(span, HEAD_SIZE)
-        group_values = value_block[:, :, lanes].reshape(span, HEAD_SIZE)
-        mixed = []
-        for head in range(group * shared_heads, (group + 1) * shared_heads):
-            scores = lax.dot_general(
-                queries_ref[:, head * HEAD_SIZE : (head + 1) * HEAD_SIZE],
-                group_keys,
-                (((1,), (1,)), ((), ())),
-                preferred_element_type=jnp.float32,
+    lanes = slice(group * HEAD_SIZE, (group + 1) * HEAD_SIZE)
+    group_keys = key_block[:, :, lanes].reshape(span, HEAD_SIZE)
+    group_values = value_block[:, :, lanes].reshape(span, HEAD_SIZE)
+    mixed = []
+    for head in range(group * shared_heads, (group + 1) * shared_heads):
+        scores = lax.dot_general(
+            queries_ref[:, head * HEAD_SIZE : (head + 1) * HEAD_SIZE],
+            group_keys,
+            (((1,), (1,)), ((), ())),
+            preferred_element_type=jnp.float32,
+        )
+        scores = jnp.where(allowed, scores * HEAD_SIZE ** (-0.5), -1e30)
+        sink = sinks_ref[head : head + 1, :1]
+        largest = jnp.maximum(jnp.max(scores, axis=1, keepdims=True), sink)
+        raised = jnp.where(allowed, jnp.exp(scores - largest), 0.0)
+        sink_raised = jnp.exp(sink - largest)
+        denominator = jnp.sum(raised, axis=1, keepdims=True) + sink_raised
+        probs = raised / denominator
+        probs_ref[head] = probs
+        sink_probs_ref[head] = sink_raised / denominator
+        mixed.append(
+            jnp.dot(
+                probs.astype(jnp.bfloat16), group_values, preferred_element_type=jnp.float32
             )
-            scores = jnp.where(allowed, scores * HEAD_SIZE ** (-0.5), -1e30)
-            sink = sinks_ref[head : head + 1, :1]
-            largest = jnp.maximum(jnp.max(scores, axis=1, keepdims=True), sink)
-            raised = jnp.where(allowed, jnp.exp(scores - largest), 0.0)
-            sink_raised = jnp.exp(sink - largest)
-            denominator = jnp.sum(raised, axis=1, keepdims=True) + sink_raised
-            probs = raised / denominator
-            probs_ref[head] = probs
-            sink_probs_ref[head] = sink_raised / denominator
-            mixed.append(
-                jnp.dot(
-                    probs.astype(jnp.bfloat16), group_values, preferred_element_type=jnp.float32
-                )
+        )
+        if len(mixed) * HEAD_SIZE == 128:
+            end = (head + 1) * HEAD_SIZE
+            attended_ref[:, end - 128 : end] = jnp.concatenate(mixed, axis=1).astype(
+                jnp.bfloat16
             )
-            if len(mixed) * HEAD_SIZE == 128:
-                end = (head + 1) * HEAD_SIZE
-                attended_ref[:, end - 128 : end] = jnp.concatenate(mixed, axis=1).astype(
-                    jnp.bfloat16
-                )
-                mixed = []
+            mixed = []
 
 
 def gather_kernel(
@@ -820,9 +819,22 @@
     value_block[1] = values_ref[...]
     for halo in halos:
         halo.wait()
-    attend(
-        side, queries_ref, key_block, value_block, sinks_ref, attended_ref, probs_ref, sink_probs_ref
-    )
+
+    def attend_group(group):
+        attend(
+            group,
+            side,
+            queries_ref,
+            key_block,
+            value_block,
+            sinks_ref,
+            attended_ref,
+            probs_ref,
+            sink_probs_ref,
+        )
+
+    groups = list(range(KEY_VALUE_HEADS))
+    attend_group(groups.pop())
 
     def line_step(wave):
         for chunk in (0, 1):
@@ -870,10 +882,16 @@
     ordered = [[None]] + waved
     for wave in range(waves):
         line_step(wave)
+        if groups:
+            attend_group(groups.pop())
         pair_step(ordered[wave])
+        if groups:
+            attend_group(groups.pop())
         if wave:
             side_step(waved[wave - 1], 0)
             side_step(ordered[wave - 1], 1)
+    for group in groups:
+        attend_group(group)
     pair_step(ordered[waves])
     side_step(waved[waves - 1], 0)
     side_step(ordered[waves - 1], 1)
@@ -939,22 +957,37 @@
         ),
         name="gather_kernel",
     )(weight, queries, keys, values, sink_rows)
-    heads = (KEY_VALUE_HEADS, QUERY_HEADS // KEY_VALUE_HEADS, tokens)
-    return (
-        full.reshape(count * weight.shape[0], weight.shape[1]),
-        attended,
-        probs.reshape(heads + (2 * tokens,)),
-        sink_probs.reshape(heads),
-        key_block.reshape(2 * tokens, keys.shape[1]),
-        value_block.reshape(2 * tokens, values.shape[1]),
-    )
+    full = full.reshape(count * weight.shape[0], weight.shape[1])
+    return full, attended, probs, sink_probs, key_block, value_block
 
 
 def tail_kernel(
-    count, sinks_ref, halo_ref, sums_ref, came_ref, parts, half, far_half, dp_send, dp_recv, seq_send, seq_recv
+    count,
+    queries_ref,
+    key_block,
+    value_block,
+    probs_ref,
+    sink_probs_ref,
+    mixed_ref,
+    grad_queries_ref,
+    grad_keys_ref,
+    grad_values_ref,
+    sums_ref,
+    score_grads,
+    outgoing,
+    came,
+    sinks,
+    parts,
+    half,
+    far_half,
+    dp_send,
+    dp_recv,
+    seq_send,
+    seq_recv,
 ):
     me = lax.axis_index("dp")
-    far = 1 - lax.axis_index("seq")
+    side = lax.axis_index("seq")
+    far = 1 - side
     barrier = pltpu.get_barrier_semaphore()
     pl.semaphore_signal(barrier, inc=1, device_id={"seq": far}, device_id_type=MESH)
 
@@ -965,6 +998,53 @@
         return carry
 
     lax.fori_loop(1, count, greet, 0)
+
+    tokens = queries_ref.shape[0]
+    span = 2 * tokens
+    shared_heads = QUERY_HEADS // KEY_VALUE_HEADS
+    scaling = HEAD_SIZE ** (-0.5)
+    contract_last = (((1,), (1,)), ((), ()))
+    contract_first = (((0,), (0,)), ((), ()))
+
+    def lanes(head):
+        return slice(head * HEAD_SIZE, (head + 1) * HEAD_SIZE)
+
+    own_keys, own_values = [], []
+    for group in range(KEY_VALUE_HEADS):
+        group_values = value_block[:, :, lanes(group)].reshape(span, HEAD_SIZE)
+        key_grad = jnp.zeros((span, HEAD_SIZE), jnp.float32)
+        value_grad = jnp.zeros((span, HEAD_SIZE), jnp.float32)
+        for head in range(group * shared_heads, (group + 1) * shared_heads):
+            mixed = mixed_ref[:, lanes(head)]
+            probs = probs_ref[head]
+            prob_grad = lax.dot_general(
+                mixed, group_values, contract_last, preferred_element_type=jnp.float32
+            )
+            spread = jnp.sum(probs * prob_grad, axis=1, keepdims=True)
+            sinks[head : head + 1] = jnp.broadcast_to(
+                -jnp.sum(sink_probs_ref[head] * spread, axis=0, keepdims=True), (1, 128)
+            )
+            score_grad = (probs * (prob_grad - spread)).astype(jnp.bfloat16)
+            score_grads[head] = score_grad
+            key_grad += lax.dot_general(
+                score_grad,
+                queries_ref[:, lanes(head)],
+                contract_first,
+                preferred_element_type=jnp.float32,
+            )
+            value_grad += lax.dot_general(
+                probs.astype(jnp.bfloat16),
+                mixed,
+                contract_first,
+                preferred_element_type=jnp.float32,
+            )
+        own_keys.append(key_grad * scaling)
+        own_values.append(value_grad)
+    key_grad = jnp.concatenate(own_keys, axis=1)
+    value_grad = jnp.concatenate(own_values, axis=1)
+    outgoing[0] = key_grad[:tokens].astype(jnp.bfloat16)
+    outgoing[1] = value_grad[:tokens].astype(jnp.bfloat16)
+
     pl.semaphore_wait(barrier, count)
 
     def across(source, target, at):
@@ -979,7 +1059,7 @@
 
     def part_copy(step):
         return pltpu.make_async_remote_copy(
-            src_ref=sinks_ref,
+            src_ref=sinks,
             dst_ref=parts.at[me],
             send_sem=dp_send.at[step],
             recv_sem=dp_recv.at[step],
@@ -995,33 +1075,60 @@
         part_copy(step).wait()
         return carry
 
+    halo = across(outgoing, came, 0)
+    halo.start()
     lax.fori_loop(1, count, start_part, 0)
-    halo = across(halo_ref, came_ref, 0)
-    halo.start()
-    parts[me] = sinks_ref[...]
+    parts[me] = sinks[...]
+
+    def query_grads(group):
+        group_keys = key_block[:, :, lanes(group)].reshape(span, HEAD_SIZE)
+        pieces = []
+        for head in range(group * shared_heads, (group + 1) * shared_heads):
+            pieces.append(
+                jnp.dot(score_grads[head], group_keys, preferred_element_type=jnp.float32) * scaling
+            )
+        start = group * shared_heads * HEAD_SIZE
+        grad_queries_ref[:, start : start + shared_heads * HEAD_SIZE] = jnp.concatenate(
+            pieces, axis=1
+        ).astype(jnp.bfloat16)
+
+    early = KEY_VALUE_HEADS // 2
+    for group in range(early):
+        query_grads(group)
     lax.fori_loop(1, count, wait_part, 0)
     half[...] = jnp.sum(parts[...], axis=0)
     swap = across(half, far_half, 1)
     swap.start()
+    for group in range(early, KEY_VALUE_HEADS):
+        query_grads(group)
+    halo.wait()
+    taken = jnp.where(side == 0, came[...].astype(jnp.float32), 0.0)
+    grad_keys_ref[...] = (key_grad[tokens:] + taken[0]).astype(jnp.bfloat16)
+    grad_values_ref[...] = (value_grad[tokens:] + taken[1]).astype(jnp.bfloat16)
     swap.wait()
     sums_ref[...] = half[...] + far_half[...]
-    halo.wait()
-
-
-def tail_exchange(sinks, halo, count):
+
+
+def attention_backward(queries, key_block, value_block, probs, sink_probs, mixed, count):
     vmem = pl.BlockSpec(memory_space=pltpu.VMEM)
     dma = pltpu.SemaphoreType.DMA
-    tile = (8, 128)
-    row = jnp.zeros(tile, jnp.float32).at[0, : sinks.shape[0]].set(sinks)
-    sums, came = pl.pallas_call(
+    tile = (QUERY_HEADS, 128)
+    rows = jax.ShapeDtypeStruct(key_block.shape[1:], jnp.bfloat16)
+    grad_queries, grad_keys, grad_values, sums = pl.pallas_call(
         functools.partial(tail_kernel, count),
         out_shape=(
+            jax.ShapeDtypeStruct(queries.shape, jnp.bfloat16),
+            rows,
+            rows,
             jax.ShapeDtypeStruct(tile, jnp.float32),
-            jax.ShapeDtypeStruct(halo.shape, halo.dtype),
         ),
-        in_specs=[vmem] * 2,
-        out_specs=(vmem, vmem),
+        in_specs=[vmem] * 6,
+        out_specs=(vmem,) * 4,
         scratch_shapes=[
+            pltpu.VMEM(probs.shape, jnp.bfloat16),
+            pltpu.VMEM(key_block.shape, jnp.bfloat16),
+            pltpu.VMEM(key_block.shape, jnp.bfloat16),
+            pltpu.VMEM(tile, jnp.float32),
             pltpu.VMEM((count,) + tile, jnp.float32),
             pltpu.VMEM(tile, jnp.float32),
             pltpu.VMEM(tile, jnp.float32),
@@ -1030,10 +1137,12 @@
             dma((2,)),
             dma((2,)),
         ],
-        compiler_params=pltpu.CompilerParams(collective_id=3, has_side_effects=True),
+        compiler_params=pltpu.CompilerParams(
+            collective_id=3, has_side_effects=True, vmem_limit_bytes=40 * MIB
+        ),
         name="tail_kernel",
-    )(row, halo)
-    return sums[0, : sinks.shape[0]], came
+    )(queries, key_block, value_block, probs, sink_probs, mixed)
+    return grad_queries, grad_keys, grad_values, sums[:, 0]
 
 
 def shards(
@@ -1071,10 +1180,9 @@
     mask_wide = response_mask[0].astype(jnp.float32)
     local_count = jnp.sum(mask_wide)
     first_device = (seq_index == 0).astype(jnp.float32)
-    out_full, attended, probs, sink_probs, key_tile_block, value_tile_block = gather_and_attend(
+    out_full, attended, probs, sink_probs, key_block, value_block = gather_and_attend(
         out_weight, query_rows, own_keys, own_values, head_sink_logits, dp_count
     )
-    reduced_probabilities = probs.astype(jnp.bfloat16)
     projected = jnp.dot(attended, out_full, preferred_element_type=jnp.float32)
     mid_rows = lax.optimization_barrier(
         (residual[0].astype(jnp.float32) + projected).astype(jnp.bfloat16)
@@ -1156,32 +1264,13 @@
     grad_attended = lax.dot_general(
         grad_residual, out_full, CONTRACT_LAST, preferred_element_type=jnp.float32
     ).astype(jnp.bfloat16)
-    query_gradient, key_gradient, value_gradient, sink_gradient = head_grads(
-        probs,
-        reduced_probabilities,
-        sink_probs,
-        query_rows,
-        key_tile_block,
-        value_tile_block,
-        grad_attended,
-    )
-    halo = jnp.concatenate([key_gradient[:WINDOW], value_gradient[:WINDOW]], axis=0)
-    grad_sinks, came = tail_exchange(sink_gradient, halo.astype(jnp.bfloat16), dp_count)
-    came = jnp.where(seq_index + 1 < seq_count, came.astype(jnp.float32), 0.0)
-    next_keys, next_values = came[:WINDOW], came[WINDOW:]
-    own_key_grad = key_gradient[WINDOW:]
-    own_value_grad = value_gradient[WINDOW:]
-    split_at = tokens_here - WINDOW
-    grad_key_rows = jnp.concatenate(
-        [own_key_grad[:split_at], own_key_grad + next_keys], axis=0
-    ).astype(jnp.bfloat16)
-    grad_value_rows = jnp.concatenate(
-        [own_value_grad[:split_at], own_value_grad + next_values], axis=0
-    ).astype(jnp.bfloat16)
+    grad_queries, grad_keys, grad_values, grad_sinks = attention_backward(
+        query_rows, key_block, value_block, probs, sink_probs, grad_attended, dp_count
+    )
     return (
-        query_gradient[None],
-        grad_key_rows[None],
-        grad_value_rows[None],
+        grad_queries[None],
+        grad_keys[None],
+        grad_values[None],
         grad_residual[None],
         grad_sinks,
     )

time: 217 us -> 193 us (0.89)
  local copies, waits for them, and re-layouts: 27 us -> 15.3 us
  matrix products: 31.5 us -> 23.9 us
  Pallas kernels: 144 us -> 138 us
    pallas_call x1, Pallas kernels: 68.4 us -> 59.1 us  [gather_and_attend(): pl.pallas_call(functools.partial(gather_kernel, count), out_shape=(jax.Sh...]
    dot_general x4 -> x0, matrix products: 8.01 us -> none  [the longest x1 3.09 us: head_grads(): jnp.einsum('baqj,eaj->aqbe', heads_gradient, value_head_rows, preferred_e...]
    reshape x1 -> x0, local copies, waits for them, and re-layouts: 5.4 us -> none  [gather_and_attend(): probs.reshape(heads + (2 * tokens,))]
    pallas_call x1, Pallas kernels: 11.4 us -> 15.7 us  [attention_backward(): pl.pallas_call(functools.partial(tail_kernel, count), out_shape=(jax.Shap...]
    unnamed x60 -> x65, local copies, waits for them, and re-layouts: 12.4 us -> 9.5 us
    reshape x2, local copies, waits for them, and re-layouts: 0.48 us -> 3.09 us  [shards(): slots = slots.reshape(EW, 2 * CAP, dp_count, depth).transpose(0, 2, 1, 3)]
    slice x9 -> x1, local copies, waits for them, and re-layouts: 2.9 us -> 0.63 us  [attention_backward(): return (grad_queries, grad_keys, grad_values, sums[:, 0])]
where the time goes in v4:
time: 193 us; the launch traced here: 192 us
  Pallas kernels  138 us (72%)
  matrix products  23.9 us (12%)
  local copies, waits for them, and re-layouts  15.3 us (8%)
  other arithmetic  10.4 us (5%)
  between operations  4.43 us (2%)
    pallas_call x1, Pallas kernels, in_place_experts(): pl.pallas_call(functools.partial(expert_kernel, count), out_shape=(result...  63.4 us
    pallas_call x1, Pallas kernels, gather_and_attend(): pl.pallas_call(functools.partial(gather_kernel, count), out_shape=(jax.Sh...  59.1 us
    pallas_call x1, Pallas kernels, attention_backward(): pl.pallas_call(functools.partial(tail_kernel, count), out_shape=(jax.Shap...  15.7 us
    unnamed x65, local copies, waits for them, and re-layouts  9.5 us
    dot_general x1, matrix products, shards(): lax.dot_general(grad_residual, out_full, CONTRACT_LAST, preferred_element...  8.81 us
    dot_general x1, matrix products, shards(): projected = jnp.dot(attended, out_full, preferred_element_type=jnp.float32)  8.52 us

profile of v4, /device:TPU:0, one launch (start us, length us, event | category | flops | bytes accessed | tf_op | source)
XLA Modules:
  0.0 192.2 jit_solution(921891638779690884)
XLA Ops:
  2.1 1.3 convert_reduce_fusion
  3.6 0.7 select_maximum_fusion
  4.4 0.7 broadcast_in_dim.58.sinks_ref
  5.1 0.8 iota_compare_fusion
  5.9 0.6 copy-done.24
  6.6 0.2 reduce_window_sum.11
  6.8 2.1 %fusion.12 = f32[2,4,2880]{2,1,0:T(4,128)} fusion(pred[128,2,4]{0,2,1:T(4,128)(4,1)S(1)} %fusion.25, bf16[1,128,2880]{1,2,0:T(8,128)(2,1)} %param.31), kind=kOutput, calls=%fused_computation.18 | convolution fusion | flops 5898240 | bytes 830464 | tf_op jit(solution)/shard_map/tec,td->ecd/dot_general | solution.py:1212
  8.9 0.3 copy.31.weight_ref
  9.3 59.1 %gather_kernel.1 = (bf16[16,128,2880]{2,1,0:T(8,128)(2,1)}, bf16[128,2048]{1,0:T(8,128)(2,1)S(1)}, f32[32,128,256]{2,1,0:T(8,128)S(1)}, f32[32,128,1]{2,1,0:T(8,...) custom-call(bf16[128,2880]{1,0:T(8,128)(2,1)S(1)} %copy.31.weight_ref, ...), custom_call_target="tpu_custom_call" | custom-call | tf_op jit(solution)/shard_map/gather_kernel/pallas_call | solution.py:930
  68.5 2.0 %copy-done.1 = f32[32,128,256]{2,1,0:T(8,128)} copy-done((f32[32,128,256]{2,1,0:T(8,128)}, f32[32,128,256]{2,1,0:T(8,128)S(1)}, u32[]{:S(2)}) %copy-start.1) | copy-done | bytes 4194328
  70.4 1.3 copy-done.3
  71.7 0.6 copy-done.11
  72.4 0.7 copy-done.13
  73.1 8.5 %fusion.1 = bf16[128,2880]{0,1:T(8,128)(2,1)S(1)} fusion(bf16[128,2048]{1,0:T(8,128)(2,1)S(1)} %get-tuple-element.21, bf16[2048,2880]{1,0:T(8,128)(2,1)} %bitcast.82, bf16[1,128,2880]{1,2,0:T(8,128)(2,1)S(1)} %copy-done.22), kind=kOutput, calls=%fused_computation.4 | convolution fusion | flops 1511055360 | bytes 13795328 | tf_op jit(solution)/shard_map/dot_general | solution.py:1186
  81.6 0.4 fusion.11
  82.0 0.9 fusion.16
  82.9 0.1 select_reduce_fusion.1
  83.1 0.5 copy-done.27
  83.6 0.6 exponential_divide_fusion
  84.2 0.6 fusion.14
  84.8 0.7 pad_maximum_fusion
  85.5 2.0 %reshape.132 = f32[2,8,16,180]{3,2,1,0:T(8,128)} reshape(f32[2,8,2880]{2,1,0:T(8,128)} %pad_maximum_fusion) | data formatting | bytes 368640 | tf_op jit(solution)/shard_map/reshape | solution.py:1218
  87.5 1.1 copy.48
  88.7 63.4 %expert_kernel.1 = (f32[17,8,256]{2,1,0:T(8,128)S(1)}, f32[17,8,256]{2,1,0:T(8,128)S(1)}) custom-call(f32[2,16,8,256]{3,2,1,0:T(8,128)S(1)} %pad.8.slots_ref, f32[8,256]{1,0:T(8,128)S(1)} %broadcast_in_dim.88.facts_ref, bf16[180,2048]{1,0:T(8,128)(2,1)S(1)} %copy-done.6, bf16[180,2048]{1,0:T(8,128)(2,1)S(1)} %copy-done.7, bf16[180,2048]{1,0:T(8,128)(2,1)S(1)} %copy-done.8), custom_call_target="tpu_custom_call" | custom-call | tf_op jit(solution)/shard_map/expert_kernel/pallas_call | solution.py:569
  152.1 0.6 copy-done.9
  152.8 0.6 slice.43
  153.6 0.2 fusion.27
  153.8 0.7 select_reduce_fusion.4
  156.4 0.7 fusion.31
  157.1 0.8 fusion.29
  157.9 1.2 fusion.20
  159.2 0.1 reshape.134
  159.4 0.1 fusion.33
  159.5 0.7 select_reduce_fusion.3
  160.2 0.1 fusion.34
  160.4 0.6 multiply_reduce_fusion
  161.0 0.6 subtract_multiply_fusion
  161.6 0.2 select_reduce_fusion
  161.9 1.4 convolution_bitcast_fusion
  163.4 0.6 fusion.6
  163.9 0.5 copy-done.19
  164.5 0.4 fusion.10
  165.0 8.8 %convolution_convert_fusion.mixed_ref = bf16[128,2048]{1,0:T(8,128)(2,1)S(1)} fusion(bf16[128,2880]{0,1:T(8,128)(2,1)S(1)} %fusion.10, bf16[2048,2880]{1,0:T(8,128)(2,1)} %bitcast.83), kind=kOutput, calls=%fused_computation.5 | convolution fusion | flops 1510211584 | bytes 13058048 | tf_op jit(solution)/shard_map/dot_general | solution.py:1264
  173.9 15.7 %tail_kernel.1 = (bf16[128,2048]{1,0:T(8,128)(2,1)S(1)}, bf16[128,256]{1,0:T(8,128)(2,1)S(1)}, bf16[128,256]{1,0:T(8,128)(2,1)S(1)}, f32[32,128]{1,0:T(8,128)S(1)}) custom-call(bf16[128,2048]{1,0:T(8,128)(2,1)S(1)} %bitcast.74, bf16[2,128,256]{2,1,0:T(8,128)(2,1)S(1)} %copy-done.12, bf16[2,128,256]{2,1,0:T(8,128)(2,1)S(1)} %copy-done.14, ...), custom_call_target="tpu_custom_call" | custom-call | tf_op jit(solution)/shard_map/tail_kernel/pallas_call | solution.py:1117
  189.5 0.6 slice_reduce_fusion
  190.2 0.8 copy.54
  190.9 0.6 copy.55
  191.6 0.6 copy.56
  (76 shorter events, 1.1 us)
Async XLA Ops:
  0.6 81.4 %copy-start = (bf16[2880,128]{1,0:T(8,128)(2,1)S(1)}, bf16[2880,128]{1,0:T(8,128)(2,1)}, u32[]{:S(2)}) copy-start(bf16[2880,128]{1,0:T(8,128)(2,1)} %param.23) | copy-start | bytes 2211844
  0.6 8.3 %copy-start.21 = (bf16[128,2880]{0,1:T(8,128)(2,1)S(1)}, bf16[128,2880]{0,1:T(8,128)(2,1)}, u32[]{:S(2)}) copy-start(bf16[128,2880]{0,1:T(8,128)(2,1)} %param.21) | copy-start | bytes 2211844
  0.7 8.6 %copy-start.16 = (bf16[1,128,256]{2,1,0:T(8,128)(2,1)S(1)}, bf16[1,128,256]{2,1,0:T(8,128)(2,1)}, u32[]{:S(2)}) copy-start(bf16[1,128,256]{2,1,0:T(8,128)(2,1)} %param.18) | copy-start | bytes 196612
  0.7 8.6 %copy-start.15 = (bf16[1,128,256]{2,1,0:T(8,128)(2,1)S(1)}, bf16[1,128,256]{2,1,0:T(8,128)(2,1)}, u32[]{:S(2)}) copy-start(bf16[1,128,256]{2,1,0:T(8,128)(2,1)} %param.17) | copy-start | bytes 196612
  0.7 8.6 %copy-start.5 = (bf16[1,128,2048]{2,1,0:T(8,128)(2,1)S(1)}, bf16[1,128,2048]{2,1,0:T(8,128)(2,1)}, u32[]{:S(2)}) copy-start(bf16[1,128,2048]{2,1,0:T(8,128)(2,1)} %param.16) | copy-start | bytes 1572868
  5.8 0.6 copy-start.24
  9.3 63.7 %copy-start.22 = (bf16[1,128,2880]{1,2,0:T(8,128)(2,1)S(1)}, bf16[1,128,2880]{1,2,0:T(8,128)(2,1)}, u32[]{:S(2)}) copy-start(bf16[1,128,2880]{1,2,0:T(8,128)(2,1)} %param.20) | copy-start | bytes 2211844
  68.5 2.0 %copy-start.1 = (f32[32,128,256]{2,1,0:T(8,128)}, f32[32,128,256]{2,1,0:T(8,128)S(1)}, u32[]{:S(2)}) copy-start(f32[32,128,256]{2,1,0:T(8,128)S(1)} %get-tuple-element.19.probs_ref) | copy-start | bytes 12582916
  70.4 1.3 copy-start.3
  71.7 0.6 copy-start.11
  72.4 0.7 copy-start.13
  73.0 9.0 %copy-start.26 = (f32[2880]{0:T(1024)S(1)}, f32[2880]{0:T(1024)}, u32[]{:S(2)}) copy-start(f32[2880]{0:T(1024)} %param.22) | copy-start | bytes 34564
  81.6 3.2 %copy-start.17 = (bf16[128,2880]{0,1:T(8,128)(2,1)}, bf16[128,2880]{0,1:T(8,128)(2,1)S(1)}, u32[]{:S(2)}) copy-start(bf16[128,2880]{0,1:T(8,128)(2,1)S(1)} %fusion.1) | copy-start | bytes 2211844
  81.6 1.3 copy-start.25
  82.0 2.8 %copy-start.28 = (f32[128]{0:T(128)}, f32[128]{0:T(128)S(1)}, u32[]{:S(2)}) copy-start(f32[128]{0:T(128)S(1)} %add_rsqrt_fusion) | copy-start | bytes 1540
  82.0 2.7 %copy-start.23 = (f32[2,4,2880]{2,1,0:T(4,128)S(1)}, f32[2,4,2880]{2,1,0:T(4,128)}, u32[]{:S(2)}) copy-start(f32[2,4,2880]{2,1,0:T(4,128)} %fusion.12) | copy-start | bytes 276484
  83.1 0.5 copy-start.27
  84.2 4.4 %copy-start.6 = (bf16[180,2048]{1,0:T(8,128)(2,1)S(1)}, bf16[180,2048]{1,0:T(8,128)(2,1)}, u32[]{:S(2)}) copy-start(bf16[180,2048]{1,0:T(8,128)(2,1)} %gate_ref.1) | copy-start | bytes 2211844
  84.2 4.4 %copy-start.7 = (bf16[180,2048]{1,0:T(8,128)(2,1)S(1)}, bf16[180,2048]{1,0:T(8,128)(2,1)}, u32[]{:S(2)}) copy-start(bf16[180,2048]{1,0:T(8,128)(2,1)} %up_ref.1) | copy-start | bytes 2211844
  84.2 4.5 %copy-start.8 = (bf16[180,2048]{1,0:T(8,128)(2,1)S(1)}, bf16[180,2048]{1,0:T(8,128)(2,1)}, u32[]{:S(2)}) copy-start(bf16[180,2048]{1,0:T(8,128)(2,1)} %down_ref.1) | copy-start | bytes 2211844
  152.1 0.6 copy-start.9
  152.1 0.7 copy-start.10
  152.8 10.5 %copy-start.18 = (bf16[128,2880]{0,1:T(8,128)(2,1)S(1)}, bf16[128,2880]{0,1:T(8,128)(2,1)}, u32[]{:S(2)}) copy-start(bf16[128,2880]{0,1:T(8,128)(2,1)} %copy-done.17) | copy-start | bytes 2211844
  152.8 10.6 %copy-start.29 = (f32[128]{0:T(128)S(1)}, f32[128]{0:T(128)}, u32[]{:S(2)}) copy-start(f32[128]{0:T(128)} %copy-done.28) | copy-start | bytes 1540
  163.4 1.1 copy-start.19
  164.9 8.9 %copy-start.20 = (bf16[128,2880]{0,1:T(8,128)(2,1)}, bf16[128,2880]{0,1:T(8,128)(2,1)S(1)}, u32[]{:S(2)}) copy-start(bf16[128,2880]{0,1:T(8,128)(2,1)S(1)} %fusion.10) | copy-start | bytes 2211844
  164.9 8.9 %copy-start.2 = (f32[32,128,256]{2,1,0:T(8,128)S(1)}, f32[32,128,256]{2,1,0:T(8,128)}, u32[]{:S(2)}) copy-start(f32[32,128,256]{2,1,0:T(8,128)} %copy-done.1) | copy-start | bytes 12582916
  165.0 8.9 %copy-start.4 = (f32[32,128,1]{2,1,0:T(8,128)S(1)}, f32[32,128,1]{2,1,0:T(8,128)}, u32[]{:S(2)}) copy-start(f32[32,128,1]{2,1,0:T(8,128)} %copy-done.3) | copy-start | bytes 49156
  165.0 8.9 %copy-start.12 = (bf16[2,128,256]{2,1,0:T(8,128)(2,1)S(1)}, bf16[2,128,256]{2,1,0:T(8,128)(2,1)}, u32[]{:S(2)}) copy-start(bf16[2,128,256]{2,1,0:T(8,128)(2,1)} %copy-done.11) | copy-start | bytes 393220
  165.0 8.9 %copy-start.14 = (bf16[2,128,256]{2,1,0:T(8,128)(2,1)S(1)}, bf16[2,128,256]{2,1,0:T(8,128)(2,1)}, u32[]{:S(2)}) copy-start(bf16[2,128,256]{2,1,0:T(8,128)(2,1)} %copy-done.13) | copy-start | bytes 393220

commit v5 on v4

--- a/solution.py
+++ b/solution.py
@@ -447,42 +447,52 @@
                 preferred_element_type=jnp.float32,
             ).reshape(half, rows, tile)
 
-        for column in range(0, wide, tile):
-            yield column, jnp.concatenate([product(column), product(wide + column)], axis=1)
-
-    def halve_copy(stage):
-        blocks = half >> stage
+        def tile_at(column):
+            return jnp.concatenate([product(column), product(wide + column)], axis=1)
+
+        return tile_at
+
+    def halve_copy(stage, chunk):
+        at = pl.ds(chunk * width, width)
         return pltpu.make_async_remote_copy(
-            src_ref=sent[stage],
-            dst_ref=received[stage],
-            send_sem=halve_send.at[stage],
-            recv_sem=halve_recv.at[stage],
+            src_ref=sent[stage].at[:, :, at],
+            dst_ref=received[stage].at[:, :, at],
+            send_sem=halve_send.at[stage, chunk],
+            recv_sem=halve_recv.at[stage, chunk],
             device_id={"dp": flipped(me, 1 << stage)},
             device_id_type=MESH,
         )
 
+    width = hidden // 2
+    chunks = wide // width
     bit_of = [lax.rem(lax.div(me, 1 << stage), 2) for stage in range(bits)]
-    for column, value in products((1 - bit_of[0]) * half):
-        sent[0][:, :, column : column + tile] = value.astype(jnp.bfloat16)
-    halve_copy(0).start()
-    for column, value in products(bit_of[0] * half):
-        total[:, :, column : column + tile] = value
+    tile_at = products((1 - bit_of[0]) * half)
+    for chunk in range(chunks):
+        for column in range(chunk * width, (chunk + 1) * width, tile):
+            sent[0][:, :, column : column + tile] = tile_at(column).astype(jnp.bfloat16)
+        halve_copy(0, chunk).start()
+    tile_at = products(bit_of[0] * half)
+    for column in range(0, wide, tile):
+        total[:, :, column : column + tile] = tile_at(column)
     base = 0
     for stage in range(1, bits):
         blocks = half >> stage
-        halve_copy(stage - 1).wait()
         away = (1 - bit_of[stage]) * blocks
         keep = bit_of[stage] * blocks
-        sent[stage][...] = (
-            total[pl.ds(base + away, blocks)]
-            + received[stage - 1][pl.ds(away, blocks)].astype(jnp.float32)
-        ).astype(jnp.bfloat16)
-        halve_copy(stage).start()
-        total[pl.ds(base + keep, blocks)] += received[stage - 1][pl.ds(keep, blocks)].astype(
-            jnp.float32
-        )
+        for chunk in range(chunks):
+            at = slice(chunk * width, (chunk + 1) * width)
+            halve_copy(stage - 1, chunk).wait()
+            sent[stage][:, :, at] = (
+                total[pl.ds(base + away, blocks), :, at]
+                + received[stage - 1][pl.ds(away, blocks), :, at].astype(jnp.float32)
+            ).astype(jnp.bfloat16)
+            halve_copy(stage, chunk).start()
+            total[pl.ds(base + keep, blocks), :, at] += received[stage - 1][
+                pl.ds(keep, blocks), :, at
+            ].astype(jnp.float32)
         base = base + keep
-    halve_copy(bits - 1).wait()
+    for chunk in range(chunks):
+        halve_copy(bits - 1, chunk).wait()
     summed = total[base] + received[bits - 1][0].astype(jnp.float32)
 
     gate_pre = summed[:rows, :hidden]
@@ -499,24 +509,35 @@
     )
     grads[place] = jnp.concatenate([grad_gate, grad_up], axis=0).astype(jnp.bfloat16)
 
-    for stage in range(bits):
+    def double_copy(stage, chunk):
         blocks = 1 << stage
-        start = place // blocks * blocks
-        copy = pltpu.make_async_remote_copy(
-            src_ref=grads.at[pl.ds(start, blocks)],
-            dst_ref=grads.at[pl.ds(start, blocks)],
-            send_sem=double_send.at[stage],
-            recv_sem=double_recv.at[stage],
+        part = grads.at[pl.ds(place // blocks * blocks, blocks), :, pl.ds(chunk * width, width)]
+        return pltpu.make_async_remote_copy(
+            src_ref=part,
+            dst_ref=part,
+            send_sem=double_send.at[stage, chunk],
+            recv_sem=double_recv.at[stage, chunk],
             device_id={"dp": flipped(me, half >> stage)},
             device_id_type=MESH,
         )
-        copy.start()
-        copy.wait()
-
-    flat = grads[...].reshape(count * 2 * rows, hidden)
+
+    for stage in range(bits):
+        for chunk in range(2):
+            if stage:
+                double_copy(stage - 1, chunk).wait()
+            double_copy(stage, chunk).start()
+
     contract = (((1,), (1,)), ((), ()))
-    from_gate = lax.dot_general(flat, gate_ref[...], contract, preferred_element_type=jnp.float32)
-    from_up = lax.dot_general(flat, up_ref[...], contract, preferred_element_type=jnp.float32)
+    from_gate = jnp.zeros((count * 2 * rows, depth), jnp.float32)
+    from_up = jnp.zeros((count * 2 * rows, depth), jnp.float32)
+    for chunk in range(2):
+        double_copy(bits - 1, chunk).wait()
+        at = slice(chunk * width, (chunk + 1) * width)
+        flat = grads[:, :, at].reshape(count * 2 * rows, width)
+        from_gate += lax.dot_general(
+            flat, gate_ref[:, at], contract, preferred_element_type=jnp.float32
+        )
+        from_up += lax.dot_general(flat, up_ref[:, at], contract, preferred_element_type=jnp.float32)
     from_gate = from_gate.reshape(count, 2 * rows, depth)
     from_up = from_up.reshape(count, 2 * rows, depth)
     back[:, :, :depth] = from_gate[:, :rows] + from_up[:, rows:]
@@ -584,10 +605,10 @@
             dma((2,)),
             dma((count,)),
             dma((count,)),
-            dma((bits,)),
-            dma((bits,)),
-            dma((bits,)),
-            dma((bits,)),
+            dma((bits, 3)),
+            dma((bits, 3)),
+            dma((bits, 2)),
+            dma((bits, 2)),
             dma((count,)),
             dma((count,)),
         ],

time: 193 us -> 187 us (0.969)
  Pallas kernels: 138 us -> 133 us
    pallas_call x1, Pallas kernels: 63.4 us -> 58 us  [in_place_experts(): pl.pallas_call(functools.partial(expert_kernel, count), out_shape=(result...]
where the time goes in v5:
time: 187 us
  Pallas kernels  133 us (71%)
  matrix products  23.9 us (13%)
  local copies, waits for them, and re-layouts  15.3 us (8%)
  other arithmetic  10.4 us (6%)
  between operations  4.43 us (2%)
    pallas_call x1, Pallas kernels, gather_and_attend(): pl.pallas_call(functools.partial(gather_kernel, count), out_shape=(jax.Sh...  59.1 us
    pallas_call x1, Pallas kernels, in_place_experts(): pl.pallas_call(functools.partial(expert_kernel, count), out_shape=(result...  58 us
    pallas_call x1, Pallas kernels, attention_backward(): pl.pallas_call(functools.partial(tail_kernel, count), out_shape=(jax.Shap...  15.4 us
    unnamed x65, local copies, waits for them, and re-layouts  9.5 us
    dot_general x1, matrix products, shards(): lax.dot_general(grad_residual, out_full, CONTRACT_LAST, preferred_element...  8.8 us
    dot_general x1, matrix products, shards(): projected = jnp.dot(attended, out_full, preferred_element_type=jnp.float32)  8.52 us

profile of v5, /device:TPU:0, one launch (start us, length us, event | category | flops | bytes accessed | tf_op | source)
XLA Modules:
  0.0 186.5 jit_solution(5385144866912832984)
XLA Ops:
  2.1 1.3 convert_reduce_fusion
  3.6 0.7 select_maximum_fusion
  4.4 0.7 broadcast_in_dim.58.sinks_ref
  5.1 0.8 iota_compare_fusion
  5.9 0.6 copy-done.24
  6.6 0.2 reduce_window_sum.11
  6.8 2.1 %fusion.12 = f32[2,4,2880]{2,1,0:T(4,128)} fusion(pred[128,2,4]{0,2,1:T(4,128)(4,1)S(1)} %fusion.25, bf16[1,128,2880]{1,2,0:T(8,128)(2,1)} %param.31), kind=kOutput, calls=%fused_computation.18 | convolution fusion | flops 5898240 | bytes 830464 | tf_op jit(solution)/shard_map/tec,td->ecd/dot_general | solution.py:1233
  8.9 0.3 copy.31.weight_ref
  9.3 59.1 %gather_kernel.1 = (bf16[16,128,2880]{2,1,0:T(8,128)(2,1)}, bf16[128,2048]{1,0:T(8,128)(2,1)S(1)}, f32[32,128,256]{2,1,0:T(8,128)S(1)}, f32[32,128,1]{2,1,0:T(8,...) custom-call(bf16[128,2880]{1,0:T(8,128)(2,1)S(1)} %copy.31.weight_ref, ...), custom_call_target="tpu_custom_call" | custom-call | tf_op jit(solution)/shard_map/gather_kernel/pallas_call | solution.py:951
  68.5 2.0 %copy-done.1 = f32[32,128,256]{2,1,0:T(8,128)} copy-done((f32[32,128,256]{2,1,0:T(8,128)}, f32[32,128,256]{2,1,0:T(8,128)S(1)}, u32[]{:S(2)}) %copy-start.1) | copy-done | bytes 4194328
  70.4 1.3 copy-done.3
  71.7 0.6 copy-done.11
  72.4 0.7 copy-done.13
  73.1 8.5 %fusion.1 = bf16[128,2880]{0,1:T(8,128)(2,1)S(1)} fusion(bf16[128,2048]{1,0:T(8,128)(2,1)S(1)} %get-tuple-element.21, bf16[2048,2880]{1,0:T(8,128)(2,1)} %bitcast.82, bf16[1,128,2880]{1,2,0:T(8,128)(2,1)S(1)} %copy-done.22), kind=kOutput, calls=%fused_computation.4 | convolution fusion | flops 1511055360 | bytes 13795328 | tf_op jit(solution)/shard_map/dot_general | solution.py:1207
  81.6 0.4 fusion.11
  82.0 0.9 fusion.16
  82.9 0.1 select_reduce_fusion.1
  83.1 0.5 copy-done.27
  83.6 0.6 exponential_divide_fusion
  84.2 0.6 fusion.14
  84.8 0.7 pad_maximum_fusion
  85.5 2.0 %reshape.132 = f32[2,8,16,180]{3,2,1,0:T(8,128)} reshape(f32[2,8,2880]{2,1,0:T(8,128)} %pad_maximum_fusion) | data formatting | bytes 368640 | tf_op jit(solution)/shard_map/reshape | solution.py:1239
  87.5 1.1 copy.48
  88.7 58.0 %expert_kernel.1 = (f32[17,8,256]{2,1,0:T(8,128)S(1)}, f32[17,8,256]{2,1,0:T(8,128)S(1)}) custom-call(f32[2,16,8,256]{3,2,1,0:T(8,128)S(1)} %pad.8.slots_ref, f32[8,256]{1,0:T(8,128)S(1)} %broadcast_in_dim.88.facts_ref, bf16[180,2048]{1,0:T(8,128)(2,1)S(1)} %copy-done.6, bf16[180,2048]{1,0:T(8,128)(2,1)S(1)} %copy-done.7, bf16[180,2048]{1,0:T(8,128)(2,1)S(1)} %copy-done.8), custom_call_target="tpu_custom_call" | custom-call | tf_op jit(solution)/shard_map/expert_kernel/pallas_call | solution.py:590
  146.7 0.6 copy-done.9
  147.4 0.6 slice.43
  148.2 0.2 fusion.27
  148.4 0.7 select_reduce_fusion.4
  151.0 0.7 fusion.31
  151.7 0.8 fusion.29
  152.4 1.2 fusion.20
  153.8 0.1 reshape.134
  154.0 0.1 fusion.33
  154.1 0.7 select_reduce_fusion.3
  154.8 0.1 fusion.34
  155.0 0.6 multiply_reduce_fusion
  155.6 0.6 subtract_multiply_fusion
  156.2 0.2 select_reduce_fusion
  156.5 1.4 convolution_bitcast_fusion
  158.0 0.6 fusion.6
  158.5 0.5 copy-done.19
  159.1 0.4 fusion.10
  159.6 8.8 %convolution_convert_fusion.mixed_ref = bf16[128,2048]{1,0:T(8,128)(2,1)S(1)} fusion(bf16[128,2880]{0,1:T(8,128)(2,1)S(1)} %fusion.10, bf16[2048,2880]{1,0:T(8,128)(2,1)} %bitcast.83), kind=kOutput, calls=%fused_computation.5 | convolution fusion | flops 1510211584 | bytes 13058048 | tf_op jit(solution)/shard_map/dot_general | solution.py:1285
  168.4 15.4 %tail_kernel.1 = (bf16[128,2048]{1,0:T(8,128)(2,1)S(1)}, bf16[128,256]{1,0:T(8,128)(2,1)S(1)}, bf16[128,256]{1,0:T(8,128)(2,1)S(1)}, f32[32,128]{1,0:T(8,128)S(1)}) custom-call(bf16[128,2048]{1,0:T(8,128)(2,1)S(1)} %bitcast.74, bf16[2,128,256]{2,1,0:T(8,128)(2,1)S(1)} %copy-done.12, bf16[2,128,256]{2,1,0:T(8,128)(2,1)S(1)} %copy-done.14, ...), custom_call_target="tpu_custom_call" | custom-call | tf_op jit(solution)/shard_map/tail_kernel/pallas_call | solution.py:1138
  183.9 0.6 slice_reduce_fusion
  184.5 0.8 copy.54
  185.3 0.6 copy.55
  185.9 0.6 copy.56
  (76 shorter events, 1.1 us)
Async XLA Ops:
  0.6 81.4 %copy-start = (bf16[2880,128]{1,0:T(8,128)(2,1)S(1)}, bf16[2880,128]{1,0:T(8,128)(2,1)}, u32[]{:S(2)}) copy-start(bf16[2880,128]{1,0:T(8,128)(2,1)} %param.23) | copy-start | bytes 2211844
  0.6 8.3 %copy-start.21 = (bf16[128,2880]{0,1:T(8,128)(2,1)S(1)}, bf16[128,2880]{0,1:T(8,128)(2,1)}, u32[]{:S(2)}) copy-start(bf16[128,2880]{0,1:T(8,128)(2,1)} %param.21) | copy-start | bytes 2211844
  0.7 8.6 %copy-start.16 = (bf16[1,128,256]{2,1,0:T(8,128)(2,1)S(1)}, bf16[1,128,256]{2,1,0:T(8,128)(2,1)}, u32[]{:S(2)}) copy-start(bf16[1,128,256]{2,1,0:T(8,128)(2,1)} %param.18) | copy-start | bytes 196612
  0.7 8.6 %copy-start.15 = (bf16[1,128,256]{2,1,0:T(8,128)(2,1)S(1)}, bf16[1,128,256]{2,1,0:T(8,128)(2,1)}, u32[]{:S(2)}) copy-start(bf16[1,128,256]{2,1,0:T(8,128)(2,1)} %param.17) | copy-start | bytes 196612
  0.7 8.6 %copy-start.5 = (bf16[1,128,2048]{2,1,0:T(8,128)(2,1)S(1)}, bf16[1,128,2048]{2,1,0:T(8,128)(2,1)}, u32[]{:S(2)}) copy-start(bf16[1,128,2048]{2,1,0:T(8,128)(2,1)} %param.16) | copy-start | bytes 1572868
  5.8 0.6 copy-start.24
  9.3 63.7 %copy-start.22 = (bf16[1,128,2880]{1,2,0:T(8,128)(2,1)S(1)}, bf16[1,128,2880]{1,2,0:T(8,128)(2,1)}, u32[]{:S(2)}) copy-start(bf16[1,128,2880]{1,2,0:T(8,128)(2,1)} %param.20) | copy-start | bytes 2211844
  68.5 2.0 %copy-start.1 = (f32[32,128,256]{2,1,0:T(8,128)}, f32[32,128,256]{2,1,0:T(8,128)S(1)}, u32[]{:S(2)}) copy-start(f32[32,128,256]{2,1,0:T(8,128)S(1)} %get-tuple-element.19.probs_ref) | copy-start | bytes 12582916
  70.4 1.3 copy-start.3
  71.7 0.6 copy-start.11
  72.4 0.7 copy-start.13
  73.0 9.0 %copy-start.26 = (f32[2880]{0:T(1024)S(1)}, f32[2880]{0:T(1024)}, u32[]{:S(2)}) copy-start(f32[2880]{0:T(1024)} %param.22) | copy-start | bytes 34564
  81.6 3.2 %copy-start.17 = (bf16[128,2880]{0,1:T(8,128)(2,1)}, bf16[128,2880]{0,1:T(8,128)(2,1)S(1)}, u32[]{:S(2)}) copy-start(bf16[128,2880]{0,1:T(8,128)(2,1)S(1)} %fusion.1) | copy-start | bytes 2211844
  81.6 1.3 copy-start.25
  82.0 2.8 %copy-start.28 = (f32[128]{0:T(128)}, f32[128]{0:T(128)S(1)}, u32[]{:S(2)}) copy-start(f32[128]{0:T(128)S(1)} %add_rsqrt_fusion) | copy-start | bytes 1540
  82.0 2.7 %copy-start.23 = (f32[2,4,2880]{2,1,0:T(4,128)S(1)}, f32[2,4,2880]{2,1,0:T(4,128)}, u32[]{:S(2)}) copy-start(f32[2,4,2880]{2,1,0:T(4,128)} %fusion.12) | copy-start | bytes 276484
  83.1 0.5 copy-start.27
  84.2 4.4 %copy-start.6 = (bf16[180,2048]{1,0:T(8,128)(2,1)S(1)}, bf16[180,2048]{1,0:T(8,128)(2,1)}, u32[]{:S(2)}) copy-start(bf16[180,2048]{1,0:T(8,128)(2,1)} %gate_ref.1) | copy-start | bytes 2211844
  84.2 4.4 %copy-start.7 = (bf16[180,2048]{1,0:T(8,128)(2,1)S(1)}, bf16[180,2048]{1,0:T(8,128)(2,1)}, u32[]{:S(2)}) copy-start(bf16[180,2048]{1,0:T(8,128)(2,1)} %up_ref.1) | copy-start | bytes 2211844
  84.2 4.5 %copy-start.8 = (bf16[180,2048]{1,0:T(8,128)(2,1)S(1)}, bf16[180,2048]{1,0:T(8,128)(2,1)}, u32[]{:S(2)}) copy-start(bf16[180,2048]{1,0:T(8,128)(2,1)} %down_ref.1) | copy-start | bytes 2211844
  146.7 0.6 copy-start.9
  146.7 0.7 copy-start.10
  147.4 10.5 %copy-start.18 = (bf16[128,2880]{0,1:T(8,128)(2,1)S(1)}, bf16[128,2880]{0,1:T(8,128)(2,1)}, u32[]{:S(2)}) copy-start(bf16[128,2880]{0,1:T(8,128)(2,1)} %copy-done.17) | copy-start | bytes 2211844
  147.4 10.6 %copy-start.29 = (f32[128]{0:T(128)S(1)}, f32[128]{0:T(128)}, u32[]{:S(2)}) copy-start(f32[128]{0:T(128)} %copy-done.28) | copy-start | bytes 1540
  158.0 1.1 copy-start.19
  159.5 8.9 %copy-start.20 = (bf16[128,2880]{0,1:T(8,128)(2,1)}, bf16[128,2880]{0,1:T(8,128)(2,1)S(1)}, u32[]{:S(2)}) copy-start(bf16[128,2880]{0,1:T(8,128)(2,1)S(1)} %fusion.10) | copy-start | bytes 2211844
  159.5 8.9 %copy-start.2 = (f32[32,128,256]{2,1,0:T(8,128)S(1)}, f32[32,128,256]{2,1,0:T(8,128)}, u32[]{:S(2)}) copy-start(f32[32,128,256]{2,1,0:T(8,128)} %copy-done.1) | copy-start | bytes 12582916
  159.5 8.9 %copy-start.4 = (f32[32,128,1]{2,1,0:T(8,128)S(1)}, f32[32,128,1]{2,1,0:T(8,128)}, u32[]{:S(2)}) copy-start(f32[32,128,1]{2,1,0:T(8,128)} %copy-done.3) | copy-start | bytes 49156
  159.5 8.9 %copy-start.12 = (bf16[2,128,256]{2,1,0:T(8,128)(2,1)S(1)}, bf16[2,128,256]{2,1,0:T(8,128)(2,1)}, u32[]{:S(2)}) copy-start(bf16[2,128,256]{2,1,0:T(8,128)(2,1)} %copy-done.11) | copy-start | bytes 393220
  159.6 8.9 %copy-start.14 = (bf16[2,128,256]{2,1,0:T(8,128)(2,1)S(1)}, bf16[2,128,256]{2,1,0:T(8,128)(2,1)}, u32[]{:S(2)}) copy-start(bf16[2,128,256]{2,1,0:T(8,128)(2,1)} %copy-done.13) | copy-start | bytes 393220

commit v6 on v5

--- a/solution.py
+++ b/solution.py
@@ -671,10 +671,13 @@
     sinks_ref,
     full_ref,
     attended_ref,
+    probs_out,
+    sink_probs_out,
+    key_block,
+    value_block,
     probs_ref,
     sink_probs_ref,
-    key_block,
-    value_block,
+    save_sem,
     halo_send,
     halo_recv,
     own_sem,
@@ -854,6 +857,18 @@
             sink_probs_ref,
         )
 
+        for copy in saves(group):
+            copy.start()
+
+    def saves(group):
+        shared_heads = QUERY_HEADS // KEY_VALUE_HEADS
+        heads = pl.ds(group * shared_heads, shared_heads)
+        pairs = ((probs_ref, probs_out), (sink_probs_ref, sink_probs_out))
+        return [
+            pltpu.make_async_copy(held_ref.at[heads], out.at[heads], save_sem.at[at, group])
+            for at, (held_ref, out) in enumerate(pairs)
+        ]
+
     groups = list(range(KEY_VALUE_HEADS))
     attend_group(groups.pop())
 
@@ -919,6 +934,9 @@
     side_step(ordered[waves], 1)
 
     keep.wait()
+    for group in range(KEY_VALUE_HEADS):
+        for copy in saves(group):
+            copy.wait()
     for piece in [None] + sum(waved, []):
 
         def finish(piece=piece):
@@ -959,8 +977,11 @@
             jax.ShapeDtypeStruct((2,) + values.shape, values.dtype),
         ),
         in_specs=[vmem] * 5,
-        out_specs=(hbm,) + (vmem,) * 5,
+        out_specs=(hbm, vmem, hbm, hbm, vmem, vmem),
         scratch_shapes=[
+            pltpu.VMEM((QUERY_HEADS, tokens, 2 * tokens), jnp.float32),
+            pltpu.VMEM((QUERY_HEADS, tokens, 1), jnp.float32),
+            dma((2, KEY_VALUE_HEADS)),
             dma((2,)),
             dma((2,)),
             dma,

time: 187 us -> 187 us (level)
  no operation moved by 1% of the time
where the time goes in v6:
time: 187 us; the launch traced here: 186 us
  Pallas kernels  133 us (71%)
  matrix products  23.7 us (13%)
  local copies, waits for them, and re-layouts  15.3 us (8%)
  other arithmetic  10.4 us (6%)
  between operations  4.43 us (2%)
    pallas_call x1, Pallas kernels, gather_and_attend(): pl.pallas_call(functools.partial(gather_kernel, count), out_shape=(jax.Sh...  59.3 us
    pallas_call x1, Pallas kernels, in_place_experts(): pl.pallas_call(functools.partial(expert_kernel, count), out_shape=(result...  58.2 us
    pallas_call x1, Pallas kernels, attention_backward(): pl.pallas_call(functools.partial(tail_kernel, count), out_shape=(jax.Shap...  15.2 us
    unnamed x65, local copies, waits for them, and re-layouts  9.5 us
    dot_general x1, matrix products, shards(): lax.dot_general(grad_residual, out_full, CONTRACT_LAST, preferred_element...  8.8 us
    dot_general x1, matrix products, shards(): projected = jnp.dot(attended, out_full, preferred_element_type=jnp.float32)  8.32 us

profile of v6, /device:TPU:0, one launch (start us, length us, event | category | flops | bytes accessed | tf_op | source)
XLA Modules:
  0.0 186.5 jit_solution(7350885019320594204)
XLA Ops:
  2.1 1.3 convert_reduce_fusion
  3.6 0.7 select_maximum_fusion
  4.4 0.7 broadcast_in_dim.58.sinks_ref
  5.1 0.8 iota_compare_fusion
  5.9 0.6 copy-done.24
  6.6 0.2 reduce_window_sum.11
  6.8 2.1 %fusion.12 = f32[2,4,2880]{2,1,0:T(4,128)} fusion(pred[128,2,4]{0,2,1:T(4,128)(4,1)S(1)} %fusion.25, bf16[1,128,2880]{1,2,0:T(8,128)(2,1)} %param.31), kind=kOutput, calls=%fused_computation.18 | convolution fusion | flops 5898240 | bytes 830464 | tf_op jit(solution)/shard_map/tec,td->ecd/dot_general | solution.py:1254
  8.9 0.3 copy.31.weight_ref
  9.3 59.3 %gather_kernel.1 = (bf16[16,128,2880]{2,1,0:T(8,128)(2,1)}, bf16[128,2048]{1,0:T(8,128)(2,1)S(1)}, f32[32,128,256]{2,1,0:T(8,128)S(1)}, f32[32,128,1]{2,1,0:T(8,...) custom-call(bf16[128,2880]{1,0:T(8,128)(2,1)S(1)} %copy.31.weight_ref, ...), custom_call_target="tpu_custom_call" | custom-call | tf_op jit(solution)/shard_map/gather_kernel/pallas_call | solution.py:969
  68.7 2.0 %copy-done.1 = f32[32,128,256]{2,1,0:T(8,128)} copy-done((f32[32,128,256]{2,1,0:T(8,128)}, f32[32,128,256]{2,1,0:T(8,128)S(1)}, u32[]{:S(2)}) %copy-start.1) | copy-done | bytes 4194328
  70.6 1.3 copy-done.3
  71.9 0.6 copy-done.11
  72.6 0.7 copy-done.13
  73.2 8.3 %fusion.1 = bf16[128,2880]{0,1:T(8,128)(2,1)S(1)} fusion(bf16[128,2048]{1,0:T(8,128)(2,1)S(1)} %get-tuple-element.21, bf16[2048,2880]{1,0:T(8,128)(2,1)} %bitcast.82, bf16[1,128,2880]{1,2,0:T(8,128)(2,1)S(1)} %copy-done.22), kind=kOutput, calls=%fused_computation.4 | convolution fusion | flops 1511055360 | bytes 13795328 | tf_op jit(solution)/shard_map/dot_general | solution.py:1228
  81.6 0.4 fusion.11
  82.0 0.9 fusion.16
  82.9 0.1 select_reduce_fusion.1
  83.1 0.5 copy-done.27
  83.6 0.6 exponential_divide_fusion
  84.2 0.6 fusion.14
  84.8 0.7 pad_maximum_fusion
  85.5 2.0 %reshape.132 = f32[2,8,16,180]{3,2,1,0:T(8,128)} reshape(f32[2,8,2880]{2,1,0:T(8,128)} %pad_maximum_fusion) | data formatting | bytes 368640 | tf_op jit(solution)/shard_map/reshape | solution.py:1260
  87.5 1.1 copy.48
  88.7 58.2 %expert_kernel.1 = (f32[17,8,256]{2,1,0:T(8,128)S(1)}, f32[17,8,256]{2,1,0:T(8,128)S(1)}) custom-call(f32[2,16,8,256]{3,2,1,0:T(8,128)S(1)} %pad.8.slots_ref, f32[8,256]{1,0:T(8,128)S(1)} %broadcast_in_dim.88.facts_ref, bf16[180,2048]{1,0:T(8,128)(2,1)S(1)} %copy-done.6, bf16[180,2048]{1,0:T(8,128)(2,1)S(1)} %copy-done.7, bf16[180,2048]{1,0:T(8,128)(2,1)S(1)} %copy-done.8), custom_call_target="tpu_custom_call" | custom-call | tf_op jit(solution)/shard_map/expert_kernel/pallas_call | solution.py:590
  146.9 0.6 copy-done.9
  147.6 0.6 slice.43
  148.4 0.2 fusion.27
  148.6 0.7 select_reduce_fusion.4
  151.2 0.7 fusion.31
  151.9 0.8 fusion.29
  152.7 1.2 fusion.20
  154.0 0.1 reshape.134
  154.2 0.1 fusion.33
  154.3 0.7 select_reduce_fusion.3
  155.0 0.1 fusion.34
  155.2 0.6 multiply_reduce_fusion
  155.8 0.6 subtract_multiply_fusion
  156.4 0.2 select_reduce_fusion
  156.7 1.4 convolution_bitcast_fusion
  158.2 0.6 fusion.6
  158.7 0.5 copy-done.19
  159.3 0.4 fusion.10
  159.8 8.8 %convolution_convert_fusion.mixed_ref = bf16[128,2048]{1,0:T(8,128)(2,1)S(1)} fusion(bf16[128,2880]{0,1:T(8,128)(2,1)S(1)} %fusion.10, bf16[2048,2880]{1,0:T(8,128)(2,1)} %bitcast.83), kind=kOutput, calls=%fused_computation.5 | convolution fusion | flops 1510211584 | bytes 13058048 | tf_op jit(solution)/shard_map/dot_general | solution.py:1306
  168.6 15.2 %tail_kernel.1 = (bf16[128,2048]{1,0:T(8,128)(2,1)S(1)}, bf16[128,256]{1,0:T(8,128)(2,1)S(1)}, bf16[128,256]{1,0:T(8,128)(2,1)S(1)}, f32[32,128]{1,0:T(8,128)S(1)}) custom-call(bf16[128,2048]{1,0:T(8,128)(2,1)S(1)} %bitcast.74, bf16[2,128,256]{2,1,0:T(8,128)(2,1)S(1)} %copy-done.12, bf16[2,128,256]{2,1,0:T(8,128)(2,1)S(1)} %copy-done.14, ...), custom_call_target="tpu_custom_call" | custom-call | tf_op jit(solution)/shard_map/tail_kernel/pallas_call | solution.py:1159
  183.8 0.6 slice_reduce_fusion
  184.4 0.8 copy.54
  185.2 0.6 copy.55
  185.8 0.6 copy.56
  (76 shorter events, 1.1 us)
Async XLA Ops:
  0.6 81.4 %copy-start = (bf16[2880,128]{1,0:T(8,128)(2,1)S(1)}, bf16[2880,128]{1,0:T(8,128)(2,1)}, u32[]{:S(2)}) copy-start(bf16[2880,128]{1,0:T(8,128)(2,1)} %param.23) | copy-start | bytes 2211844
  0.6 8.3 %copy-start.21 = (bf16[128,2880]{0,1:T(8,128)(2,1)S(1)}, bf16[128,2880]{0,1:T(8,128)(2,1)}, u32[]{:S(2)}) copy-start(bf16[128,2880]{0,1:T(8,128)(2,1)} %param.21) | copy-start | bytes 2211844
  0.7 8.6 %copy-start.16 = (bf16[1,128,256]{2,1,0:T(8,128)(2,1)S(1)}, bf16[1,128,256]{2,1,0:T(8,128)(2,1)}, u32[]{:S(2)}) copy-start(bf16[1,128,256]{2,1,0:T(8,128)(2,1)} %param.18) | copy-start | bytes 196612
  0.7 8.6 %copy-start.15 = (bf16[1,128,256]{2,1,0:T(8,128)(2,1)S(1)}, bf16[1,128,256]{2,1,0:T(8,128)(2,1)}, u32[]{:S(2)}) copy-start(bf16[1,128,256]{2,1,0:T(8,128)(2,1)} %param.17) | copy-start | bytes 196612
  0.7 8.6 %copy-start.5 = (bf16[1,128,2048]{2,1,0:T(8,128)(2,1)S(1)}, bf16[1,128,2048]{2,1,0:T(8,128)(2,1)}, u32[]{:S(2)}) copy-start(bf16[1,128,2048]{2,1,0:T(8,128)(2,1)} %param.16) | copy-start | bytes 1572868
  5.8 0.6 copy-start.24
  9.3 63.9 %copy-start.22 = (bf16[1,128,2880]{1,2,0:T(8,128)(2,1)S(1)}, bf16[1,128,2880]{1,2,0:T(8,128)(2,1)}, u32[]{:S(2)}) copy-start(bf16[1,128,2880]{1,2,0:T(8,128)(2,1)} %param.20) | copy-start | bytes 2211844
  68.6 2.0 %copy-start.1 = (f32[32,128,256]{2,1,0:T(8,128)}, f32[32,128,256]{2,1,0:T(8,128)S(1)}, u32[]{:S(2)}) copy-start(f32[32,128,256]{2,1,0:T(8,128)S(1)} %get-tuple-element.19.probs_ref) | copy-start | bytes 12582916
  70.6 1.3 copy-start.3
  71.9 0.6 copy-start.11
  72.6 0.7 copy-start.13
  73.2 8.8 %copy-start.26 = (f32[2880]{0:T(1024)S(1)}, f32[2880]{0:T(1024)}, u32[]{:S(2)}) copy-start(f32[2880]{0:T(1024)} %param.22) | copy-start | bytes 34564
  81.6 3.2 %copy-start.17 = (bf16[128,2880]{0,1:T(8,128)(2,1)}, bf16[128,2880]{0,1:T(8,128)(2,1)S(1)}, u32[]{:S(2)}) copy-start(bf16[128,2880]{0,1:T(8,128)(2,1)S(1)} %fusion.1) | copy-start | bytes 2211844
  81.6 1.3 copy-start.25
  82.0 2.7 %copy-start.28 = (f32[128]{0:T(128)}, f32[128]{0:T(128)S(1)}, u32[]{:S(2)}) copy-start(f32[128]{0:T(128)S(1)} %add_rsqrt_fusion) | copy-start | bytes 1540
  82.0 2.7 %copy-start.23 = (f32[2,4,2880]{2,1,0:T(4,128)S(1)}, f32[2,4,2880]{2,1,0:T(4,128)}, u32[]{:S(2)}) copy-start(f32[2,4,2880]{2,1,0:T(4,128)} %fusion.12) | copy-start | bytes 276484
  83.1 0.5 copy-start.27
  84.2 4.4 %copy-start.6 = (bf16[180,2048]{1,0:T(8,128)(2,1)S(1)}, bf16[180,2048]{1,0:T(8,128)(2,1)}, u32[]{:S(2)}) copy-start(bf16[180,2048]{1,0:T(8,128)(2,1)} %gate_ref.1) | copy-start | bytes 2211844
  84.2 4.4 %copy-start.7 = (bf16[180,2048]{1,0:T(8,128)(2,1)S(1)}, bf16[180,2048]{1,0:T(8,128)(2,1)}, u32[]{:S(2)}) copy-start(bf16[180,2048]{1,0:T(8,128)(2,1)} %up_ref.1) | copy-start | bytes 2211844
  84.2 4.5 %copy-start.8 = (bf16[180,2048]{1,0:T(8,128)(2,1)S(1)}, bf16[180,2048]{1,0:T(8,128)(2,1)}, u32[]{:S(2)}) copy-start(bf16[180,2048]{1,0:T(8,128)(2,1)} %down_ref.1) | copy-start | bytes 2211844
  146.9 0.6 copy-start.9
  146.9 0.7 copy-start.10
  147.6 10.5 %copy-start.18 = (bf16[128,2880]{0,1:T(8,128)(2,1)S(1)}, bf16[128,2880]{0,1:T(8,128)(2,1)}, u32[]{:S(2)}) copy-start(bf16[128,2880]{0,1:T(8,128)(2,1)} %copy-done.17) | copy-start | bytes 2211844
  147.6 10.6 %copy-start.29 = (f32[128]{0:T(128)S(1)}, f32[128]{0:T(128)}, u32[]{:S(2)}) copy-start(f32[128]{0:T(128)} %copy-done.28) | copy-start | bytes 1540
  158.2 1.1 copy-start.19
  159.7 8.9 %copy-start.20 = (bf16[128,2880]{0,1:T(8,128)(2,1)}, bf16[128,2880]{0,1:T(8,128)(2,1)S(1)}, u32[]{:S(2)}) copy-start(bf16[128,2880]{0,1:T(8,128)(2,1)S(1)} %fusion.10) | copy-start | bytes 2211844
  159.7 8.9 %copy-start.2 = (f32[32,128,256]{2,1,0:T(8,128)S(1)}, f32[32,128,256]{2,1,0:T(8,128)}, u32[]{:S(2)}) copy-start(f32[32,128,256]{2,1,0:T(8,128)} %copy-done.1) | copy-start | bytes 12582916
  159.7 8.9 %copy-start.4 = (f32[32,128,1]{2,1,0:T(8,128)S(1)}, f32[32,128,1]{2,1,0:T(8,128)}, u32[]{:S(2)}) copy-start(f32[32,128,1]{2,1,0:T(8,128)} %copy-done.3) | copy-start | bytes 49156
  159.8 8.9 %copy-start.12 = (bf16[2,128,256]{2,1,0:T(8,128)(2,1)S(1)}, bf16[2,128,256]{2,1,0:T(8,128)(2,1)}, u32[]{:S(2)}) copy-start(bf16[2,128,256]{2,1,0:T(8,128)(2,1)} %copy-done.11) | copy-start | bytes 393220
  159.8 8.9 %copy-start.14 = (bf16[2,128,256]{2,1,0:T(8,128)(2,1)S(1)}, bf16[2,128,256]{2,1,0:T(8,128)(2,1)}, u32[]{:S(2)}) copy-start(bf16[2,128,256]{2,1,0:T(8,128)(2,1)} %copy-done.13) | copy-start | bytes 393220
